TPU v7x, 32 devices: a whole 2x2x4 slice. The times are simulated.
32 devices in a mesh: row: 4 (over z), col: 4 (over y, x), rep: 2 (over core).
Axes of the slice: x: 2, y: 2, z: 4, core: 2. Of those that a mesh axis runs over, the one named last changes fastest.
Arguments:
- tokens: bfloat16 [3072, 5120], P('row'), may hold values from -6 to 6
- up_weight: bfloat16 [5120, 10240], P('row', 'col'), may hold values from -0.125 to 0.125
- block_mask: int32 [80, 160], replicated, may hold values from 0 to 1
Outputs:
- hidden: bfloat16 [3072, 10240], P('row', ('col', 'rep'))
All inputs are finite; a program needn't handle non-finite values.
Results may differ from a plain program's by a relative error of at most 0.001.
Values may be sent and summed in bfloat16 or wider, within the bound.
No kernel may reach another device: no remote copies, remote signals or barrier semaphores. Data moves between devices by JAX's collectives and lax.ppermute only.
A program may use at most 64 MiB of HBM per device.

v0:
```python
import jax
import jax.numpy as jnp
from jax import lax
from jax.sharding import PartitionSpec as P

BLOCK = 64


def body(tokens, up_weight, block_mask):
    weight_rows_dev, hidden_dev = up_weight.shape
    rep_count = lax.axis_size("rep")
    row_index = lax.axis_index("row")
    col_index = lax.axis_index("col")
    rep_index = lax.axis_index("rep")
    row_ids = row_index * weight_rows_dev + lax.iota(jnp.int32, weight_rows_dev)
    col_ids = col_index * hidden_dev + lax.iota(jnp.int32, hidden_dev)
    row_onehot = (
        row_ids[:, None] // BLOCK == lax.iota(jnp.int32, block_mask.shape[0])[None, :]
    ).astype(jnp.float32)
    col_onehot = (
        col_ids[:, None] // BLOCK == lax.iota(jnp.int32, block_mask.shape[1])[None, :]
    ).astype(jnp.float32)
    mask_rows = jnp.dot(row_onehot, block_mask.astype(jnp.float32), precision=lax.Precision.HIGHEST)
    local_mask = jnp.dot(mask_rows, col_onehot.T, precision=lax.Precision.HIGHEST)
    masked_weight = up_weight * local_mask.astype(jnp.bfloat16)
    share = hidden_dev // rep_count
    my_columns = lax.dynamic_slice_in_dim(masked_weight, rep_index * share, share, 1)
    preact = jnp.dot(
        tokens,
        lax.all_gather(my_columns, "row", axis=0, tiled=True),
        preferred_element_type=jnp.float32,
    )
    return jax.nn.gelu(preact, approximate=True).astype(jnp.bfloat16)


def solution(mesh):
    in_specs = (P("row", None), P("row", "col"), P())
    out_specs = P("row", ("col", "rep"))
    return jax.shard_map(body, mesh=mesh, in_specs=in_specs, out_specs=out_specs, check_vma=False)
```

profile of v0, /device:TPU:0, one launch (start us, length us, event | category | flops | bytes accessed | tf_op | source)
XLA Modules:
  0.0 272.1 jit_solution(2279541156190921349)
XLA Ops:
  6.5 0.0 all-gather.2.cloned.1.call-start
  6.6 1.6 fusion.11
  8.2 0.0 copy-start
  8.2 6.1 %fusion.9 = bf16[1280,2560]{1,0:T(8,128)(2,1)S(1)} fusion(f32[1280,160]{1,0:T(8,128)S(1)} %fusion.11, s32[2560]{0:T(1024)S(1)} %add_select_fusion), kind=kOutput, calls=%fused_computation.12 | convolution fusion | flops 6291865600 | bytes 7383040 | tf_op jit(solution)/shard_map/dot_general | solution.py:24
  14.3 0.0 copy-done
  14.3 2.7 fusion.8
  17.1 0.0 all-gather.2.cloned.1.call-update
  17.1 229.6 %all-gather.2.cloned.1.call-done = bf16[5120,1280]{1,0:T(8,128)(2,1)} async-done(((bf16[1280,1280]{1,0:T(8,128)(2,1)}), bf16[5120,1280]{1,0:T(8,128)(2,1)}) %all-gather.2.cloned.1.call-update) | async-done | bytes 13107216 | tf_op jit(solution)/shard_map/all_gather | solution.py:30
  246.7 16.3 %fusion.7 = bf16[768,1280]{0,1:T(8,128)(2,1)S(1)} fusion(bf16[5120,1280]{1,0:T(8,128)(2,1)} %all-gather.2.cloned.1.call-done, bf16[768,5120]{1,0:T(8,128)(2,1)} %param.3), kind=kOutput, calls=%fused_computation.9 | convolution fusion | flops 10075176960 | bytes 22937600 | tf_op jit(solution)/shard_map/dot_general | solution.py:28
  263.0 2.3 copy.4
  (2 shorter events, 0.0 us)
Async XLA Ops:
  6.5 240.2 %all-gather.2.cloned.1.call-start = ((), (), s32[]{:S(2)}) async-start(), calls=%async_computation | async-start | bytes 16384000 | tf_op jit(solution)/shard_map/all_gather | solution.py:30
  8.2 6.1 %copy-start = (bf16[1280,2560]{1,0:T(8,128)(2,1)S(1)}, bf16[1280,2560]{1,0:T(8,128)(2,1)}, u32[]{:S(2)}) copy-start(bf16[1280,2560]{1,0:T(8,128)(2,1)} %param.4) | copy-start | bytes 19660804
Sparse Core Ops, SparseCore 0:
  17.2 229.4 all-gather.1
where the time goes:
time: 272 us
  waiting for transfers between devices  230 us (85%)
  matrix products  24 us (9%)
  between operations  13.4 us (5%)
  other arithmetic  2.73 us (1%)
    all_gather x1, waiting for transfers between devices, body(): lax.all_gather(my_columns, 'row', axis=0, tiled=True)  230 us
    dot_general x1, matrix products, body(): jnp.dot(tokens, lax.all_gather(my_columns, 'row', axis=0, tiled=True), pr...  16.3 us
    dot_general x1, matrix products, body(): jnp.dot(mask_rows, col_onehot.T, precision=lax.Precision.HIGHEST)  6.12 us
  transfers between devices with their start and end apart: 1, of which 1 were waited for; matrix products, arithmetic and copies ran while one was open for 0% of the time, Pallas kernels for 0%

commit v1 on v0

--- a/solution.py
+++ b/solution.py
@@ -1,12 +1,17 @@
+import functools
+
 import jax
 import jax.numpy as jnp
 from jax import lax
+from jax.experimental import pallas as pl
+from jax.experimental.pallas import tpu as pltpu
 from jax.sharding import PartitionSpec as P
 
 BLOCK = 64
+CHUNK = 256
 
 
-def body(tokens, up_weight, block_mask):
+def gather_body(tokens, up_weight, block_mask):
     weight_rows_dev, hidden_dev = up_weight.shape
     rep_count = lax.axis_size("rep")
     row_index = lax.axis_index("row")
@@ -33,7 +38,117 @@
     return jax.nn.gelu(preact, approximate=True).astype(jnp.bfloat16)
 
 
+def mask_kernel(place, mask, w_ref, *out_refs):
+    row_blocks, tiles = w_ref.shape[0] // BLOCK, w_ref.shape[1] // (2 * BLOCK)
+    lane = lax.broadcasted_iota(jnp.int32, (BLOCK, 2 * BLOCK), 1)
+    per = CHUNK // (2 * BLOCK)
+
+    for chunk, out in enumerate(out_refs):
+        def step(i, _):
+            for t in range(per):
+                tile = chunk * per + t
+                col = place[1] + 2 * tile
+                left = mask[place[0] + i, col]
+                right = mask[place[0] + i, col + 1]
+                rows = pl.ds(pl.multiple_of(i * BLOCK, BLOCK), BLOCK)
+                keep = jnp.where(lane < BLOCK, left, right)
+                value = w_ref[rows, tile * 2 * BLOCK : (tile + 1) * 2 * BLOCK]
+                out[rows, t * 2 * BLOCK : (t + 1) * 2 * BLOCK] = value * keep.astype(jnp.bfloat16)
+            return 0
+
+        lax.fori_loop(0, row_blocks, step, 0)
+
+
+def masked_chunks(place, mask, weight, share, rep_index):
+    rows = weight.shape[0]
+    chunks = share // CHUNK
+    return pl.pallas_call(
+        mask_kernel,
+        grid_spec=pltpu.PrefetchScalarGridSpec(
+            num_scalar_prefetch=2,
+            grid=(1,),
+            in_specs=[pl.BlockSpec((rows, share), lambda i, place, mask: (0, place[2]))],
+            out_specs=[pl.BlockSpec((rows, CHUNK), lambda i, place, mask: (0, 0))] * chunks,
+        ),
+        out_shape=[jax.ShapeDtypeStruct((rows, CHUNK), jnp.bfloat16)] * chunks,
+        compiler_params=pltpu.CompilerParams(vmem_limit_bytes=40 * 2**20),
+    )(place, mask, weight)
+
+
+INWARD = [(0, 1), (3, 2)]
+OUTWARD = [(1, 0), (2, 3)]
+MIDDLE = [(1, 2), (2, 1)]
+SWAP_X = [(0, 1), (1, 0), (2, 3), (3, 2)]
+SWAP_Y = [(0, 2), (2, 0), (1, 3), (3, 1)]
+SWAP_CORE = [(0, 1), (1, 0)]
+
+
+def line_body(tokens, up_weight, block_mask):
+    depth, hidden_dev = up_weight.shape
+    row_count, rep_count = lax.axis_size("row"), lax.axis_size("rep")
+    col_count = lax.axis_size("col")
+    r, c, p = (lax.axis_index(a).astype(jnp.int32) for a in ("row", "col", "rep"))
+    share = hidden_dev // rep_count
+    chunks = share // CHUNK
+    width = tokens.shape[1]
+
+    parts = col_count * rep_count
+    piece = width // parts
+    mine = lax.dynamic_slice_in_dim(tokens, (c * rep_count + p) * piece, piece, 1)
+    mine = lax.ppermute(mine, "row", INWARD)
+    half = tokens.shape[0] // 2
+    a, b = mine[:half], mine[half:]
+    ax = lax.ppermute(a, "col", SWAP_X)
+    by = lax.ppermute(b, "col", SWAP_Y)
+    a2, b2 = jnp.stack([a, ax]), jnp.stack([b, by])
+    ay = lax.ppermute(a2, "col", SWAP_Y)
+    bx = lax.ppermute(b2, "col", SWAP_X)
+    four = jnp.concatenate(
+        [
+            jnp.concatenate([a2, ay], 0),
+            jnp.stack([b, bx[0], by, bx[1]]),
+        ],
+        1,
+    )
+    four_other = lax.ppermute(four, "rep", SWAP_CORE)
+    both = jnp.stack([four, four_other], 1)
+    order = [
+        lax.dynamic_index_in_dim(
+            both.reshape(parts, tokens.shape[0], piece), ((i // rep_count) ^ c) * rep_count + ((i % rep_count) ^ p), 0, False
+        )
+        for i in range(parts)
+    ]
+    tokens_end = jnp.concatenate(order, 1)
+
+    place = jnp.stack([r * (depth // BLOCK), (c * rep_count + p) * (share // BLOCK), p])
+    own = masked_chunks(place, block_mask, up_weight, share, p)
+    middle = lax.ppermute(jnp.stack(own), "row", MIDDLE)
+    near = [lax.ppermute(w, "row", INWARD) for w in own]
+    far = [lax.ppermute(w, "row", MIDDLE) for w in near]
+
+    is_one = r <= 1
+    def ordered(i):
+        first = jnp.concatenate([near[i], own[i], middle[i], far[i]], 0)
+        second = jnp.concatenate([far[i], middle[i], own[i], near[i]], 0)
+        return jnp.where(is_one, first, second)
+
+    def hidden(t, w):
+        preact = jnp.dot(t, w, preferred_element_type=jnp.float32)
+        return jax.nn.gelu(preact, approximate=True).astype(jnp.bfloat16)
+
+    is_middle = (r == 1) | (r == 2)
+    out = []
+    for i in range(chunks):
+        w = ordered(i)
+        here = hidden(tokens, w)
+        back = lax.ppermute(hidden(tokens_end, w), "row", OUTWARD)
+        out.append(jnp.where(is_middle, here, back))
+    return jnp.concatenate(out, 1)
+
+
 def solution(mesh):
     in_specs = (P("row", None), P("row", "col"), P())
     out_specs = P("row", ("col", "rep"))
+    line = dict(mesh.shape) == {"row": 4, "col": 4, "rep": 2}
+    body = line_body if line else gather_body
     return jax.shard_map(body, mesh=mesh, in_specs=in_specs, out_specs=out_specs, check_vma=False)

time: 272 us -> 263 us (0.967)
  waiting for transfers between devices: 230 us -> 64.9 us
  starting transfers between devices: 0.01 us -> 73.5 us
  matrix products: 24 us -> 76.6 us
  local copies, waits for them, and re-layouts: 2.27 us -> 25.7 us
  other arithmetic: 2.73 us -> 16.1 us
  between operations: 13.4 us -> 0.32 us
  Pallas kernels: 0 us -> 4.4 us
    all_gather x1 -> x0, waiting for transfers between devices: 230 us -> none  [body(): lax.all_gather(my_columns, 'row', axis=0, tiled=True)]
    ppermute x0 -> x22, starting transfers between devices: none -> 73.5 us  [the longest x5 44.3 us: line_body(): near = [lax.ppermute(w, 'row', INWARD) for w in own]]
    ppermute x0 -> x22, waiting for transfers between devices: none -> 64.9 us  [the longest x5 18.8 us: line_body(): near = [lax.ppermute(w, 'row', INWARD) for w in own]]
    dot_general x3 -> x10, matrix products: 24 us -> 76.6 us  [hidden(): preact = jnp.dot(t, w, preferred_element_type=jnp.float32)]
    unnamed x2 -> x39, local copies, waits for them, and re-layouts: 0.01 us -> 14 us
    another operation x0 -> x5, other arithmetic: none -> 10.8 us  [the longest x2 10.5 us: line_body(): both = jnp.stack([four, four_other], 1)]
    concatenate x0 -> x1, other arithmetic: none -> 5.33 us  [line_body(): jnp.concatenate([jnp.concatenate([a2, ay], 0), jnp.stack([b, bx[0], by, b...]
    pallas_call x0 -> x1, Pallas kernels: none -> 4.4 us  [masked_chunks(): pl.pallas_call(mask_kernel, grid_spec=pltpu.PrefetchScalarGridSpec(num_sc...]
  transfers between devices with their start and end apart: 1 -> 22, of which waited for: 1 -> 8; matrix products, arithmetic and copies ran while one was open for 0% -> 38% of each run, Pallas kernels for 0% -> 2%
where the time goes in v1:
time: 263 us; the launch traced here: 262 us
  matrix products  76.6 us (29%)
  starting transfers between devices  73.5 us (28%)
  waiting for transfers between devices  64.9 us (25%)
  local copies, waits for them, and re-layouts  25.7 us (10%)
  other arithmetic  16.1 us (6%)
  Pallas kernels  4.4 us (2%)
    dot_general x10, matrix products, hidden(): preact = jnp.dot(t, w, preferred_element_type=jnp.float32)  76.6 us
    ppermute x5, starting transfers between devices, line_body(): near = [lax.ppermute(w, 'row', INWARD) for w in own]  44.3 us
    ppermute x5, waiting for transfers between devices, line_body(): near = [lax.ppermute(w, 'row', INWARD) for w in own]  18.8 us
    ppermute x1, waiting for transfers between devices, line_body(): bx = lax.ppermute(b2, 'col', SWAP_X)  14.8 us
    unnamed x39, local copies, waits for them, and re-layouts  14 us
    ppermute x5, waiting for transfers between devices, line_body(): back = lax.ppermute(hidden(tokens_end, w), 'row', OUTWARD)  12 us
    another operation x2, other arithmetic, line_body(): both = jnp.stack([four, four_other], 1)  10.5 us
    ppermute x1, waiting for transfers between devices, line_body(): mine = lax.ppermute(mine, 'row', INWARD)  10.3 us
  transfers between devices with their start and end apart: 22, of which 8 were waited for; matrix products, arithmetic and copies ran while one was open for 38% of the time, Pallas kernels for 2%

profile of v1, /device:TPU:0, one launch (start us, length us, event | category | flops | bytes accessed | tf_op | source)
XLA Modules:
  0.0 261.6 jit_solution(17131040402858797578)
XLA Ops:
  0.0 2.2 constant_dynamic-slice_fusion
  2.2 5.9 %collective-permute-start.3 = (bf16[768,640]{1,0:T(8,128)(2,1)}, bf16[768,640]{1,0:T(8,128)(2,1)}, u32[]{:S(2)}, u32[]{:S(2)}) collective-permute-start(bf16[768,640]{1,0:T(8,128)(2,1)} %constant_dynamic-slice_fusion), channel_id=1, source_target_pairs={{0,8},{24,16},{1,9},{25,17},{2,10},{26,18},{3,11},{27,19},{4,12},{... | collective-permute-start | bytes 2949128 | tf_op jit(solution)/shard_map/ppermute | solution.py:98
  8.2 2.9 %copy-done = bf16[1280,2560]{1,0:T(8,128)(2,1)S(1)} copy-done((bf16[1280,2560]{1,0:T(8,128)(2,1)S(1)}, bf16[1280,2560]{1,0:T(8,128)(2,1)}, u32[]{:S(2)}) %copy-start) | copy-done | bytes 6553624
  11.0 0.9 copy-done.1
  11.9 4.4 %shard_map.37 = (bf16[1280,256]{1,0:T(8,128)(2,1)S(1)}, bf16[1280,256]{1,0:T(8,128)(2,1)S(1)}, bf16[1280,256]{1,0:T(8,128)(2,1)S(1)}, bf16[1280,256]{1,0:T(8,128)(2,1)S(1)}, bf16[1280,256]{1,0:T(8,128)(2,1)S(1)}) custom-call(s32[3]{0:T(128)S(1)} %pad_add_fusion.place, s32[80,160]{1,0:T(8,128)S(1)} %copy-done.1, bf16[1280,2560]{1,0:T(8,128)(2,1)S(1)} %copy-done), custom_call_target="tpu_custom_call" | custom-call | tf_op jit(solution)/shard_map/pallas_call | solution.py:65
  16.3 0.9 bitcast_dynamic-update-slice_fusion.12
  17.3 0.9 bitcast_dynamic-update-slice_fusion.11
  18.2 10.3 %collective-permute-done.3 = bf16[768,640]{1,0:T(8,128)(2,1)} collective-permute-done((bf16[768,640]{1,0:T(8,128)(2,1)}, bf16[768,640]{1,0:T(8,128)(2,1)}, u32[]{:S(2)}, u32[]{:S(2)}) %collective-permute-start.3) | collective-permute-done | bytes 983072 | tf_op jit(solution)/shard_map/ppermute | solution.py:98
  28.5 1.3 slice_bitcast_fusion.6
  29.8 1.6 collective-permute-start.6
  31.4 1.5 collective-permute-start.4
  32.9 0.9 bitcast_dynamic-update-slice_fusion.10
  33.8 8.2 %collective-permute-done.6 = bf16[384,640]{1,0:T(8,128)(2,1)S(1)} collective-permute-done((bf16[384,640]{1,0:T(8,128)(2,1)S(1)}, bf16[384,640]{1,0:T(8,128)(2,1)S(1)}, u32[]{:S(2)}, u32[]{:S(2)}) %collective-permute-start.6) | collective-permute-done | bytes 491552 | tf_op jit(solution)/shard_map/ppermute | solution.py:102
  42.0 0.1 pad_maximum_fusion.2
  42.1 1.6 collective-permute-start.7
  43.6 0.1 pad_maximum_fusion.1
  43.8 1.6 collective-permute-start.5
  45.3 0.9 bitcast_dynamic-update-slice_fusion.9
  46.2 0.9 bitcast_dynamic-update-slice_fusion.8
  47.1 2.4 collective-permute-start.1
  49.5 14.8 %collective-permute-done.7 = bf16[2,384,640]{2,1,0:T(8,128)(2,1)S(1)} collective-permute-done((bf16[2,384,640]{2,1,0:T(8,128)(2,1)S(1)}, bf16[2,384,640]{2,1,0:T(8,128)(2,1)S(1)}, u32[]{:S(2)}, u32[]{:S(2)}) %collective-permute-start.7) | collective-permute-done | bytes 983072 | tf_op jit(solution)/shard_map/ppermute | solution.py:105
  64.4 0.9 collective-permute-done.5
  65.2 5.3 %maximum_maximum_fusion = bf16[4,768,640]{2,1,0:T(8,128)(2,1)} fusion(bf16[1,384,640]{2,1,0:T(8,128)(2,1)S(1)} %get-tuple-element.25, bf16[1,384,640]{2,1,0:T(8,128)(2,1)S(1)} %bitcast.120, bf16[1,384,640]{2,1,0:T(8,128)(2,1)S(1)} %get-tuple-element.24, bf16[1,384,640]{2,1,0:T(8,128)(2,1)S(1)} %get-tuple-element.21, ...), kind=kLoop, calls=%fused_computation.1 | loop fusion | flops 27525120 | bytes 7864320 | tf_op jit(solution)/shard_map/concatenate | solution.py:106
  70.7 5.2 %collective-permute-start.19 = (bf16[1280,256]{1,0:T(8,128)(2,1)S(1)}, bf16[1280,256]{1,0:T(8,128)(2,1)}, u32[]{:S(2)}, u32[]{:S(2)}) collective-permute-start(bf16[1280,256]{1,0:T(8,128)(2,1)S(1)} %get-tuple-element.14), channel_id=1, source_target_pairs={{0,8},{24,16},{1,9},{25,17},{2,10},{26,18},{3,11},{27,19},{4,12},{... | collective-permute-start | bytes 1966088 | tf_op jit(solution)/shard_map/ppermute | solution.py:126
  75.9 2.2 collective-permute-start.16
  78.1 2.1 collective-permute-start.13
  80.2 9.9 %collective-permute-done.19 = bf16[1280,256]{1,0:T(8,128)(2,1)} collective-permute-done((bf16[1280,256]{1,0:T(8,128)(2,1)S(1)}, bf16[1280,256]{1,0:T(8,128)(2,1)}, u32[]{:S(2)}, u32[]{:S(2)}) %collective-permute-start.19) | collective-permute-done | bytes 655392 | tf_op jit(solution)/shard_map/ppermute | solution.py:126
  90.1 5.3 %collective-permute-start.10 = (bf16[1280,256]{1,0:T(8,128)(2,1)S(1)}, bf16[1280,256]{1,0:T(8,128)(2,1)}, u32[]{:S(2)}, u32[]{:S(2)}) collective-permute-start(bf16[1280,256]{1,0:T(8,128)(2,1)S(1)} %get-tuple-element.11), channel_id=1, source_target_pairs={{0,8},{24,16},{1,9},{25,17},{2,10},{26,18},{3,11},{27,19},{4,12},{... | collective-permute-start | bytes 1966088 | tf_op jit(solution)/shard_map/ppermute | solution.py:126
  95.4 29.4 %collective-permute-start = (bf16[1280,256]{1,0:T(8,128)(2,1)S(1)}, bf16[1280,256]{1,0:T(8,128)(2,1)}, u32[]{:S(2)}, u32[]{:S(2)}) collective-permute-start(bf16[1280,256]{1,0:T(8,128)(2,1)S(1)} %get-tuple-element.10), channel_id=1, source_target_pairs={{0,8},{24,16},{1,9},{25,17},{2,10},{26,18},{3,11},{27,19},{4,12},{... | collective-permute-start | bytes 1966088 | tf_op jit(solution)/shard_map/ppermute | solution.py:126
  124.9 4.5 %fusion.106 = bf16[4,1,768,640]{3,2,1,0:T(8,128)(2,1)S(1)} fusion(bf16[1,384,640]{2,1,0:T(8,128)(2,1)} %copy-done.8, bf16[1,384,640]{2,1,0:T(8,128)(2,1)} %bitcast.121, bf16[1,384,640]{2,1,0:T(8,128)(2,1)} %copy-done.7, bf16[1,384,640]{2,1,0:T(8,128)(2,1)} %copy-done.4, bf16[2,384,640]{2,1,0:T(8,128)(2,1)} %copy-done.9, bf16[1,384,640]{2,1,0:T(8,128)(2,1)} %bitcast.124, ...), kind=kLoop, calls=%fused_computation.142 | loop fusion | flops 27525120 | bytes 7864320 | tf_op jit(solution)/shard_map/stack | solution.py:114
  129.4 2.9 %slice_bitcast_fusion = (bf16[1280,256]{1,0:T(8,128)(2,1)S(1)}, bf16[1280,256]{1,0:T(8,128)(2,1)S(1)}, bf16[1280,256]{1,0:T(8,128)(2,1)S(1)}, bf16[1280,256]{1,0:T(8,128)(2,1)S(1)}, bf16[1280,256]{1,0:T(8,128)(2,1)}) fusion(bf16[5,1280,256]{2,1,0:T(8,128)(2,1)} %collective-permute-done.1), kind=kLoop, calls=%fused_computation.122 | loop fusion | bytes 6553600 | tf_op jit(solution)/shard_map/squeeze | solution.py:131
  132.3 1.5 collective-permute-start.20
  133.9 1.5 collective-permute-start.17
  135.4 1.5 collective-permute-start.14
  136.9 8.9 %collective-permute-done = bf16[1280,256]{1,0:T(8,128)(2,1)} collective-permute-done((bf16[1280,256]{1,0:T(8,128)(2,1)S(1)}, bf16[1280,256]{1,0:T(8,128)(2,1)}, u32[]{:S(2)}, u32[]{:S(2)}) %collective-permute-start) | collective-permute-done | bytes 655392 | tf_op jit(solution)/shard_map/ppermute | solution.py:126
  145.9 1.5 collective-permute-start.11
  147.4 1.5 collective-permute-start.2
  148.9 6.0 %pad_maximum_fusion = bf16[4,2,768,640]{3,2,1,0:T(8,128)(2,1)} fusion(bf16[4,1,768,640]{3,2,1,0:T(8,128)(2,1)} %bitcast.16, bf16[4,1,768,640]{3,2,1,0:T(8,128)(2,1)S(1)} %fusion.106), kind=kLoop, calls=%fused_computation | loop fusion | flops 3932160 | bytes 15728640 | tf_op jit(solution)/shard_map/stack | solution.py:114
  154.9 1.5 bitcast_dynamic-update-slice_fusion.7
  156.4 1.7 bitcast_dynamic-update-slice_fusion.6
  158.1 1.4 bitcast_dynamic-update-slice_fusion.5
  159.5 1.4 bitcast_dynamic-update-slice_fusion.4
  160.9 0.2 bitcast_dynamic-update-slice_fusion.3
  161.1 0.2 bitcast_dynamic-update-slice_fusion.2
  161.4 0.2 bitcast_dynamic-update-slice_fusion.1
  161.6 0.2 bitcast_dynamic-update-slice_fusion
  161.8 8.1 %fusion.89 = bf16[768,256]{0,1:T(8,128)(2,1)S(1)} fusion(bf16[768,5120]{1,0:T(8,128)(2,1)S(1)} %bitcast_dynamic-update-slice_fusion, bf16[1280,256]{1,0:T(8,128)(2,1)} %collective-permute-done.20, bf16[1280,256]{1,0:T(8,128)(2,1)S(1)} %get-tuple-element.15, bf16[1280,256]{1,0:T(8,128)(2,1)S(1)} %get-tuple-element.14, ...), kind=kOutput, calls=%fused_computation.121 | convolution fusion | flops 2037317632 | bytes 10878977 | tf_op jit(solution)/shard_map/dot_general | solution.py:136
  169.9 1.5 collective-permute-start.21
  171.4 7.2 %fusion.71 = bf16[768,256]{0,1:T(8,128)(2,1)S(1)} fusion(bf16[768,5120]{1,0:T(8,128)(2,1)S(1)} %bitcast_dynamic-update-slice_fusion, bf16[1280,256]{1,0:T(8,128)(2,1)} %collective-permute-done.17, bf16[1280,256]{1,0:T(8,128)(2,1)S(1)} %get-tuple-element.16, bf16[1280,256]{1,0:T(8,128)(2,1)S(1)} %get-tuple-element.13, ...), kind=kOutput, calls=%fused_computation.103 | convolution fusion | flops 2037317632 | bytes 10878977 | tf_op jit(solution)/shard_map/dot_general | solution.py:136
  178.6 1.3 collective-permute-start.18
  179.9 7.8 %fusion.53 = bf16[768,256]{0,1:T(8,128)(2,1)} fusion(bf16[768,5120]{1,0:T(8,128)(2,1)S(1)} %bitcast_dynamic-update-slice_fusion, bf16[1280,256]{1,0:T(8,128)(2,1)} %collective-permute-done.14, bf16[1280,256]{1,0:T(8,128)(2,1)S(1)} %get-tuple-element.17, bf16[1280,256]{1,0:T(8,128)(2,1)S(1)} %get-tuple-element.12, ...), kind=kOutput, calls=%fused_computation.85 | convolution fusion | flops 2037317632 | bytes 10878977 | tf_op jit(solution)/shard_map/dot_general | solution.py:136
  187.7 1.3 collective-permute-start.15
  189.1 7.2 %fusion.17 = bf16[768,256]{0,1:T(8,128)(2,1)} fusion(bf16[768,5120]{1,0:T(8,128)(2,1)} %copy-done.11, bf16[1280,256]{1,0:T(8,128)(2,1)} %collective-permute-done.2, bf16[1280,256]{1,0:T(8,128)(2,1)S(1)} %copy-done.10, bf16[1280,256]{1,0:T(8,128)(2,1)S(1)} %get-tuple-element.10, bf16[1280,256]{1,0:T(8,128)(2,1)} %collective-permute-done, pred[]{:T(512)S(6)} %le.3), kind=kOutput, calls=%fused_computation.49 | convolution fusion | flops 2037317632 | bytes 10878977 | tf_op jit(solution)/shard_map/dot_general | solution.py:136
  196.3 1.5 collective-permute-start.9
  197.8 7.1 %fusion.35 = bf16[768,256]{0,1:T(8,128)(2,1)} fusion(bf16[768,5120]{1,0:T(8,128)(2,1)} %copy-done.11, bf16[1280,256]{1,0:T(8,128)(2,1)} %collective-permute-done.11, bf16[1280,256]{1,0:T(8,128)(2,1)S(1)} %get-tuple-element.18, bf16[1280,256]{1,0:T(8,128)(2,1)S(1)} %get-tuple-element.11, bf16[1280,256]{1,0:T(8,128)(2,1)} %collective-permute-done.10, pred[]{:T(512)S(6)} %le.3), kind=kOutput, calls=%fused_computation.67 | convolution fusion | flops 2037317632 | bytes 10878977 | tf_op jit(solution)/shard_map/dot_general | solution.py:136
  204.9 1.5 collective-permute-start.12
  206.4 11.0 %collective-permute-done.9 = bf16[768,256]{0,1:T(8,128)(2,1)} collective-permute-done((bf16[768,256]{0,1:T(8,128)(2,1)}, bf16[768,256]{0,1:T(8,128)(2,1)}, u32[]{:S(2)}, u32[]{:S(2)}) %collective-permute-start.9) | collective-permute-done | bytes 393248 | tf_op jit(solution)/shard_map/ppermute | solution.py:144
  217.4 7.9 %fusion.9 = bf16[768,1280]{0,1:T(8,128)(2,1)} fusion(bf16[768,256]{0,1:T(8,128)(2,1)} %collective-permute-done.9, bf16[768,5120]{1,0:T(8,128)(2,1)S(1)} %bitcast.126, pred[]{:T(512)S(6)} %or.3, bf16[1280,256]{1,0:T(8,128)(2,1)} %collective-permute-done.2, bf16[1280,256]{1,0:T(8,128)(2,1)S(1)} %copy-done.10, bf16[1280,256]{1,0:T(8,128)(2,1)S(1)} %get-tuple-element.10, ...), kind=kOutput, calls=%fused_computation.41 | convolution fusion | flops 2037514240 | bytes 11272194 | tf_op jit(solution)/shard_map/dot_general | solution.py:136
  225.3 1.0 collective-permute-done.12
  226.3 7.8 %fusion.27 = bf16[768,1280]{0,1:T(8,128)(2,1)} fusion(bf16[768,1280]{0,1:T(8,128)(2,1)} %fusion.9, bf16[768,256]{0,1:T(8,128)(2,1)S(1)} %collective-permute-done.12, bf16[768,5120]{1,0:T(8,128)(2,1)S(1)} %bitcast.126, pred[]{:T(512)S(6)} %or.3, bf16[1280,256]{1,0:T(8,128)(2,1)} %collective-permute-done.11, bf16[1280,256]{1,0:T(8,128)(2,1)S(1)} %get-tuple-element.18, ...), kind=kOutput, calls=%fused_computation.59 | convolution fusion | flops 2037514240 | bytes 11272194 | tf_op jit(solution)/shard_map/dot_general | solution.py:136
  234.1 7.8 %fusion.45 = bf16[768,1280]{0,1:T(8,128)(2,1)} fusion(bf16[768,1280]{0,1:T(8,128)(2,1)} %fusion.27, bf16[768,256]{0,1:T(8,128)(2,1)} %collective-permute-done.15, bf16[768,5120]{1,0:T(8,128)(2,1)S(1)} %bitcast.126, pred[]{:T(512)S(6)} %or.3, bf16[1280,256]{1,0:T(8,128)(2,1)} %collective-permute-done.14, bf16[1280,256]{1,0:T(8,128)(2,1)S(1)} %get-tuple-element.17, ...), kind=kOutput, calls=%fused_computation.77 | convolution fusion | flops 2037514240 | bytes 11272194 | tf_op jit(solution)/shard_map/dot_general | solution.py:136
  241.9 7.9 %fusion.63 = bf16[768,1280]{0,1:T(8,128)(2,1)} fusion(bf16[768,1280]{0,1:T(8,128)(2,1)} %fusion.45, bf16[768,256]{0,1:T(8,128)(2,1)S(1)} %collective-permute-done.18, bf16[768,5120]{1,0:T(8,128)(2,1)S(1)} %bitcast.126, pred[]{:T(512)S(6)} %or.3, bf16[1280,256]{1,0:T(8,128)(2,1)} %collective-permute-done.17, bf16[1280,256]{1,0:T(8,128)(2,1)S(1)} %get-tuple-element.16, ...), kind=kOutput, calls=%fused_computation.95 | convolution fusion | flops 2037514240 | bytes 11272194 | tf_op jit(solution)/shard_map/dot_general | solution.py:136
  249.8 7.9 %fusion.81 = bf16[768,1280]{0,1:T(8,128)(2,1)} fusion(bf16[768,1280]{0,1:T(8,128)(2,1)} %fusion.63, bf16[768,256]{0,1:T(8,128)(2,1)S(1)} %collective-permute-done.21, bf16[768,5120]{1,0:T(8,128)(2,1)S(1)} %bitcast.126, pred[]{:T(512)S(6)} %or.3, bf16[1280,256]{1,0:T(8,128)(2,1)} %collective-permute-done.20, bf16[1280,256]{1,0:T(8,128)(2,1)S(1)} %get-tuple-element.15, ...), kind=kOutput, calls=%fused_computation.113 | convolution fusion | flops 2037514240 | bytes 11272194 | tf_op jit(solution)/shard_map/dot_general | solution.py:136
  257.6 4.0 %copy.56 = bf16[768,1280]{1,0:T(8,128)(2,1)} copy(bf16[768,1280]{0,1:T(8,128)(2,1)} %fusion.81) | data formatting | bytes 3932160 | tf_op jit(solution)/shard_map/concatenate | solution.py:146
  (44 shorter events, 0.3 us)
Async XLA Ops:
  2.2 26.2 %collective-permute-start.3 = (bf16[768,640]{1,0:T(8,128)(2,1)}, bf16[768,640]{1,0:T(8,128)(2,1)}, u32[]{:S(2)}, u32[]{:S(2)}) collective-permute-start(bf16[768,640]{1,0:T(8,128)(2,1)} %constant_dynamic-slice_fusion), channel_id=1, source_target_pairs={{0,8},{24,16},{1,9},{25,17},{2,10},{26,18},{3,11},{27,19},{4,12},{... | collective-permute-start | bytes 2949128 | tf_op jit(solution)/shard_map/ppermute | solution.py:98
  8.2 2.9 %copy-start = (bf16[1280,2560]{1,0:T(8,128)(2,1)S(1)}, bf16[1280,2560]{1,0:T(8,128)(2,1)}, u32[]{:S(2)}) copy-start(bf16[1280,2560]{1,0:T(8,128)(2,1)} %w_ref.1) | copy-start | bytes 19660804
  11.0 0.9 copy-start.1
  29.8 40.8 %copy-start.3 = (bf16[1,384,640]{2,1,0:T(8,128)(2,1)}, bf16[1,384,640]{2,1,0:T(8,128)(2,1)S(1)}, u32[]{:S(2)}) copy-start(bf16[1,384,640]{2,1,0:T(8,128)(2,1)S(1)} %get-tuple-element.20) | copy-start | bytes 1474564
  29.8 40.8 %copy-start.4 = (bf16[1,384,640]{2,1,0:T(8,128)(2,1)}, bf16[1,384,640]{2,1,0:T(8,128)(2,1)S(1)}, u32[]{:S(2)}) copy-start(bf16[1,384,640]{2,1,0:T(8,128)(2,1)S(1)} %get-tuple-element.21) | copy-start | bytes 1474564
  29.8 12.2 %collective-permute-start.6 = (bf16[384,640]{1,0:T(8,128)(2,1)S(1)}, bf16[384,640]{1,0:T(8,128)(2,1)S(1)}, u32[]{:S(2)}, u32[]{:S(2)}) collective-permute-start(bf16[384,640]{1,0:T(8,128)(2,1)S(1)} %get-tuple-element.22), channel_id=1, source_target_pairs={{0,4},{4,0},{2,6},{6,2},{1,5},{5,1},{3,7},{7,3},{8,12},{12,8},{10,... | collective-permute-start | bytes 1474568 | tf_op jit(solution)/shard_map/ppermute | solution.py:102
  31.4 12.2 %collective-permute-start.4 = (bf16[384,640]{1,0:T(8,128)(2,1)S(1)}, bf16[384,640]{1,0:T(8,128)(2,1)S(1)}, u32[]{:S(2)}, u32[]{:S(2)}) collective-permute-start(bf16[384,640]{1,0:T(8,128)(2,1)S(1)} %get-tuple-element.23), channel_id=1, source_target_pairs={{0,2},{2,0},{4,6},{6,4},{1,3},{3,1},{5,7},{7,5},{8,10},{10,8},{12,... | collective-permute-start | bytes 1474568 | tf_op jit(solution)/shard_map/ppermute | solution.py:101
  42.0 28.6 %copy-start.5 = (bf16[384,640]{1,0:T(8,128)(2,1)}, bf16[384,640]{1,0:T(8,128)(2,1)S(1)}, u32[]{:S(2)}) copy-start(bf16[384,640]{1,0:T(8,128)(2,1)S(1)} %collective-permute-done.6) | copy-start | bytes 1474564
  42.1 22.2 %collective-permute-start.7 = (bf16[2,384,640]{2,1,0:T(8,128)(2,1)S(1)}, bf16[2,384,640]{2,1,0:T(8,128)(2,1)S(1)}, u32[]{:S(2)}, u32[]{:S(2)}) collective-permute-start(bf16[2,384,640]{2,1,0:T(8,128)(2,1)S(1)} %pad_maximum_fusion.2), channel_id=1, source_target_pairs={{0,2},{2,0},{4,6},{6,4},{1,3},{3,1},{5,7},{7,5},{8,10},{10,8},{12,... | collective-permute-start | bytes 2949128 | tf_op jit(solution)/shard_map/ppermute | solution.py:105
  43.6 26.9 %copy-start.6 = (bf16[384,640]{1,0:T(8,128)(2,1)}, bf16[384,640]{1,0:T(8,128)(2,1)S(1)}, u32[]{:S(2)}) copy-start(bf16[384,640]{1,0:T(8,128)(2,1)S(1)} %collective-permute-done.4) | copy-start | bytes 1474564
  43.8 21.5 %collective-permute-start.5 = (bf16[2,384,640]{2,1,0:T(8,128)(2,1)S(1)}, bf16[2,384,640]{2,1,0:T(8,128)(2,1)S(1)}, u32[]{:S(2)}, u32[]{:S(2)}) collective-permute-start(bf16[2,384,640]{2,1,0:T(8,128)(2,1)S(1)} %pad_maximum_fusion.1), channel_id=1, source_target_pairs={{0,4},{4,0},{2,6},{6,2},{1,5},{5,1},{3,7},{7,3},{8,12},{12,8},{10,... | collective-permute-start | bytes 2949128 | tf_op jit(solution)/shard_map/ppermute | solution.py:104
  47.1 48.3 %collective-permute-start.1 = (bf16[5,1280,256]{2,1,0:T(8,128)(2,1)}, bf16[5,1280,256]{2,1,0:T(8,128)(2,1)}, u32[]{:S(2)}, u32[]{:S(2)}) collective-permute-start(bf16[5,1280,256]{2,1,0:T(8,128)(2,1)} %bitcast_dynamic-update-slice_fusion.8), channel_id=1, source_target_pairs={{8,16},{16,8},{9,17},{17,9},{10,18},{18,10},{11,19},{19,11},{12,20... | collective-permute-start | bytes 9830408 | tf_op jit(solution)/shard_map/ppermute | solution.py:125
  64.4 11.5 %copy-start.7 = (bf16[1,384,640]{2,1,0:T(8,128)(2,1)}, bf16[1,384,640]{2,1,0:T(8,128)(2,1)S(1)}, u32[]{:S(2)}) copy-start(bf16[1,384,640]{2,1,0:T(8,128)(2,1)S(1)} %get-tuple-element.24) | copy-start | bytes 1474564
  64.4 13.7 %copy-start.8 = (bf16[1,384,640]{2,1,0:T(8,128)(2,1)}, bf16[1,384,640]{2,1,0:T(8,128)(2,1)S(1)}, u32[]{:S(2)}) copy-start(bf16[1,384,640]{2,1,0:T(8,128)(2,1)S(1)} %get-tuple-element.25) | copy-start | bytes 1474564
  65.2 12.8 %copy-start.9 = (bf16[2,384,640]{2,1,0:T(8,128)(2,1)}, bf16[2,384,640]{2,1,0:T(8,128)(2,1)S(1)}, u32[]{:S(2)}) copy-start(bf16[2,384,640]{2,1,0:T(8,128)(2,1)S(1)} %collective-permute-done.5) | copy-start | bytes 2949124
  70.6 76.8 %collective-permute-start.8 = (bf16[4,768,640]{2,1,0:T(8,128)(2,1)}, bf16[4,768,640]{2,1,0:T(8,128)(2,1)}, u32[]{:S(2)}, u32[]{:S(2)}) collective-permute-start(bf16[4,768,640]{2,1,0:T(8,128)(2,1)} %maximum_maximum_fusion), channel_id=1, source_target_pairs={{0,1},{1,0},{2,3},{3,2},{4,5},{5,4},{6,7},{7,6},{8,9},{9,8},{10,11... | collective-permute-start | bytes 11796488 | tf_op jit(solution)/shard_map/ppermute | solution.py:113
  70.7 19.4 %collective-permute-start.19 = (bf16[1280,256]{1,0:T(8,128)(2,1)S(1)}, bf16[1280,256]{1,0:T(8,128)(2,1)}, u32[]{:S(2)}, u32[]{:S(2)}) collective-permute-start(bf16[1280,256]{1,0:T(8,128)(2,1)S(1)} %get-tuple-element.14), channel_id=1, source_target_pairs={{0,8},{24,16},{1,9},{25,17},{2,10},{26,18},{3,11},{27,19},{4,12},{... | collective-permute-start | bytes 1966088 | tf_op jit(solution)/shard_map/ppermute | solution.py:126
  75.9 56.4 %collective-permute-start.16 = (bf16[1280,256]{1,0:T(8,128)(2,1)S(1)}, bf16[1280,256]{1,0:T(8,128)(2,1)}, u32[]{:S(2)}, u32[]{:S(2)}) collective-permute-start(bf16[1280,256]{1,0:T(8,128)(2,1)S(1)} %get-tuple-element.13), channel_id=1, source_target_pairs={{0,8},{24,16},{1,9},{25,17},{2,10},{26,18},{3,11},{27,19},{4,12},{... | collective-permute-start | bytes 1966088 | tf_op jit(solution)/shard_map/ppermute | solution.py:126
  78.1 55.8 %collective-permute-start.13 = (bf16[1280,256]{1,0:T(8,128)(2,1)S(1)}, bf16[1280,256]{1,0:T(8,128)(2,1)}, u32[]{:S(2)}, u32[]{:S(2)}) collective-permute-start(bf16[1280,256]{1,0:T(8,128)(2,1)S(1)} %get-tuple-element.12), channel_id=1, source_target_pairs={{0,8},{24,16},{1,9},{25,17},{2,10},{26,18},{3,11},{27,19},{4,12},{... | collective-permute-start | bytes 1966088 | tf_op jit(solution)/shard_map/ppermute | solution.py:126
  90.1 45.3 %collective-permute-start.10 = (bf16[1280,256]{1,0:T(8,128)(2,1)S(1)}, bf16[1280,256]{1,0:T(8,128)(2,1)}, u32[]{:S(2)}, u32[]{:S(2)}) collective-permute-start(bf16[1280,256]{1,0:T(8,128)(2,1)S(1)} %get-tuple-element.11), channel_id=1, source_target_pairs={{0,8},{24,16},{1,9},{25,17},{2,10},{26,18},{3,11},{27,19},{4,12},{... | collective-permute-start | bytes 1966088 | tf_op jit(solution)/shard_map/ppermute | solution.py:126
  95.4 50.4 %collective-permute-start = (bf16[1280,256]{1,0:T(8,128)(2,1)S(1)}, bf16[1280,256]{1,0:T(8,128)(2,1)}, u32[]{:S(2)}, u32[]{:S(2)}) collective-permute-start(bf16[1280,256]{1,0:T(8,128)(2,1)S(1)} %get-tuple-element.10), channel_id=1, source_target_pairs={{0,8},{24,16},{1,9},{25,17},{2,10},{26,18},{3,11},{27,19},{4,12},{... | collective-permute-start | bytes 1966088 | tf_op jit(solution)/shard_map/ppermute | solution.py:126
  132.3 29.5 %collective-permute-start.20 = (bf16[1280,256]{1,0:T(8,128)(2,1)}, bf16[1280,256]{1,0:T(8,128)(2,1)}, u32[]{:S(2)}, u32[]{:S(2)}) collective-permute-start(bf16[1280,256]{1,0:T(8,128)(2,1)} %collective-permute-done.19), channel_id=1, source_target_pairs={{8,16},{16,8},{9,17},{17,9},{10,18},{18,10},{11,19},{19,11},{12,20... | collective-permute-start | bytes 1966088 | tf_op jit(solution)/shard_map/ppermute | solution.py:127
  133.9 37.5 %collective-permute-start.17 = (bf16[1280,256]{1,0:T(8,128)(2,1)}, bf16[1280,256]{1,0:T(8,128)(2,1)}, u32[]{:S(2)}, u32[]{:S(2)}) collective-permute-start(bf16[1280,256]{1,0:T(8,128)(2,1)} %collective-permute-done.16), channel_id=1, source_target_pairs={{8,16},{16,8},{9,17},{17,9},{10,18},{18,10},{11,19},{19,11},{12,20... | collective-permute-start | bytes 1966088 | tf_op jit(solution)/shard_map/ppermute | solution.py:127
  135.4 44.5 %collective-permute-start.14 = (bf16[1280,256]{1,0:T(8,128)(2,1)}, bf16[1280,256]{1,0:T(8,128)(2,1)}, u32[]{:S(2)}, u32[]{:S(2)}) collective-permute-start(bf16[1280,256]{1,0:T(8,128)(2,1)} %collective-permute-done.13), channel_id=1, source_target_pairs={{8,16},{16,8},{9,17},{17,9},{10,18},{18,10},{11,19},{19,11},{12,20... | collective-permute-start | bytes 1966088 | tf_op jit(solution)/shard_map/ppermute | solution.py:127
  145.9 51.9 %collective-permute-start.11 = (bf16[1280,256]{1,0:T(8,128)(2,1)}, bf16[1280,256]{1,0:T(8,128)(2,1)}, u32[]{:S(2)}, u32[]{:S(2)}) collective-permute-start(bf16[1280,256]{1,0:T(8,128)(2,1)} %collective-permute-done.10), channel_id=1, source_target_pairs={{8,16},{16,8},{9,17},{17,9},{10,18},{18,10},{11,19},{19,11},{12,20... | collective-permute-start | bytes 1966088 | tf_op jit(solution)/shard_map/ppermute | solution.py:127
  147.4 41.6 %collective-permute-start.2 = (bf16[1280,256]{1,0:T(8,128)(2,1)}, bf16[1280,256]{1,0:T(8,128)(2,1)}, u32[]{:S(2)}, u32[]{:S(2)}) collective-permute-start(bf16[1280,256]{1,0:T(8,128)(2,1)} %collective-permute-done), channel_id=1, source_target_pairs={{8,16},{16,8},{9,17},{17,9},{10,18},{18,10},{11,19},{19,11},{12,20... | collective-permute-start | bytes 1966088 | tf_op jit(solution)/shard_map/ppermute | solution.py:127
  154.9 6.0 %copy-start.2 = (bf16[4,2,768,640]{3,2,1,0:T(8,128)(2,1)S(1)}, bf16[4,2,768,640]{3,2,1,0:T(8,128)(2,1)}, u32[]{:S(2)}) copy-start(bf16[4,2,768,640]{3,2,1,0:T(8,128)(2,1)} %pad_maximum_fusion) | copy-start | bytes 23592964
  161.8 18.1 %copy-start.11 = (bf16[768,5120]{1,0:T(8,128)(2,1)}, bf16[768,5120]{1,0:T(8,128)(2,1)S(1)}, u32[]{:S(2)}) copy-start(bf16[768,5120]{1,0:T(8,128)(2,1)S(1)} %bitcast_dynamic-update-slice_fusion) | copy-start | bytes 23592964
  169.9 79.9 %collective-permute-start.21 = (bf16[768,256]{0,1:T(8,128)(2,1)S(1)}, bf16[768,256]{0,1:T(8,128)(2,1)S(1)}, u32[]{:S(2)}, u32[]{:S(2)}) collective-permute-start(bf16[768,256]{0,1:T(8,128)(2,1)S(1)} %fusion.89), channel_id=1, source_target_pairs={{8,0},{16,24},{9,1},{17,25},{10,2},{18,26},{11,3},{19,27},{12,4},{... | collective-permute-start | bytes 1179656 | tf_op jit(solution)/shard_map/ppermute | solution.py:144
  178.6 63.3 %collective-permute-start.18 = (bf16[768,256]{0,1:T(8,128)(2,1)S(1)}, bf16[768,256]{0,1:T(8,128)(2,1)S(1)}, u32[]{:S(2)}, u32[]{:S(2)}) collective-permute-start(bf16[768,256]{0,1:T(8,128)(2,1)S(1)} %fusion.71), channel_id=1, source_target_pairs={{8,0},{16,24},{9,1},{17,25},{10,2},{18,26},{11,3},{19,27},{12,4},{... | collective-permute-start | bytes 1179656 | tf_op jit(solution)/shard_map/ppermute | solution.py:144
  179.9 9.1 %copy-start.10 = (bf16[1280,256]{1,0:T(8,128)(2,1)S(1)}, bf16[1280,256]{1,0:T(8,128)(2,1)}, u32[]{:S(2)}) copy-start(bf16[1280,256]{1,0:T(8,128)(2,1)} %get-tuple-element.19) | copy-start | bytes 1966084
  187.7 46.3 %collective-permute-start.15 = (bf16[768,256]{0,1:T(8,128)(2,1)}, bf16[768,256]{0,1:T(8,128)(2,1)}, u32[]{:S(2)}, u32[]{:S(2)}) collective-permute-start(bf16[768,256]{0,1:T(8,128)(2,1)} %fusion.53), channel_id=1, source_target_pairs={{8,0},{16,24},{9,1},{17,25},{10,2},{18,26},{11,3},{19,27},{12,4},{... | collective-permute-start | bytes 1179656 | tf_op jit(solution)/shard_map/ppermute | solution.py:144
  189.1 28.3 %slice-start = ((s8[7864320]{0:T(1024)(128)(4,1)}), s8[4194304]{0:T(1024)(128)(4,1)S(1)}, s32[]{:S(2)}) async-start(s8[7864320]{0:T(1024)(128)(4,1)} %bitcast.125), calls=%async_computation | async-start | bytes 8388608
  196.3 21.1 %slice-start.1 = ((s8[7864320]{0:T(1024)(128)(4,1)}), s8[3670016]{0:T(1024)(128)(4,1)S(1)}, s32[]{:S(2)}) async-start(s8[7864320]{0:T(1024)(128)(4,1)} %bitcast.125), calls=%async_computation.1 | async-start | bytes 7340032
  196.3 21.1 %collective-permute-start.9 = (bf16[768,256]{0,1:T(8,128)(2,1)}, bf16[768,256]{0,1:T(8,128)(2,1)}, u32[]{:S(2)}, u32[]{:S(2)}) collective-permute-start(bf16[768,256]{0,1:T(8,128)(2,1)} %fusion.17), channel_id=1, source_target_pairs={{8,0},{16,24},{9,1},{17,25},{10,2},{18,26},{11,3},{19,27},{12,4},{... | collective-permute-start | bytes 1179656 | tf_op jit(solution)/shard_map/ppermute | solution.py:144
  204.9 21.4 %collective-permute-start.12 = (bf16[768,256]{0,1:T(8,128)(2,1)}, bf16[768,256]{0,1:T(8,128)(2,1)S(1)}, u32[]{:S(2)}, u32[]{:S(2)}) collective-permute-start(bf16[768,256]{0,1:T(8,128)(2,1)} %fusion.35), channel_id=1, source_target_pairs={{8,0},{16,24},{9,1},{17,25},{10,2},{18,26},{11,3},{19,27},{12,4},{... | collective-permute-start | bytes 1179656 | tf_op jit(solution)/shard_map/ppermute | solution.py:144

commit v2 on v0

--- a/solution.py
+++ b/solution.py
@@ -1,12 +1,16 @@
+import functools
+
 import jax
 import jax.numpy as jnp
 from jax import lax
+from jax.experimental import pallas as pl
+from jax.experimental.pallas import tpu as pltpu
 from jax.sharding import PartitionSpec as P
 
 BLOCK = 64
 
 
-def body(tokens, up_weight, block_mask):
+def gather_body(tokens, up_weight, block_mask):
     weight_rows_dev, hidden_dev = up_weight.shape
     rep_count = lax.axis_size("rep")
     row_index = lax.axis_index("row")
@@ -33,7 +37,574 @@
     return jax.nn.gelu(preact, approximate=True).astype(jnp.bfloat16)
 
 
+UP = [(0, 1), (1, 2), (2, 3)]
+DOWN = [(3, 2), (2, 1), (1, 0)]
+INWARD = [(0, 1), (3, 2)]
+OUTWARD = [(1, 0), (2, 3)]
+MIDDLE = [(1, 2), (2, 1)]
+SWAP_X = [(0, 1), (1, 0), (2, 3), (3, 2)]
+SWAP_Y = [(0, 2), (2, 0), (1, 3), (3, 1)]
+SWAP_DIAGONAL = [(0, 3), (3, 0), (1, 2), (2, 1)]
+SWAPS = (SWAP_X, SWAP_Y, SWAP_DIAGONAL)
+SWAP_CORE = [(0, 1), (1, 0)]
+CHIPS = 4
+CORES = 2
+OWN = 20
+SPARE = 4
+SLOTS = OWN + SPARE
+LIGHT = 16
+HEAVY = (SLOTS - LIGHT) // 2
+CAP = 66
+TILE = 2 * BLOCK
+EMPTY = CHIPS * CORES * OWN
+ROW_TILE = 384
+SIZE = CAP * BLOCK
+MIB = 2**20
+BRIEF = pl.CostEstimate(flops=1, bytes_accessed=1, transcendentals=0)
+
+
+def after(value, *earlier):
+    return lax.optimization_barrier((value, *earlier))[0]
+
+
+def vmem(limit):
+    return pltpu.CompilerParams(vmem_limit_bytes=limit * MIB)
+
+
+def swap_halves(value):
+    return pltpu.roll(value.astype(jnp.float32), BLOCK, 1).astype(jnp.bfloat16)
+
+
+def make_plan(count, key, table, shared, c, p):
+    loads = []
+    for group in range(CHIPS * CORES):
+        total = count[group * OWN]
+        for i in range(1, OWN):
+            total += count[group * OWN + i]
+        loads.append(total)
+    chip = [loads[2 * i] + loads[2 * i + 1] for i in range(CHIPS)]
+    h, best = jnp.int32(0), chip[0]
+    for i in range(1, CHIPS):
+        more = chip[i] > best
+        h, best = jnp.where(more, i, h), jnp.where(more, chip[i], best)
+    shared[0] = h
+    taken = []
+    for core in range(CORES):
+        mine = [loads[2 * i + core] for i in range(CHIPS)]
+        heavy = sum(jnp.where(h == i, mine[i], 0) for i in range(CHIPS))
+
+        def given(kept):
+            out = []
+            for i in range(CHIPS):
+                spare = heavy * kept - OWN * mine[i]
+                n = sum((spare >= k * heavy).astype(jnp.int32) for k in range(1, SPARE + 1))
+                out.append(jnp.where(h == i, 0, n))
+            return out
+
+        kept = lax.while_loop(
+            lambda kept: OWN - sum(given(kept)) > kept, lambda kept: kept + 1, jnp.int32(OWN - 3 * SPARE)
+        )
+        taken.append(given(kept))
+        for i in range(CHIPS):
+            shared[1 + CORES * i + core] = taken[core][i]
+    taken = [jnp.where(p == 0, first, second) for first, second in zip(*taken)]
+    order = [jnp.where(h <= k, taken[k + 1], taken[k]) for k in range(CHIPS - 1)]
+    extra = sum(jnp.where(c == i, taken[i], 0) for i in range(CHIPS))
+    base = (c * CORES + p) * OWN
+
+    gone = []
+    for i in range(OWN):
+        k, j = i // SPARE, i % SPARE
+        gone.append((c == h) & (j < order[k]) if k < CHIPS - 1 else jnp.bool_(False))
+        key[i] = jnp.where(gone[i], -1, count[base + i])
+    for q in range(SPARE):
+        table[q] = EMPTY
+        table[SLOTS + q] = 0
+    for i in range(OWN):
+        rank = jnp.int32(0)
+        for j in range(OWN):
+            if j != i:
+                first = key[j] <= key[i] if j < i else key[j] < key[i]
+                rank += first.astype(jnp.int32)
+        slot = SPARE - extra + rank
+        table[slot] = jnp.where(gone[i], EMPTY, base + i)
+        table[SLOTS + slot] = i
+        k = min(i // SPARE, CHIPS - 2)
+        other = k + (h <= k).astype(jnp.int32)
+        back = SLOTS + ((c ^ other) - 1) * SPARE + (SPARE - 1 - i % SPARE)
+        table[2 * SLOTS + i] = jnp.where(gone[i], back, slot)
+    k = c - (c > h).astype(jnp.int32)
+    for i in range(SPARE):
+
+        @pl.when(i < extra)
+        def _():
+            table[SLOTS - 1 - i] = (h * CORES + p) * OWN + SPARE * k + i
+            table[2 * SLOTS - 1 - i] = OWN + i
+
+    table[2 * SLOTS + OWN] = c ^ h
+
+
+TABLE = 2 * SLOTS + OWN + 1
+
+
+def pack_kernel(place, mask, count, w_ref, table, shared, packed, own_heavy, key, both, line):
+    r, c, p = place[0], place[1], place[2]
+    make_plan(count, key, table, shared, c, p)
+    row_blocks = w_ref.shape[0] // BLOCK
+    for t in range(w_ref.shape[1] // TILE):
+        value = w_ref[:, t * TILE : (t + 1) * TILE]
+        both[0, :, t * TILE : (t + 1) * TILE] = value
+        both[1, :, t * TILE : (t + 1) * TILE] = swap_halves(value)
+    side = lax.broadcasted_iota(jnp.int32, (BLOCK, TILE), 1) // BLOCK
+
+    def lanes(source):
+        return pl.ds(pl.multiple_of((source >> 1) * TILE, TILE), TILE)
+
+    def column(q, s):
+        col = table[q]
+        source = table[SLOTS + q]
+        for i in range(row_blocks):
+            at = jnp.minimum(s, 2 * CAP)
+            value = both[(source ^ at) & 1, i * BLOCK : (i + 1) * BLOCK, lanes(source)]
+            line[pl.ds(pl.multiple_of(at * BLOCK, BLOCK), BLOCK), :] = value
+            s = s + mask[r * row_blocks + i, col]
+        return s
+
+    lax.fori_loop(0, LIGHT, column, jnp.int32(0))
+    for n in range(CAP):
+        left = line[2 * n * BLOCK : (2 * n + 1) * BLOCK, :]
+        right = line[(2 * n + 1) * BLOCK : (2 * n + 2) * BLOCK, :]
+        packed[n * BLOCK : (n + 1) * BLOCK, :] = jnp.where(side == 0, left, right)
+
+    for t in range(HEAVY // 2):
+        slots = (LIGHT + 2 * t, LIGHT + 2 * t + 1)
+
+        def block(i, _):
+            rows = pl.ds(pl.multiple_of(i * BLOCK, BLOCK), BLOCK)
+            values = []
+            for half in range(2):
+                source, col = table[SLOTS + slots[half]], table[slots[half]]
+                value = both[(source & 1) ^ half, rows, lanes(source)]
+                values.append(jnp.where(mask[r * row_blocks + i, col] != 0, value, jnp.zeros_like(value)))
+            own_heavy[rows, t * TILE : (t + 1) * TILE] = jnp.where(side == 0, values[0], values[1])
+            return 0
+
+        lax.fori_loop(0, row_blocks, block, 0)
+
+
+def pack_columns(place, mask, count, weight):
+    depth, share = weight.shape[0], OWN * BLOCK
+    smem = pl.BlockSpec(memory_space=pltpu.SMEM)
+    return pl.pallas_call(
+        pack_kernel,
+        grid_spec=pltpu.PrefetchScalarGridSpec(
+            num_scalar_prefetch=3,
+            grid=(1,),
+            in_specs=[pl.BlockSpec((depth, share), lambda i, place, mask, count: (0, place[2]))],
+            out_specs=[
+                smem,
+                smem,
+                pl.BlockSpec((CAP * BLOCK, TILE), lambda i, place, mask, count: (0, 0)),
+                pl.BlockSpec((depth, HEAVY * BLOCK), lambda i, place, mask, count: (0, 0)),
+            ],
+            scratch_shapes=[
+                pltpu.SMEM((OWN,), jnp.int32),
+                pltpu.VMEM((2, depth, share), jnp.bfloat16),
+                pltpu.VMEM((2 * SIZE + BLOCK, TILE), jnp.bfloat16),
+            ],
+        ),
+        out_shape=[
+            jax.ShapeDtypeStruct((TABLE,), jnp.int32),
+            jax.ShapeDtypeStruct((1 + CHIPS * CORES,), jnp.int32),
+            jax.ShapeDtypeStruct((CAP * BLOCK, TILE), jnp.bfloat16),
+            jax.ShapeDtypeStruct((depth, HEAVY * BLOCK), jnp.bfloat16),
+        ],
+        cost_estimate=BRIEF,
+        compiler_params=vmem(48),
+    )(place, mask, count, weight)
+
+
+def most_packed(counts, count, shared):
+    groups = CHIPS * CORES
+    column = lax.iota(jnp.int32, groups * OWN)
+    group, i = column // OWN, column % OWN
+    h, taken = shared[0], shared[1 : 1 + groups]
+    to = i // SPARE + (h <= i // SPARE).astype(jnp.int32)
+    ways = jnp.sum(jnp.where((to * CORES + group % CORES)[:, None] == lax.iota(jnp.int32, groups), taken, 0), 1)
+    gone = (group // CORES == h) & (i < 3 * SPARE) & (i % SPARE < ways)
+    key = jnp.where(gone, -1, count)
+    before = (key[None, :] < key[:, None]) | ((key[None, :] == key[:, None]) & (column[None, :] < column[:, None]))
+    rank = jnp.sum((before & (group[None, :] == group[:, None])).astype(jnp.int32), 1)
+    extra = jnp.sum(jnp.where(group[:, None] == lax.iota(jnp.int32, groups), taken, 0), 1)
+    light = (SPARE - extra + rank < LIGHT) & ~gone
+    return jnp.max(jnp.sum(jnp.where(light, counts, 0).reshape(counts.shape[0], groups, OWN), 2))
+
+
+def whole_kernel(first, place, mask, table, w_ref, x_ref, y_ref, d_ref, *rest):
+    *outs, taken = rest
+    r = place[0]
+    row_blocks = w_ref.shape[0] // BLOCK
+    side = lax.broadcasted_iota(jnp.int32, (BLOCK, TILE), 1) // BLOCK
+    for i, ref in enumerate((x_ref, y_ref, d_ref)):
+
+        @pl.when(table[2 * SLOTS + OWN] == i + 1)
+        def _():
+            taken[...] = ref[...]
+
+    slot = first
+    for out in outs:
+        for t in range(out.shape[1] // TILE):
+            halves = []
+            for half in range(2):
+                source, col = table[SLOTS + slot], table[slot]
+                slot += 1
+                own = jnp.minimum(source, OWN - 1)
+                other = jnp.maximum(source - OWN, 0)
+                halves.append((
+                    source >= OWN, col, (source & 1) != half,
+                    pl.ds(pl.multiple_of((own >> 1) * TILE, TILE), TILE),
+                    pl.ds(pl.multiple_of((other >> 1) * TILE, TILE), TILE),
+                ))
+
+            def block(i, _):
+                rows = pl.ds(pl.multiple_of(i * BLOCK, BLOCK), BLOCK)
+                values = []
+                for is_taken, col, swap, own, other in halves:
+                    value = jnp.where(is_taken, taken[rows, other], w_ref[rows, own])
+                    value = jnp.where(swap, swap_halves(value), value)
+                    values.append(jnp.where(mask[r * row_blocks + i, col] != 0, value, jnp.zeros_like(value)))
+                out[rows, t * TILE : (t + 1) * TILE] = jnp.where(side == 0, values[0], values[1])
+                return 0
+
+            lax.fori_loop(0, row_blocks, block, 0)
+
+
+def whole_columns(first, widths, place, mask, table, weight, taken):
+    rows, width = weight.shape[0], OWN * BLOCK
+    full = lambda shape: pl.BlockSpec(shape, lambda i, place, mask, table: (0, 0))
+    return pl.pallas_call(
+        functools.partial(whole_kernel, first),
+        grid_spec=pltpu.PrefetchScalarGridSpec(
+            num_scalar_prefetch=3,
+            grid=(1,),
+            in_specs=[pl.BlockSpec((rows, width), lambda i, place, mask, table: (0, place[2]))]
+            + [full(taken[0].shape)] * 3,
+            out_specs=[full((rows, w * BLOCK)) for w in widths],
+            scratch_shapes=[pltpu.VMEM(taken[0].shape, jnp.bfloat16)],
+        ),
+        out_shape=[jax.ShapeDtypeStruct((rows, w * BLOCK), jnp.bfloat16) for w in widths],
+        cost_estimate=BRIEF,
+        compiler_params=vmem(48),
+    )(place, mask, table, weight, *taken)
+
+
+def gelu(preact):
+    return jax.nn.gelu(preact, approximate=True).astype(jnp.bfloat16)
+
+
+def light_sources(me, nearest):
+    if nearest:
+        return [(me, me >= 0), (me - 1, me >= 1), (me + 1, me <= 2)]
+    side = jnp.where(me <= 1, 1, -1)
+    return [(me + 2 * side, me >= 0), (me + 3 * side, (me == 0) | (me == 3))]
+
+
+def light_kernel(nearest, place, mask, table, *rest):
+    n = 3 if nearest else 2
+    pieces, rest = rest[: n if nearest else 2 * n], rest[n if nearest else 2 * n :]
+    if nearest:
+        here_ref, total, weight, blocks, lines, sems = rest
+    else:
+        here_ref, before, out_ref, total, weight, blocks, lines, sems, before_sem = rest
+        load = pltpu.make_async_copy(before, total, before_sem)
+    step = pl.program_id(0)
+    row_blocks = weight.shape[0] // BLOCK
+    zero = lines.shape[1] - BLOCK
+    me = place[0]
+    sources = light_sources(me, nearest)
+
+    def copies(i):
+        slot = blocks.at[pl.ds(i * SIZE, SIZE)]
+        if nearest:
+            return [(sources[i][1], pltpu.make_async_copy(pieces[i], slot, sems.at[i]))]
+        return [
+            (sources[i][1] & (me <= 1 if k else me > 1), pltpu.make_async_copy(pieces[2 * i + k], slot, sems.at[i]))
+            for k in range(2)
+        ]
+
+    @pl.when(step == 0)
+    def _():
+        for i in range(n):
+            for there, copy in copies(i):
+                pl.when(there)(copy.start)
+        for half in range(2):
+            lines[half, zero : zero + BLOCK, :] = jnp.zeros((BLOCK, TILE), jnp.bfloat16)
+        if nearest:
+            total[...] = jnp.zeros_like(total)
+        else:
+            load.start()
+
+    for i in range(n):
+        for there, copy in copies(i):
+            pl.when((step == i) & there)(copy.wait)
+
+    source, valid = sources[0]
+    for i in range(1, n):
+        source = jnp.where(step == i, sources[i][0], source)
+        valid = jnp.where(step == i, sources[i][1], valid)
+
+    @pl.when(valid)
+    def _():
+        side = lax.broadcasted_iota(jnp.int32, (BLOCK, TILE), 1) // BLOCK
+        many = 11
+
+        def spread(t, _):
+            value = blocks[pl.ds(pl.multiple_of(step * SIZE + t * many * BLOCK, BLOCK), many * BLOCK), :]
+            other = swap_halves(value)
+            for k in range(many):
+                first = pl.ds(pl.multiple_of(2 * (t * many + k) * BLOCK, BLOCK), BLOCK)
+                second = pl.ds(pl.multiple_of(2 * (t * many + k) * BLOCK + BLOCK, BLOCK), BLOCK)
+                rows = slice(k * BLOCK, (k + 1) * BLOCK)
+                lines[0, first, :] = value[rows]
+                lines[1, first, :] = other[rows]
+                lines[0, second, :] = other[rows]
+                lines[1, second, :] = value[rows]
+            return 0
+
+        lax.fori_loop(0, CAP // many, spread, 0)
+
+        def pair(t, row):
+            cols = [table[2 * t], table[2 * t + 1]]
+            kept = [[mask[source * row_blocks + i, col] * BLOCK for i in range(row_blocks)] for col in cols]
+            at = [row, row + sum(kept[0])]
+            lanes = pl.ds(pl.multiple_of(t * TILE, TILE), TILE)
+            for i in range(row_blocks):
+                values = []
+                for half in range(2):
+                    rows = pl.multiple_of(jnp.where(kept[half][i] != 0, at[half], zero), BLOCK)
+                    values.append(lines[half, pl.ds(rows, BLOCK), :])
+                    at[half] = at[half] + kept[half][i]
+                weight[i * BLOCK : (i + 1) * BLOCK, lanes] = jnp.where(side == 0, values[0], values[1])
+            return at[1]
+
+        lax.fori_loop(0, LIGHT // 2, pair, jnp.int32(0))
+        if not nearest:
+            pl.when(step == 0)(load.wait)
+        for first in range(0, total.shape[0], ROW_TILE):
+            rows = slice(first, first + ROW_TILE)
+            total[rows, :] += jnp.dot(here_ref[rows, :], weight[...], preferred_element_type=jnp.float32)
+
+    if not nearest:
+
+        @pl.when(step == n - 1)
+        def _():
+            out_ref[...] = gelu(total[...])
+
+
+def light_columns(place, mask, table, pieces, here, before=None):
+    rows, width = here.shape
+    depth, columns = width // 4, LIGHT * BLOCK
+    full = pl.BlockSpec((rows, columns), lambda i, *_: (0, 0))
+    nearest = before is None
+    n = 3 if nearest else 2
+
+    def block(i, place, *_):
+        source = jnp.int32(0)
+        last = jnp.int32(0)
+        for k, (at, valid) in enumerate(light_sources(place[0], nearest)):
+            last = jnp.where(valid, at, last)
+            source = jnp.where(i == k, last, source)
+        return 0, source
+
+    scratch = [
+        pltpu.VMEM((depth, columns), jnp.bfloat16),
+        pltpu.VMEM((n * SIZE, TILE), jnp.bfloat16),
+        pltpu.VMEM((2, LIGHT * depth + BLOCK, TILE), jnp.bfloat16),
+        pltpu.SemaphoreType.DMA((n,)),
+    ]
+    if not nearest:
+        scratch = [pltpu.VMEM((rows, columns), jnp.float32), *scratch, pltpu.SemaphoreType.DMA]
+    any_space = pl.BlockSpec(memory_space=pl.ANY)
+    return pl.pallas_call(
+        functools.partial(light_kernel, nearest),
+        grid_spec=pltpu.PrefetchScalarGridSpec(
+            num_scalar_prefetch=3,
+            grid=(n,),
+            in_specs=[any_space] * len(pieces) + [pl.BlockSpec((rows, depth), block)] + ([] if nearest else [any_space]),
+            out_specs=full,
+            scratch_shapes=scratch,
+        ),
+        out_shape=jax.ShapeDtypeStruct((rows, columns), jnp.float32 if nearest else jnp.bfloat16),
+        cost_estimate=BRIEF,
+        compiler_params=vmem(52),
+    )(place, mask, table, *pieces, here, *([] if nearest else [before]))
+
+
+def product_kernel(place, *rest):
+    *pieces, here_ref, end_ref, first_here, second_here, first_end, second_end, weight, sems = rest
+    depth, columns = pieces[0].shape
+    step = pl.program_id(0)
+    half = pl.num_programs(0) // 2
+
+    works = place[4] != 0
+
+    @pl.when(works & (step == 0))
+    def _():
+        copies = []
+        for i, piece in enumerate(pieces):
+            rows = pl.ds(pl.multiple_of(place[i % 4] * depth, depth), depth)
+            lanes = pl.ds((i // 4) * columns, columns)
+            copies.append(pltpu.make_async_copy(piece, weight.at[rows, lanes], sems.at[i]))
+        for copy in copies:
+            copy.start()
+        for copy in copies:
+            copy.wait()
+
+    def finish(preact, first_ref, second_ref):
+        hidden = gelu(preact)
+        first_ref[...] = hidden[:, :columns]
+        second_ref[...] = hidden[:, columns:]
+
+    @pl.when(works & (step < half))
+    def _():
+        finish(jnp.dot(here_ref[...], weight[...], preferred_element_type=jnp.float32), first_here, second_here)
+
+    @pl.when(works & (step >= half))
+    def _():
+        parts, _, piece = end_ref.shape
+        total = jnp.zeros((end_ref.shape[1], 2 * columns), jnp.float32)
+        for i in range(parts):
+            rows = slice(i * piece, (i + 1) * piece)
+            total += jnp.dot(end_ref[i], weight[rows, :], preferred_element_type=jnp.float32)
+        finish(total, first_end, second_end)
+
+
+def products(place, pieces, here, end):
+    columns = pieces[0].shape[1]
+    rows, width = here.shape
+    steps = rows // ROW_TILE
+    return pl.pallas_call(
+        product_kernel,
+        grid_spec=pltpu.PrefetchScalarGridSpec(
+            num_scalar_prefetch=1,
+            grid=(2 * steps,),
+            in_specs=[pl.BlockSpec(memory_space=pl.ANY)] * 8
+            + [pl.BlockSpec((ROW_TILE, width), lambda i, place: (jnp.minimum(i, steps - 1) * place[4], 0))]
+            + [pl.BlockSpec((end.shape[0], ROW_TILE, end.shape[2]), lambda i, place: (0, jnp.maximum(i - steps, 0) * place[4], 0))],
+            out_specs=[pl.BlockSpec((ROW_TILE, columns), lambda i, place: (jnp.minimum(i, steps - 1), 0))] * 2
+            + [pl.BlockSpec((ROW_TILE, columns), lambda i, place: (jnp.maximum(i - steps, 0), 0))] * 2,
+            scratch_shapes=[pltpu.VMEM((width, 2 * columns), jnp.bfloat16), pltpu.SemaphoreType.DMA((8,))],
+        ),
+        out_shape=[jax.ShapeDtypeStruct((rows, columns), jnp.bfloat16)] * 4,
+        cost_estimate=BRIEF,
+        compiler_params=vmem(52),
+    )(place, *pieces, here, end)
+
+
+def order_kernel(table, *rest):
+    *sources, out_ref, results = rest
+    at = 0
+    for ref in sources:
+        results[:, at : at + ref.shape[1]] = ref[...]
+        at += ref.shape[1]
+    side = lax.broadcasted_iota(jnp.int32, (out_ref.shape[0], TILE), 1) // BLOCK
+    for t in range(OWN // 2):
+        values = []
+        for half in range(2):
+            slot = table[2 * SLOTS + 2 * t + half]
+            value = results[:, pl.ds(pl.multiple_of((slot >> 1) * TILE, TILE), TILE)]
+            values.append(jnp.where((slot & 1) == half, value, swap_halves(value)))
+        out_ref[:, t * TILE : (t + 1) * TILE] = jnp.where(side == 0, values[0], values[1])
+
+
+def in_order(table, sources):
+    rows = sources[0].shape[0]
+    tile = rows // 4
+    widths = [s.shape[1] for s in sources]
+    return pl.pallas_call(
+        order_kernel,
+        grid_spec=pltpu.PrefetchScalarGridSpec(
+            num_scalar_prefetch=1,
+            grid=(4,),
+            in_specs=[pl.BlockSpec((tile, w), lambda i, table: (i, 0)) for w in widths],
+            out_specs=pl.BlockSpec((tile, OWN * BLOCK), lambda i, table: (i, 0)),
+            scratch_shapes=[pltpu.VMEM((tile, sum(widths)), jnp.bfloat16)],
+        ),
+        out_shape=jax.ShapeDtypeStruct((rows, OWN * BLOCK), jnp.bfloat16),
+        cost_estimate=BRIEF,
+        compiler_params=vmem(32),
+    )(table, *sources)
+
+
+def line_body(tokens, up_weight, block_mask):
+    depth, hidden_dev = up_weight.shape
+    r, c, p = (lax.axis_index(a).astype(jnp.int32) for a in ("row", "col", "rep"))
+    share = hidden_dev // CORES
+    rows, width = tokens.shape
+    parts = CHIPS * CORES
+    piece = width // parts
+    place = jnp.stack([r, c, p])
+    is_middle = (r == 1) | (r == 2)
+
+    given_mask = block_mask
+    block_mask = jnp.pad(block_mask, ((0, 0), (0, 1)))
+    counts = block_mask.reshape(lax.axis_size("row"), -1, block_mask.shape[1]).sum(1)
+    count = counts.sum(0)
+    table, shared, packed, own_heavy = pack_columns(place, block_mask, count, up_weight)
+    most = most_packed(counts[:, :EMPTY], count[:EMPTY], shared)
+
+    up1, down1 = lax.ppermute(packed, "row", UP), lax.ppermute(packed, "row", DOWN)
+    handed = []
+    for i in range(len(SWAPS)):
+        other = c ^ (i + 1)
+        k = other - (other > c).astype(jnp.int32)
+        handed.append(lax.dynamic_slice_in_dim(up_weight, p * share + k * SPARE * BLOCK, SPARE * BLOCK, 1))
+    taken = [lax.ppermute(handed[0], "col", SWAP_X), lax.ppermute(handed[1], "col", SWAP_Y)]
+    mid2 = lax.ppermute(own_heavy, "row", MIDDLE)
+    up1, down1, taken = lax.optimization_barrier((up1, down1, taken))
+    up2, down2 = lax.ppermute(up1, "row", UP[1:]), lax.ppermute(down1, "row", DOWN[1:])
+    taken.append(lax.ppermute(after(handed[2], taken), "col", SWAP_DIAGONAL))
+    light = light_columns(place, block_mask, table, [packed, up1, down1], tokens)
+    mine = lax.dynamic_slice_in_dim(tokens, (c * CORES + p) * piece, piece, 1)
+    mine = lax.ppermute(after(mine, packed), "row", INWARD)
+    end = lax.all_gather(after(mine, up2, down2, taken[2], light), ("col", "rep"), axis=0, tiled=True)
+    (first,) = whole_columns(LIGHT + HEAVY, (HEAVY,), place, block_mask, table, up_weight, taken)
+    near2 = lax.ppermute(after(own_heavy, mine), "row", INWARD)
+    up2, down2, first, mine = lax.optimization_barrier((up2, down2, first, mine))
+    up3, down3 = lax.ppermute(up2, "row", UP[2:]), lax.ppermute(down2, "row", DOWN[2:])
+    mid1 = lax.ppermute(after(first, mid2), "row", MIDDLE)
+    near1 = lax.ppermute(first, "row", INWARD)
+    far2 = lax.ppermute(near2, "row", MIDDLE)
+    far1 = lax.ppermute(after(near1, mid1), "row", MIDDLE)
+    pieces = [up2, down2, up3, down3]
+
+    end = end.reshape(parts, rows, piece)
+    at = jnp.stack([r, 3 - r, jnp.where(r <= 1, 0, 3), jnp.where(r <= 1, 3, 0), is_middle.astype(jnp.int32)])
+    at = jnp.where(is_middle, at, jnp.zeros_like(at))
+
+    weights = [first, mid1, near1, far1, own_heavy, mid2, near2, far2]
+    first_here, second_here, first_end, second_end = products(at, weights, tokens, end)
+    back1 = lax.ppermute(first_end, "row", OUTWARD)
+    back2 = lax.ppermute(second_end, "row", OUTWARD)
+    light = light_columns(place, block_mask, after(table, first_end), pieces, tokens, light)
+    hidden1 = jnp.where(is_middle, after(first_here, light), back1)
+    home = [lax.ppermute(hidden1, "col", pairs) for pairs in SWAPS]
+    hidden2 = jnp.where(is_middle, second_here, after(back2, *home))
+    return lax.cond(
+        most > 2 * CAP,
+        lambda table, *_: gather_body(tokens, up_weight, given_mask),
+        lambda table, *results: in_order(table, results),
+        table, light, hidden2, hidden1, *home,
+    )
+
+
 def solution(mesh):
     in_specs = (P("row", None), P("row", "col"), P())
     out_specs = P("row", ("col", "rep"))
+
+    def body(tokens, up_weight, block_mask):
+        line = dict(mesh.shape) == {"row": 4, "col": CHIPS, "rep": CORES}
+        line = line and up_weight.shape[1] == CORES * OWN * BLOCK and tokens.shape[0] % (4 * ROW_TILE) in (0, 2 * ROW_TILE)
+        return (line_body if line else gather_body)(tokens, up_weight, block_mask)
+
     return jax.shard_map(body, mesh=mesh, in_specs=in_specs, out_specs=out_specs, check_vma=False)

time: 272 us -> 206 us (0.76)
  the two profiles are of different devices: /device:TPU:0 before, /device:TPU:10 now
where the time goes in v2:
time: 206 us; the launch traced here: 205 us
  Pallas kernels  71.7 us (35%)
  waiting for transfers between devices  59.9 us (29%)
  starting transfers between devices  45.1 us (22%)
  between operations  14.5 us (7%)
  local copies, waits for them, and re-layouts  10.1 us (5%)
  other arithmetic  3.48 us (2%)
    pallas_call x2, Pallas kernels, light_columns(): pl.pallas_call(functools.partial(light_kernel, nearest), grid_spec=pltpu....  32.5 us
    pallas_call x1, Pallas kernels, products(): pl.pallas_call(product_kernel, grid_spec=pltpu.PrefetchScalarGridSpec(num...  17.6 us
    ppermute x1, waiting for transfers between devices, line_body(): lax.ppermute(handed[0], 'col', SWAP_X)  14.1 us
    ppermute x1, waiting for transfers between devices, line_body(): mid1 = lax.ppermute(after(first, mid2), 'row', MIDDLE)  12.4 us
    ppermute x3, waiting for transfers between devices, line_body(): home = [lax.ppermute(hidden1, 'col', pairs) for pairs in SWAPS]  11.9 us
    ppermute x1, waiting for transfers between devices, line_body(): far1 = lax.ppermute(after(near1, mid1), 'row', MIDDLE)  10.3 us
    pallas_call x1, Pallas kernels, pack_columns(): pl.pallas_call(pack_kernel, grid_spec=pltpu.PrefetchScalarGridSpec(num_sc...  9.95 us
    pallas_call x1, Pallas kernels, whole_columns(): pl.pallas_call(functools.partial(whole_kernel, first), grid_spec=pltpu.Pr...  7.65 us
  transfers between devices with their start and end apart: 22, of which 11 were waited for; matrix products, arithmetic and copies ran while one was open for 3% of the time, Pallas kernels for 28%

profile of v2, /device:TPU:10, one launch (start us, length us, event | category | flops | bytes accessed | tf_op | source)
XLA Modules:
  0.0 204.8 jit_solution(5530909896516024687)
XLA Ops:
  6.5 0.9 pad_reduce_fusion
  7.5 0.1 pad_add_fusion.place
  7.5 10.0 %shard_map.39 = (s32[69]{0:T(128)}, s32[9]{0:T(128)S(1)}, bf16[4224,128]{1,0:T(8,128)(2,1)S(1)}, bf16[1280,256]{1,0:T(8,128)(2,1)S(1)}) custom-call(s32[3]{0:T(128)S(1)} %pad_add_fusion.place, s32[80,161]{1,0:T(8,128)S(1)} %get-tuple-element.107.mask, s32[161]{0:T(256)S(1)} %get-tuple-element.106.count, bf16[1280,2560]{1,0:T(8,128)(2,1)} %w_ref.3), custom_call_target="tpu_custom_call" | custom-call | flops 1 | bytes 1 | tf_op jit(solution)/shard_map/pallas_call | solution.py:198
  17.5 3.5 %collective-permute-start = (bf16[4224,128]{1,0:T(8,128)(2,1)S(1)}, bf16[4224,128]{1,0:T(8,128)(2,1)}, u32[]{:S(2)}, u32[]{:S(2)}) collective-permute-start(bf16[4224,128]{1,0:T(8,128)(2,1)S(1)} %get-tuple-element.71.rest_0_), channel_id=1, source_target_pairs={{0,8},{8,16},{16,24},{1,9},{9,17},{17,25},{2,10},{10,18},{18,26},{... | collective-permute-start | bytes 3244040 | tf_op jit(solution)/shard_map/ppermute | solution.py:556
  21.0 3.3 %collective-permute-start.1 = (bf16[4224,128]{1,0:T(8,128)(2,1)S(1)}, bf16[4224,128]{1,0:T(8,128)(2,1)}, u32[]{:S(2)}, u32[]{:S(2)}) collective-permute-start(bf16[4224,128]{1,0:T(8,128)(2,1)S(1)} %get-tuple-element.71.rest_0_), channel_id=1, source_target_pairs={{24,16},{16,8},{8,0},{25,17},{17,9},{9,1},{26,18},{18,10},{10,2},{... | collective-permute-start | bytes 3244040 | tf_op jit(solution)/shard_map/ppermute | solution.py:556
  24.4 2.8 %constant_dynamic-slice_fusion.1 = (bf16[1280,256]{1,0:T(8,128)(2,1)}, bf16[1280,256]{1,0:T(8,128)(2,1)}, bf16[1280,256]{1,0:T(8,128)(2,1)}) fusion(bf16[1280,2560]{1,0:T(8,128)(2,1)} %w_ref.3, s32[]{:T(128)S(6)} %select_n.161, s32[]{:T(128)S(6)} %select_n.160, s32[]{:T(128)S(6)} %select_n.159), kind=kLoop, calls=%fused_computation.73 | loop fusion | bytes 3932172 | tf_op jit(solution)/shard_map/dynamic_slice | solution.py:561
  27.2 0.5 collective-permute-start.2
  27.8 1.5 collective-permute-start.3
  29.3 14.1 %collective-permute-done.2.x_ref = bf16[1280,256]{1,0:T(8,128)(2,1)S(1)} collective-permute-done((bf16[1280,256]{1,0:T(8,128)(2,1)}, bf16[1280,256]{1,0:T(8,128)(2,1)S(1)}, u32[]{:S(2)}, u32[]{:S(2)}) %collective-permute-start.2) | collective-permute-done | bytes 655392 | tf_op jit(solution)/shard_map/ppermute | solution.py:562
  43.4 0.3 collective-permute-done.3.y_ref
  43.6 0.9 copy-done.3
  44.5 0.6 collective-permute-done.rest_1_
  45.1 3.2 %collective-permute-done.1.rest_2_ = bf16[4224,128]{1,0:T(8,128)(2,1)} collective-permute-done((bf16[4224,128]{1,0:T(8,128)(2,1)S(1)}, bf16[4224,128]{1,0:T(8,128)(2,1)}, u32[]{:S(2)}, u32[]{:S(2)}) %collective-permute-start.1) | collective-permute-done | bytes 1081376 | tf_op jit(solution)/shard_map/ppermute | solution.py:556
  48.4 3.5 %collective-permute-start.4 = (bf16[4224,128]{1,0:T(8,128)(2,1)}, bf16[4224,128]{1,0:T(8,128)(2,1)S(1)}, u32[]{:S(2)}, u32[]{:S(2)}) collective-permute-start(bf16[4224,128]{1,0:T(8,128)(2,1)} %collective-permute-done.rest_1_), channel_id=1, source_target_pairs={{8,16},{16,24},{9,17},{17,25},{10,18},{18,26},{11,19},{19,27},{12,... | collective-permute-start | bytes 3244040 | tf_op jit(solution)/shard_map/ppermute | solution.py:565
  51.9 1.9 collective-permute-start.5
  53.8 1.3 constant_dynamic-slice_fusion
  55.1 1.3 collective-permute-start.7
  56.4 1.6 collective-permute-start.6
  58.0 0.7 copy-done.6
  58.7 20.7 %shard_map.41.rest_5_ = f32[768,1024]{1,0:T(8,128)} custom-call(s32[3]{0:T(128)S(1)} %copy-done.6, s32[80,161]{1,0:T(8,128)S(1)} %get-tuple-element.107.mask, s32[69]{0:T(128)} %get-tuple-element.89.table, bf16[4224,128]{1,0:T(8,128)(2,1)S(1)} %get-tuple-element.71.rest_0_, bf16[4224,128]{1,0:T(8,128)(2,1)} %collective-permute-done.rest_1_, ...), custom_call_target="tpu_custom_call" | custom-call | flops 1 | bytes 1 | tf_op jit(solution)/shard_map/pallas_call | solution.py:428
  79.3 0.0 collective-permute-done.7
  79.3 0.0 collective-permute-done.6.d_ref
  79.4 0.0 all-gather.5.cloned.1.call-update
  79.4 4.9 %collective-permute-start.8 = (bf16[1280,256]{1,0:T(8,128)(2,1)S(1)}, bf16[1280,256]{1,0:T(8,128)(2,1)S(1)}, u32[]{:S(2)}, u32[]{:S(2)}) collective-permute-start(bf16[1280,256]{1,0:T(8,128)(2,1)S(1)} %get-tuple-element.83.rest_4_), channel_id=1, source_target_pairs={{8,16},{16,8},{9,17},{17,9},{10,18},{18,10},{11,19},{19,11},{12,20... | collective-permute-start | bytes 1966088 | tf_op jit(solution)/shard_map/ppermute | solution.py:563
  84.3 1.3 collective-permute-start.12
  85.6 1.1 copy-done.2
  86.7 1.2 copy-done.4
  87.9 0.7 copy-done.7
  88.6 7.6 %shard_map.40.rest_0_ = bf16[1280,256]{1,0:T(8,128)(2,1)S(1)} custom-call(s32[3]{0:T(128)S(1)} %copy-done.7, s32[80,161]{1,0:T(8,128)S(1)} %get-tuple-element.107.mask, s32[69]{0:T(128)} %get-tuple-element.89.table, bf16[1280,2560]{1,0:T(8,128)(2,1)} %w_ref.3, bf16[1280,256]{1,0:T(8,128)(2,1)S(1)} %copy-done.2, bf16[1280,256]{1,0:T(8,128)(2,1)S(1)} %copy-done.4, ...), custom_call_target="tpu_custom_call" | custom-call | flops 1 | bytes 1 | tf_op jit(solution)/shard_map/pallas_call | solution.py:285
  96.2 0.8 collective-permute-done.8.rest_5_
  97.0 3.6 %collective-permute-start.9 = (bf16[1280,256]{1,0:T(8,128)(2,1)S(1)}, bf16[1280,256]{1,0:T(8,128)(2,1)S(1)}, u32[]{:S(2)}, u32[]{:S(2)}) collective-permute-start(bf16[1280,256]{1,0:T(8,128)(2,1)S(1)} %shard_map.40.rest_0_), channel_id=1, source_target_pairs={{8,16},{16,8},{9,17},{17,9},{10,18},{18,10},{11,19},{19,11},{12,20... | collective-permute-start | bytes 1966088 | tf_op jit(solution)/shard_map/ppermute | solution.py:575
  100.7 1.3 collective-permute-start.10
  102.0 2.2 %collective-permute-start.13 = (bf16[1280,256]{1,0:T(8,128)(2,1)S(1)}, bf16[1280,256]{1,0:T(8,128)(2,1)}, u32[]{:S(2)}, u32[]{:S(2)}) collective-permute-start(bf16[1280,256]{1,0:T(8,128)(2,1)S(1)} %collective-permute-done.12.rest_6_), channel_id=1, source_target_pairs={{8,16},{16,8},{9,17},{17,9},{10,18},{18,10},{11,19},{19,11},{12,20... | collective-permute-start | bytes 1966088 | tf_op jit(solution)/shard_map/ppermute | solution.py:577
  104.2 12.4 %collective-permute-done.9.rest_1_ = bf16[1280,256]{1,0:T(8,128)(2,1)S(1)} collective-permute-done((bf16[1280,256]{1,0:T(8,128)(2,1)S(1)}, bf16[1280,256]{1,0:T(8,128)(2,1)S(1)}, u32[]{:S(2)}, u32[]{:S(2)}) %collective-permute-start.9) | collective-permute-done | bytes 655392 | tf_op jit(solution)/shard_map/ppermute | solution.py:575
  116.6 3.6 %collective-permute-start.11 = (bf16[1280,256]{1,0:T(8,128)(2,1)}, bf16[1280,256]{1,0:T(8,128)(2,1)}, u32[]{:S(2)}, u32[]{:S(2)}) collective-permute-start(bf16[1280,256]{1,0:T(8,128)(2,1)} %collective-permute-done.10.rest_2_), channel_id=1, source_target_pairs={{8,16},{16,8},{9,17},{17,9},{10,18},{18,10},{11,19},{19,11},{12,20... | collective-permute-start | bytes 1966088 | tf_op jit(solution)/shard_map/ppermute | solution.py:578
  120.2 1.7 collective-permute-start.15
  122.0 2.3 %collective-permute-start.16 = (bf16[4224,128]{1,0:T(8,128)(2,1)}, bf16[4224,128]{1,0:T(8,128)(2,1)}, u32[]{:S(2)}, u32[]{:S(2)}) collective-permute-start(bf16[4224,128]{1,0:T(8,128)(2,1)} %collective-permute-done.5.rest_1_), channel_id=1, source_target_pairs={{8,0},{9,1},{10,2},{11,3},{12,4},{13,5},{14,6},{15,7}} | collective-permute-start | bytes 3244040 | tf_op jit(solution)/shard_map/ppermute | solution.py:574
  124.2 0.1 slice.12
  124.3 0.1 stack.40
  124.4 0.1 and_select_fusion.5
  124.5 6.3 %collective-permute-done.13.rest_7_ = bf16[1280,256]{1,0:T(8,128)(2,1)} collective-permute-done((bf16[1280,256]{1,0:T(8,128)(2,1)S(1)}, bf16[1280,256]{1,0:T(8,128)(2,1)}, u32[]{:S(2)}, u32[]{:S(2)}) %collective-permute-start.13) | collective-permute-done | bytes 655392 | tf_op jit(solution)/shard_map/ppermute | solution.py:577
  130.7 10.3 %collective-permute-done.11.rest_3_ = bf16[1280,256]{1,0:T(8,128)(2,1)} collective-permute-done((bf16[1280,256]{1,0:T(8,128)(2,1)}, bf16[1280,256]{1,0:T(8,128)(2,1)}, u32[]{:S(2)}, u32[]{:S(2)}) %collective-permute-start.11) | collective-permute-done | bytes 655392 | tf_op jit(solution)/shard_map/ppermute | solution.py:578
  141.0 17.6 %shard_map.42 = (bf16[768,256]{1,0:T(8,128)(2,1)S(1)}, bf16[768,256]{1,0:T(8,128)(2,1)}, bf16[768,256]{1,0:T(8,128)(2,1)S(1)}, bf16[768,256]{1,0:T(8,128)(2,1)S(1)}) custom-call(s32[5]{0:T(128)S(1)} %broadcast_select_fusion.2.place, bf16[1280,256]{1,0:T(8,128)(2,1)S(1)} %shard_map.40.rest_0_, bf16[1280,256]{1,0:T(8,128)(2,1)} %copy-done.17, ...), custom_call_target="tpu_custom_call" | custom-call | flops 1 | bytes 1 | tf_op jit(solution)/shard_map/pallas_call | solution.py:486
  158.6 2.0 collective-permute-start.17
  160.6 0.1 select_reduce_fusion.1
  160.8 0.1 slice_select_fusion.1
  160.8 0.2 convert_reduce_fusion
  161.1 11.9 %shard_map.43 = bf16[768,1024]{1,0:T(8,128)(2,1)} custom-call(s32[3]{0:T(128)S(1)} %copy-done.8, s32[80,161]{1,0:T(8,128)S(1)} %get-tuple-element.107.mask, s32[69]{0:T(128)S(1)} %copy-done.20, bf16[4224,128]{1,0:T(8,128)(2,1)S(1)} %collective-permute-done.4.rest_0_, bf16[4224,128]{1,0:T(8,128)(2,1)} %collective-permute-done.5.rest_1_, ...), custom_call_target="tpu_custom_call" | custom-call | flops 1 | bytes 1 | tf_op jit(solution)/shard_map/pallas_call | solution.py:428
  173.0 1.3 collective-permute-start.14
  174.3 0.1 broadcast_select_fusion.1
  174.4 1.6 collective-permute-start.18
  176.0 0.5 collective-permute-start.19
  176.5 1.5 collective-permute-start.20
  178.0 0.1 reshape.149
  178.1 0.1 reduce_sum.59
  178.2 0.6 reduce_max.9
  179.5 0.1 collective-permute-done.14
  179.6 6.5 %collective-permute-done.18 = bf16[768,256]{1,0:T(8,128)(2,1)S(1)} collective-permute-done((bf16[768,256]{1,0:T(8,128)(2,1)S(1)}, bf16[768,256]{1,0:T(8,128)(2,1)S(1)}, u32[]{:S(2)}, u32[]{:S(2)}) %collective-permute-start.18) | collective-permute-done | bytes 393248 | tf_op jit(solution)/shard_map/ppermute | solution.py:591
  186.0 5.4 %collective-permute-done.19 = bf16[768,256]{1,0:T(8,128)(2,1)S(1)} collective-permute-done((bf16[768,256]{1,0:T(8,128)(2,1)S(1)}, bf16[768,256]{1,0:T(8,128)(2,1)S(1)}, u32[]{:S(2)}, u32[]{:S(2)}) %collective-permute-start.19) | collective-permute-done | bytes 393248 | tf_op jit(solution)/shard_map/ppermute | solution.py:591
  191.5 5.2 %conditional.1 = (bf16[768,1280]{1,0:T(8,128)(2,1)S(1)}) conditional(s32[]{:T(128)} %convert_element_type.36, (pred[]{:T(512)}, bf16[768,256]{1,0:T(8,128)(2,1)}, bf16[768,256]{1,0:T(8,128)(2,1)S(1)}, s32[69]{0:T(128)S(1)}, bf16[768,1024]{1,0:T(8,128)(2,1)}, /*index=5*/bf16[768,256]{1,0:T(8,128)(2,1)S(1)}, bf16[768,256]{1,0:T(8,128)(2,1)S(1)}, ...), branch_computations={%region_7.8_spmd, %region_8.9_spmd} | conditional | flops 16570380288 | bytes 120340720 | solution.py:593
  191.5 1.2 broadcast_select_fusion.rest_1_
  192.7 4.0 %branch_0_fun.1 = bf16[768,1280]{1,0:T(8,128)(2,1)S(1)} custom-call(s32[69]{0:T(128)S(1)} %get-tuple-element.34.table, bf16[768,1024]{1,0:T(8,128)(2,1)} %get-tuple-element.35.rest_0_, bf16[768,256]{1,0:T(8,128)(2,1)S(1)} %broadcast_select_fusion.rest_1_, bf16[768,256]{1,0:T(8,128)(2,1)S(1)} %get-tuple-element.39.rest_2_, ...), custom_call_target="tpu_custom_call" | custom-call | flops 1 | bytes 1 | tf_op jit(solution)/shard_map/cond/branch_0_fun/pallas_call | solution.py:524
  196.7 0.0 copy-start.14
  196.7 1.3 copy-done.14
  (48 shorter events, 0.1 us)
Async XLA Ops:
  6.5 134.5 %all-gather.5.cloned.1.call-start = ((), (), s32[]{:S(2)}) async-start(), calls=%async_computation.1 | async-start | bytes 8847360 | tf_op jit(solution)/shard_map/all_gather | solution.py:570
  7.5 13.6 %copy-start.9 = (s32[161]{0:T(256)}, s32[161]{0:T(256)S(1)}, u32[]{:S(2)}) copy-start(s32[161]{0:T(256)S(1)} %get-tuple-element.106.count) | copy-start | bytes 1936
  7.5 10.0 %copy-start.5 = (s32[3]{0:T(128)}, s32[3]{0:T(128)S(1)}, u32[]{:S(2)}) copy-start(s32[3]{0:T(128)S(1)} %pad_add_fusion.place) | copy-start | bytes 40
  17.5 9.7 %copy-start.11 = (s32[9]{0:T(128)}, s32[9]{0:T(128)S(1)}, u32[]{:S(2)}) copy-start(s32[9]{0:T(128)S(1)} %get-tuple-element.70) | copy-start | bytes 112
  17.5 66.8 %copy-start = (bf16[1280,256]{1,0:T(8,128)(2,1)}, bf16[1280,256]{1,0:T(8,128)(2,1)S(1)}, u32[]{:S(2)}) copy-start(bf16[1280,256]{1,0:T(8,128)(2,1)S(1)} %get-tuple-element.83.rest_4_) | copy-start | bytes 1966084
  17.5 27.6 %collective-permute-start = (bf16[4224,128]{1,0:T(8,128)(2,1)S(1)}, bf16[4224,128]{1,0:T(8,128)(2,1)}, u32[]{:S(2)}, u32[]{:S(2)}) collective-permute-start(bf16[4224,128]{1,0:T(8,128)(2,1)S(1)} %get-tuple-element.71.rest_0_), channel_id=1, source_target_pairs={{0,8},{8,16},{16,24},{1,9},{9,17},{17,25},{2,10},{10,18},{18,26},{... | collective-permute-start | bytes 3244040 | tf_op jit(solution)/shard_map/ppermute | solution.py:556
  21.0 27.3 %collective-permute-start.1 = (bf16[4224,128]{1,0:T(8,128)(2,1)S(1)}, bf16[4224,128]{1,0:T(8,128)(2,1)}, u32[]{:S(2)}, u32[]{:S(2)}) collective-permute-start(bf16[4224,128]{1,0:T(8,128)(2,1)S(1)} %get-tuple-element.71.rest_0_), channel_id=1, source_target_pairs={{24,16},{16,8},{8,0},{25,17},{17,9},{9,1},{26,18},{18,10},{10,2},{... | collective-permute-start | bytes 3244040 | tf_op jit(solution)/shard_map/ppermute | solution.py:556
  27.2 16.1 %collective-permute-start.2 = (bf16[1280,256]{1,0:T(8,128)(2,1)}, bf16[1280,256]{1,0:T(8,128)(2,1)S(1)}, u32[]{:S(2)}, u32[]{:S(2)}) collective-permute-start(bf16[1280,256]{1,0:T(8,128)(2,1)} %get-tuple-element.105), channel_id=1, source_target_pairs={{0,2},{2,0},{4,6},{6,4},{1,3},{3,1},{5,7},{7,5},{8,10},{10,8},{12,... | collective-permute-start | bytes 1966088 | tf_op jit(solution)/shard_map/ppermute | solution.py:562
  27.8 15.8 %collective-permute-start.3 = (bf16[1280,256]{1,0:T(8,128)(2,1)}, bf16[1280,256]{1,0:T(8,128)(2,1)S(1)}, u32[]{:S(2)}, u32[]{:S(2)}) collective-permute-start(bf16[1280,256]{1,0:T(8,128)(2,1)} %get-tuple-element.104), channel_id=1, source_target_pairs={{0,4},{4,0},{2,6},{6,2},{1,5},{5,1},{3,7},{7,3},{8,12},{12,8},{10,... | collective-permute-start | bytes 1966088 | tf_op jit(solution)/shard_map/ppermute | solution.py:562
  43.4 36.0 %copy-start.1 = (bf16[1280,256]{1,0:T(8,128)(2,1)}, bf16[1280,256]{1,0:T(8,128)(2,1)S(1)}, u32[]{:S(2)}) copy-start(bf16[1280,256]{1,0:T(8,128)(2,1)S(1)} %collective-permute-done.2.x_ref) | copy-start | bytes 1966084
  43.6 0.9 copy-start.3
  48.4 31.0 %collective-permute-start.4 = (bf16[4224,128]{1,0:T(8,128)(2,1)}, bf16[4224,128]{1,0:T(8,128)(2,1)S(1)}, u32[]{:S(2)}, u32[]{:S(2)}) collective-permute-start(bf16[4224,128]{1,0:T(8,128)(2,1)} %collective-permute-done.rest_1_), channel_id=1, source_target_pairs={{8,16},{16,24},{9,17},{17,25},{10,18},{18,26},{11,19},{19,27},{12,... | collective-permute-start | bytes 3244040 | tf_op jit(solution)/shard_map/ppermute | solution.py:565
  51.9 27.5 %collective-permute-start.5 = (bf16[4224,128]{1,0:T(8,128)(2,1)}, bf16[4224,128]{1,0:T(8,128)(2,1)}, u32[]{:S(2)}, u32[]{:S(2)}) collective-permute-start(bf16[4224,128]{1,0:T(8,128)(2,1)} %collective-permute-done.1.rest_2_), channel_id=1, source_target_pairs={{16,8},{8,0},{17,9},{9,1},{18,10},{10,2},{19,11},{11,3},{20,12},{1... | collective-permute-start | bytes 3244040 | tf_op jit(solution)/shard_map/ppermute | solution.py:565
  55.1 24.2 %collective-permute-start.7 = (bf16[768,640]{1,0:T(8,128)(2,1)S(1)}, bf16[768,640]{1,0:T(8,128)(2,1)}, u32[]{:S(2)}, u32[]{:S(2)}) collective-permute-start(bf16[768,640]{1,0:T(8,128)(2,1)S(1)} %constant_dynamic-slice_fusion), channel_id=1, source_target_pairs={{0,8},{24,16},{1,9},{25,17},{2,10},{26,18},{3,11},{27,19},{4,12},{... | collective-permute-start | bytes 2949128 | tf_op jit(solution)/shard_map/ppermute | solution.py:569
  56.4 22.9 %collective-permute-start.6 = (bf16[1280,256]{1,0:T(8,128)(2,1)}, bf16[1280,256]{1,0:T(8,128)(2,1)}, u32[]{:S(2)}, u32[]{:S(2)}) collective-permute-start(bf16[1280,256]{1,0:T(8,128)(2,1)} %get-tuple-element.77), channel_id=1, source_target_pairs={{0,6},{6,0},{2,4},{4,2},{1,7},{7,1},{3,5},{5,3},{8,14},{14,8},{10,... | collective-permute-start | bytes 1966088 | tf_op jit(solution)/shard_map/ppermute | solution.py:566
  58.0 0.7 copy-start.6
  79.4 44.8 %copy-start.12 = (s32[9]{0:T(128)S(1)}, s32[9]{0:T(128)}, u32[]{:S(2)}) copy-start(s32[9]{0:T(128)} %copy-done.11) | copy-start | bytes 112
  79.4 17.6 %collective-permute-start.8 = (bf16[1280,256]{1,0:T(8,128)(2,1)S(1)}, bf16[1280,256]{1,0:T(8,128)(2,1)S(1)}, u32[]{:S(2)}, u32[]{:S(2)}) collective-permute-start(bf16[1280,256]{1,0:T(8,128)(2,1)S(1)} %get-tuple-element.83.rest_4_), channel_id=1, source_target_pairs={{8,16},{16,8},{9,17},{17,9},{10,18},{18,10},{11,19},{19,11},{12,20... | collective-permute-start | bytes 1966088 | tf_op jit(solution)/shard_map/ppermute | solution.py:563
  84.3 17.6 %collective-permute-start.12 = (bf16[1280,256]{1,0:T(8,128)(2,1)S(1)}, bf16[1280,256]{1,0:T(8,128)(2,1)S(1)}, u32[]{:S(2)}, u32[]{:S(2)}) collective-permute-start(bf16[1280,256]{1,0:T(8,128)(2,1)S(1)} %get-tuple-element.83.rest_4_), channel_id=1, source_target_pairs={{0,8},{24,16},{1,9},{25,17},{2,10},{26,18},{3,11},{27,19},{4,12},{... | collective-permute-start | bytes 1966088 | tf_op jit(solution)/shard_map/ppermute | solution.py:572
  85.6 1.1 copy-start.2
  86.7 1.2 copy-start.4
  87.9 0.7 copy-start.7
  97.0 19.6 %copy-start.15 = (bf16[1280,256]{1,0:T(8,128)(2,1)}, bf16[1280,256]{1,0:T(8,128)(2,1)S(1)}, u32[]{:S(2)}) copy-start(bf16[1280,256]{1,0:T(8,128)(2,1)S(1)} %collective-permute-done.8.rest_5_) | copy-start | bytes 1966084
  97.0 19.6 %collective-permute-start.9 = (bf16[1280,256]{1,0:T(8,128)(2,1)S(1)}, bf16[1280,256]{1,0:T(8,128)(2,1)S(1)}, u32[]{:S(2)}, u32[]{:S(2)}) collective-permute-start(bf16[1280,256]{1,0:T(8,128)(2,1)S(1)} %shard_map.40.rest_0_), channel_id=1, source_target_pairs={{8,16},{16,8},{9,17},{17,9},{10,18},{18,10},{11,19},{19,11},{12,20... | collective-permute-start | bytes 1966088 | tf_op jit(solution)/shard_map/ppermute | solution.py:575
  100.7 15.9 %collective-permute-start.10 = (bf16[1280,256]{1,0:T(8,128)(2,1)S(1)}, bf16[1280,256]{1,0:T(8,128)(2,1)}, u32[]{:S(2)}, u32[]{:S(2)}) collective-permute-start(bf16[1280,256]{1,0:T(8,128)(2,1)S(1)} %shard_map.40.rest_0_), channel_id=1, source_target_pairs={{0,8},{24,16},{1,9},{25,17},{2,10},{26,18},{3,11},{27,19},{4,12},{... | collective-permute-start | bytes 1966088 | tf_op jit(solution)/shard_map/ppermute | solution.py:576
  102.0 39.0 %copy-start.16 = (bf16[1280,256]{1,0:T(8,128)(2,1)}, bf16[1280,256]{1,0:T(8,128)(2,1)S(1)}, u32[]{:S(2)}) copy-start(bf16[1280,256]{1,0:T(8,128)(2,1)S(1)} %collective-permute-done.12.rest_6_) | copy-start | bytes 1966084
  102.0 28.7 %collective-permute-start.13 = (bf16[1280,256]{1,0:T(8,128)(2,1)S(1)}, bf16[1280,256]{1,0:T(8,128)(2,1)}, u32[]{:S(2)}, u32[]{:S(2)}) collective-permute-start(bf16[1280,256]{1,0:T(8,128)(2,1)S(1)} %collective-permute-done.12.rest_6_), channel_id=1, source_target_pairs={{8,16},{16,8},{9,17},{17,9},{10,18},{18,10},{11,19},{19,11},{12,20... | collective-permute-start | bytes 1966088 | tf_op jit(solution)/shard_map/ppermute | solution.py:577
  116.6 3.7 %copy-start.17 = (bf16[1280,256]{1,0:T(8,128)(2,1)}, bf16[1280,256]{1,0:T(8,128)(2,1)S(1)}, u32[]{:S(2)}) copy-start(bf16[1280,256]{1,0:T(8,128)(2,1)S(1)} %collective-permute-done.9.rest_1_) | copy-start | bytes 1966084
  116.6 24.4 %collective-permute-start.11 = (bf16[1280,256]{1,0:T(8,128)(2,1)}, bf16[1280,256]{1,0:T(8,128)(2,1)}, u32[]{:S(2)}, u32[]{:S(2)}) collective-permute-start(bf16[1280,256]{1,0:T(8,128)(2,1)} %collective-permute-done.10.rest_2_), channel_id=1, source_target_pairs={{8,16},{16,8},{9,17},{17,9},{10,18},{18,10},{11,19},{19,11},{12,20... | collective-permute-start | bytes 1966088 | tf_op jit(solution)/shard_map/ppermute | solution.py:578
  120.2 40.8 %collective-permute-start.15 = (bf16[4224,128]{1,0:T(8,128)(2,1)S(1)}, bf16[4224,128]{1,0:T(8,128)(2,1)}, u32[]{:S(2)}, u32[]{:S(2)}) collective-permute-start(bf16[4224,128]{1,0:T(8,128)(2,1)S(1)} %collective-permute-done.4.rest_0_), channel_id=1, source_target_pairs={{16,24},{17,25},{18,26},{19,27},{20,28},{21,29},{22,30},{23,31}} | collective-permute-start | bytes 3244040 | tf_op jit(solution)/shard_map/ppermute | solution.py:574
  122.0 39.1 %collective-permute-start.16 = (bf16[4224,128]{1,0:T(8,128)(2,1)}, bf16[4224,128]{1,0:T(8,128)(2,1)}, u32[]{:S(2)}, u32[]{:S(2)}) collective-permute-start(bf16[4224,128]{1,0:T(8,128)(2,1)} %collective-permute-done.5.rest_1_), channel_id=1, source_target_pairs={{8,0},{9,1},{10,2},{11,3},{12,4},{13,5},{14,6},{15,7}} | collective-permute-start | bytes 3244040 | tf_op jit(solution)/shard_map/ppermute | solution.py:574
  141.0 19.8 %copy-start.10 = (s32[161]{0:T(256)S(1)}, s32[161]{0:T(256)}, u32[]{:S(2)}) copy-start(s32[161]{0:T(256)} %copy-done.9) | copy-start | bytes 1936
  141.0 20.1 %copy-start.8 = (s32[3]{0:T(128)S(1)}, s32[3]{0:T(128)}, u32[]{:S(2)}) copy-start(s32[3]{0:T(128)} %copy-done.5) | copy-start | bytes 40
  141.0 20.1 %copy-start.20 = (s32[69]{0:T(128)S(1)}, s32[69]{0:T(128)}, u32[]{:S(2)}) copy-start(s32[69]{0:T(128)} %get-tuple-element.89.table) | copy-start | bytes 832
  158.6 15.7 %collective-permute-start.17 = (bf16[768,256]{1,0:T(8,128)(2,1)S(1)}, bf16[768,256]{1,0:T(8,128)(2,1)}, u32[]{:S(2)}, u32[]{:S(2)}) collective-permute-start(bf16[768,256]{1,0:T(8,128)(2,1)S(1)} %get-tuple-element.88), channel_id=1, source_target_pairs={{8,0},{16,24},{9,1},{17,25},{10,2},{18,26},{11,3},{19,27},{12,4},{... | collective-permute-start | bytes 1179656 | tf_op jit(solution)/shard_map/ppermute | solution.py:587
  161.1 30.4 %copy-start.19 = (s32[80,160]{1,0:T(8,128)S(1)}, s32[80,160]{1,0:T(8,128)}, u32[]{:S(2)}) copy-start(s32[80,160]{1,0:T(8,128)} %param.7) | copy-start | bytes 153604
  173.0 6.6 %collective-permute-start.14 = (bf16[768,256]{1,0:T(8,128)(2,1)S(1)}, bf16[768,256]{1,0:T(8,128)(2,1)S(1)}, u32[]{:S(2)}, u32[]{:S(2)}) collective-permute-start(bf16[768,256]{1,0:T(8,128)(2,1)S(1)} %get-tuple-element.86), channel_id=1, source_target_pairs={{8,0},{16,24},{9,1},{17,25},{10,2},{18,26},{11,3},{19,27},{12,4},{... | collective-permute-start | bytes 1179656 | tf_op jit(solution)/shard_map/ppermute | solution.py:588
  174.4 11.6 %collective-permute-start.18 = (bf16[768,256]{1,0:T(8,128)(2,1)S(1)}, bf16[768,256]{1,0:T(8,128)(2,1)S(1)}, u32[]{:S(2)}, u32[]{:S(2)}) collective-permute-start(bf16[768,256]{1,0:T(8,128)(2,1)S(1)} %broadcast_select_fusion.1), channel_id=1, source_target_pairs={{0,2},{2,0},{4,6},{6,4},{1,3},{3,1},{5,7},{7,5},{8,10},{10,8},{12,... | collective-permute-start | bytes 1179656 | tf_op jit(solution)/shard_map/ppermute | solution.py:591
  176.0 15.5 %collective-permute-start.19 = (bf16[768,256]{1,0:T(8,128)(2,1)S(1)}, bf16[768,256]{1,0:T(8,128)(2,1)S(1)}, u32[]{:S(2)}, u32[]{:S(2)}) collective-permute-start(bf16[768,256]{1,0:T(8,128)(2,1)S(1)} %broadcast_select_fusion.1), channel_id=1, source_target_pairs={{0,4},{4,0},{2,6},{6,2},{1,5},{5,1},{3,7},{7,3},{8,12},{12,8},{10,... | collective-permute-start | bytes 1179656 | tf_op jit(solution)/shard_map/ppermute | solution.py:591
  176.5 15.0 %collective-permute-start.20 = (bf16[768,256]{1,0:T(8,128)(2,1)S(1)}, bf16[768,256]{1,0:T(8,128)(2,1)S(1)}, u32[]{:S(2)}, u32[]{:S(2)}) collective-permute-start(bf16[768,256]{1,0:T(8,128)(2,1)S(1)} %broadcast_select_fusion.1), channel_id=1, source_target_pairs={{0,6},{6,0},{2,4},{4,2},{1,7},{7,1},{3,5},{5,3},{8,14},{14,8},{10,... | collective-permute-start | bytes 1179656 | tf_op jit(solution)/shard_map/ppermute | solution.py:591
  191.5 1.2 copy-start.18
  196.7 1.3 copy-start.14
Sparse Core Ops, SparseCore 0:
  79.5 53.2 all-gather.4

commit v3 on v2

--- a/solution.py
+++ b/solution.py
@@ -54,7 +54,7 @@
 SLOTS = OWN + SPARE
 LIGHT = 16
 HEAVY = (SLOTS - LIGHT) // 2
-CAP = 66
+CAP = 70
 TILE = 2 * BLOCK
 EMPTY = CHIPS * CORES * OWN
 ROW_TILE = 384
@@ -75,7 +75,7 @@
     return pltpu.roll(value.astype(jnp.float32), BLOCK, 1).astype(jnp.bfloat16)
 
 
-def make_plan(count, key, table, shared, c, p):
+def make_plan(count, key, table, shared, c, p, margin):
     loads = []
     for group in range(CHIPS * CORES):
         total = count[group * OWN]
@@ -96,13 +96,13 @@
         def given(kept):
             out = []
             for i in range(CHIPS):
-                spare = heavy * kept - OWN * mine[i]
-                n = sum((spare >= k * heavy).astype(jnp.int32) for k in range(1, SPARE + 1))
+                spare = heavy * kept - 2 * OWN * (mine[i] + margin)
+                n = sum((spare >= 2 * k * heavy).astype(jnp.int32) for k in range(1, SPARE + 1))
                 out.append(jnp.where(h == i, 0, n))
             return out
 
         kept = lax.while_loop(
-            lambda kept: OWN - sum(given(kept)) > kept, lambda kept: kept + 1, jnp.int32(OWN - 3 * SPARE)
+            lambda kept: 2 * (OWN - sum(given(kept))) > kept, lambda kept: kept + 1, jnp.int32(2 * (OWN - 3 * SPARE))
         )
         taken.append(given(kept))
         for i in range(CHIPS):
@@ -149,7 +149,7 @@
 
 def pack_kernel(place, mask, count, w_ref, table, shared, packed, own_heavy, key, both, line):
     r, c, p = place[0], place[1], place[2]
-    make_plan(count, key, table, shared, c, p)
+    make_plan(count, key, table, shared, c, p, 3 * mask.shape[0] // 2)
     row_blocks = w_ref.shape[0] // BLOCK
     for t in range(w_ref.shape[1] // TILE):
         value = w_ref[:, t * TILE : (t + 1) * TILE]
@@ -302,14 +302,16 @@
     return jax.nn.gelu(preact, approximate=True).astype(jnp.bfloat16)
 
 
-def light_sources(me, nearest):
-    if nearest:
+def light_sources(me, mode):
+    if mode == "near":
         return [(me, me >= 0), (me - 1, me >= 1), (me + 1, me <= 2)]
     side = jnp.where(me <= 1, 1, -1)
-    return [(me + 2 * side, me >= 0), (me + 3 * side, (me == 0) | (me == 3))]
-
-
-def light_kernel(nearest, place, mask, table, *rest):
+    middle = (me == 1) | (me == 2)
+    return [(me + 2 * side, me >= 0), (me + 3 * side, ~middle)]
+
+
+def light_kernel(mode, place, mask, table, *rest):
+    nearest = mode == "near"
     n = 3 if nearest else 2
     pieces, rest = rest[: n if nearest else 2 * n], rest[n if nearest else 2 * n :]
     if nearest:
@@ -321,7 +323,7 @@
     row_blocks = weight.shape[0] // BLOCK
     zero = lines.shape[1] - BLOCK
     me = place[0]
-    sources = light_sources(me, nearest)
+    sources = light_sources(me, mode)
 
     def copies(i):
         slot = blocks.at[pl.ds(i * SIZE, SIZE)]
@@ -356,7 +358,7 @@
     @pl.when(valid)
     def _():
         side = lax.broadcasted_iota(jnp.int32, (BLOCK, TILE), 1) // BLOCK
-        many = 11
+        many = 10
 
         def spread(t, _):
             value = blocks[pl.ds(pl.multiple_of(step * SIZE + t * many * BLOCK, BLOCK), many * BLOCK), :]
@@ -401,17 +403,17 @@
             out_ref[...] = gelu(total[...])
 
 
-def light_columns(place, mask, table, pieces, here, before=None):
+def light_columns(mode, place, mask, table, pieces, here, before=None):
     rows, width = here.shape
     depth, columns = width // 4, LIGHT * BLOCK
     full = pl.BlockSpec((rows, columns), lambda i, *_: (0, 0))
-    nearest = before is None
+    nearest = mode == "near"
     n = 3 if nearest else 2
 
     def block(i, place, *_):
         source = jnp.int32(0)
         last = jnp.int32(0)
-        for k, (at, valid) in enumerate(light_sources(place[0], nearest)):
+        for k, (at, valid) in enumerate(light_sources(place[0], mode)):
             last = jnp.where(valid, at, last)
             source = jnp.where(i == k, last, source)
         return 0, source
@@ -426,7 +428,7 @@
         scratch = [pltpu.VMEM((rows, columns), jnp.float32), *scratch, pltpu.SemaphoreType.DMA]
     any_space = pl.BlockSpec(memory_space=pl.ANY)
     return pl.pallas_call(
-        functools.partial(light_kernel, nearest),
+        functools.partial(light_kernel, mode),
         grid_spec=pltpu.PrefetchScalarGridSpec(
             num_scalar_prefetch=3,
             grid=(n,),
@@ -440,70 +442,149 @@
     )(place, mask, table, *pieces, here, *([] if nearest else [before]))
 
 
-def product_kernel(place, *rest):
-    *pieces, here_ref, end_ref, first_here, second_here, first_end, second_end, weight, sems = rest
+def early_kernel(place, *rest):
+    *pieces, tokens_ref, total1, total2, weight, sems = rest
+    columns = pieces[0].shape[1]
+    step = pl.program_id(0)
+    works = place[4] != 0
+    copies = [
+        pltpu.make_async_copy(piece, weight.at[i % 3, :, pl.ds((i // 3) * columns, columns)], sems.at[i])
+        for i, piece in enumerate(pieces)
+    ]
+
+    @pl.when(works & (step == 0))
+    def _():
+        for copy in copies:
+            copy.start()
+
+    for k in range(3):
+
+        @pl.when(works & (step == k))
+        def _():
+            copies[k].wait()
+            if k < 2:
+                copies[3 + k].wait()
+            for first in range(0, total1.shape[0], ROW_TILE):
+                rows = slice(first, first + ROW_TILE)
+                here = tokens_ref.at[rows, :] if len(tokens_ref.shape) == 2 else tokens_ref.at[:, rows, :]
+                value = tokens_dot(here, weight.at[k] if k < 2 else weight.at[k, :, :columns])
+                if k == 0:
+                    total1[rows, :] = value[:, :columns]
+                    total2[rows, :] = value[:, columns:]
+                else:
+                    total1[rows, :] += value[:, :columns]
+                    if k < 2:
+                        total2[rows, :] += value[:, columns:]
+
+
+def tokens_dot(tokens_ref, weight):
+    if len(tokens_ref.shape) == 2:
+        return jnp.dot(tokens_ref[...], weight[...], preferred_element_type=jnp.float32)
+    parts, _, piece = tokens_ref.shape
+    dots = [
+        jnp.dot(tokens_ref[i], weight[i * piece : (i + 1) * piece, :], preferred_element_type=jnp.float32)
+        for i in range(parts)
+    ]
+    return sum(dots[1:], dots[0])
+
+
+def tokens_block(tokens, depth, rows, at):
+    if tokens.ndim == 2:
+        return pl.BlockSpec((rows, depth), lambda i, place: (at(i, place)[0], at(i, place)[1]))
+    parts = depth // tokens.shape[2]
+    return pl.BlockSpec((parts, rows, tokens.shape[2]), lambda i, place: (at(i, place)[1], at(i, place)[0], 0))
+
+
+def early_products(place, pieces, tokens):
     depth, columns = pieces[0].shape
+    rows = tokens.shape[-2]
+
+    def at(i, place):
+        return 0, jnp.where(i == 0, place[0], jnp.where(i == 1, place[1], place[2]))
+
+    return pl.pallas_call(
+        early_kernel,
+        grid_spec=pltpu.PrefetchScalarGridSpec(
+            num_scalar_prefetch=1,
+            grid=(3,),
+            in_specs=[pl.BlockSpec(memory_space=pl.ANY)] * 5 + [tokens_block(tokens, depth, rows, at)],
+            out_specs=[pl.BlockSpec((rows, columns), lambda i, place: (0, 0))] * 2,
+            scratch_shapes=[pltpu.VMEM((3, depth, 2 * columns), jnp.bfloat16), pltpu.SemaphoreType.DMA((5,))],
+        ),
+        out_shape=[jax.ShapeDtypeStruct((rows, columns), jnp.float32)] * 2,
+        cost_estimate=BRIEF,
+        compiler_params=vmem(48),
+    )(place, *pieces, tokens)
+
+
+def last_kernel(n, place, *rest):
+    pieces, here_refs, end_refs, rest = rest[:n], rest[n : 2 * n], rest[2 * n : 3 * n], rest[3 * n :]
+    here_total, end_total, out_here, out_end, weight, sems = rest
     step = pl.program_id(0)
     half = pl.num_programs(0) // 2
-
     works = place[4] != 0
 
     @pl.when(works & (step == 0))
     def _():
-        copies = []
-        for i, piece in enumerate(pieces):
-            rows = pl.ds(pl.multiple_of(place[i % 4] * depth, depth), depth)
-            lanes = pl.ds((i // 4) * columns, columns)
-            copies.append(pltpu.make_async_copy(piece, weight.at[rows, lanes], sems.at[i]))
+        copies = [pltpu.make_async_copy(piece, weight.at[i], sems.at[i]) for i, piece in enumerate(pieces)]
         for copy in copies:
             copy.start()
         for copy in copies:
             copy.wait()
 
-    def finish(preact, first_ref, second_ref):
-        hidden = gelu(preact)
-        first_ref[...] = hidden[:, :columns]
-        second_ref[...] = hidden[:, columns:]
-
-    @pl.when(works & (step < half))
-    def _():
-        finish(jnp.dot(here_ref[...], weight[...], preferred_element_type=jnp.float32), first_here, second_here)
-
-    @pl.when(works & (step >= half))
-    def _():
-        parts, _, piece = end_ref.shape
-        total = jnp.zeros((end_ref.shape[1], 2 * columns), jnp.float32)
-        for i in range(parts):
-            rows = slice(i * piece, (i + 1) * piece)
-            total += jnp.dot(end_ref[i], weight[rows, :], preferred_element_type=jnp.float32)
-        finish(total, first_end, second_end)
-
-
-def products(place, pieces, here, end):
-    columns = pieces[0].shape[1]
-    rows, width = here.shape
+    def finish(refs, total, out_ref):
+        preact = total[...]
+        for i, ref in enumerate(refs):
+            preact += tokens_dot(ref, weight.at[i])
+        out_ref[...] = gelu(preact)
+
+    pl.when(works & (step < half))(lambda: finish(here_refs, here_total, out_here))
+    pl.when(works & (step >= half))(lambda: finish(end_refs, end_total, out_end))
+
+
+def last_products(place, pieces, here, end, here_total, end_total):
+    n = len(pieces)
+    depth, columns = pieces[0].shape
+    rows = here.shape[0]
     steps = rows // ROW_TILE
+    here_at = lambda k: lambda i, place: (jnp.minimum(i, steps - 1) * place[4], place[k])
+    end_at = lambda k: lambda i, place: (jnp.maximum(i - steps, 0) * place[4], place[k])
+    total = lambda at: pl.BlockSpec((ROW_TILE, columns), lambda i, place: (at(i, place)[0], 0))
+    ks = range(4 - n, 4)
     return pl.pallas_call(
-        product_kernel,
+        functools.partial(last_kernel, n),
         grid_spec=pltpu.PrefetchScalarGridSpec(
             num_scalar_prefetch=1,
             grid=(2 * steps,),
-            in_specs=[pl.BlockSpec(memory_space=pl.ANY)] * 8
-            + [pl.BlockSpec((ROW_TILE, width), lambda i, place: (jnp.minimum(i, steps - 1) * place[4], 0))]
-            + [pl.BlockSpec((end.shape[0], ROW_TILE, end.shape[2]), lambda i, place: (0, jnp.maximum(i - steps, 0) * place[4], 0))],
-            out_specs=[pl.BlockSpec((ROW_TILE, columns), lambda i, place: (jnp.minimum(i, steps - 1), 0))] * 2
-            + [pl.BlockSpec((ROW_TILE, columns), lambda i, place: (jnp.maximum(i - steps, 0), 0))] * 2,
-            scratch_shapes=[pltpu.VMEM((width, 2 * columns), jnp.bfloat16), pltpu.SemaphoreType.DMA((8,))],
+            in_specs=[pl.BlockSpec(memory_space=pl.ANY)] * n
+            + [tokens_block(here, depth, ROW_TILE, here_at(k)) for k in ks]
+            + [tokens_block(end, depth, ROW_TILE, end_at(k)) for k in ks]
+            + [total(here_at(3)), total(end_at(3))],
+            out_specs=[
+                pl.BlockSpec((ROW_TILE, columns), lambda i, place: (jnp.minimum(i, steps - 1), 0)),
+                pl.BlockSpec((ROW_TILE, columns), lambda i, place: (jnp.maximum(i - steps, 0), 0)),
+            ],
+            scratch_shapes=[pltpu.VMEM((n, depth, columns), jnp.bfloat16), pltpu.SemaphoreType.DMA((n,))],
         ),
-        out_shape=[jax.ShapeDtypeStruct((rows, columns), jnp.bfloat16)] * 4,
+        out_shape=[jax.ShapeDtypeStruct((rows, columns), jnp.bfloat16)] * 2,
         cost_estimate=BRIEF,
-        compiler_params=vmem(52),
-    )(place, *pieces, here, end)
-
-
-def order_kernel(table, *rest):
+        compiler_params=vmem(48),
+    )(place, *pieces, *[here] * n, *[end] * n, here_total, end_total)
+
+
+def order_kernel(table, place, light, second_here, second_back, *rest):
     *sources, out_ref, results = rest
-    at = 0
+    at = light.shape[1] + second_here.shape[1]
+    results[:, : light.shape[1]] = light[...]
+
+    @pl.when(place[4] != 0)
+    def _():
+        results[:, light.shape[1] : at] = second_here[...]
+
+    @pl.when(place[4] == 0)
+    def _():
+        results[:, light.shape[1] : at] = second_back[...]
+
     for ref in sources:
         results[:, at : at + ref.shape[1]] = ref[...]
         at += ref.shape[1]
@@ -517,23 +598,24 @@
         out_ref[:, t * TILE : (t + 1) * TILE] = jnp.where(side == 0, values[0], values[1])
 
 
-def in_order(table, sources):
+def in_order(table, place, sources):
     rows = sources[0].shape[0]
     tile = rows // 4
     widths = [s.shape[1] for s in sources]
+    wide = sum(widths) - widths[1]
     return pl.pallas_call(
         order_kernel,
         grid_spec=pltpu.PrefetchScalarGridSpec(
-            num_scalar_prefetch=1,
+            num_scalar_prefetch=2,
             grid=(4,),
-            in_specs=[pl.BlockSpec((tile, w), lambda i, table: (i, 0)) for w in widths],
-            out_specs=pl.BlockSpec((tile, OWN * BLOCK), lambda i, table: (i, 0)),
-            scratch_shapes=[pltpu.VMEM((tile, sum(widths)), jnp.bfloat16)],
+            in_specs=[pl.BlockSpec((tile, w), lambda i, *_: (i, 0)) for w in widths],
+            out_specs=pl.BlockSpec((tile, OWN * BLOCK), lambda i, *_: (i, 0)),
+            scratch_shapes=[pltpu.VMEM((tile, wide), jnp.bfloat16)],
         ),
         out_shape=jax.ShapeDtypeStruct((rows, OWN * BLOCK), jnp.bfloat16),
         cost_estimate=BRIEF,
         compiler_params=vmem(32),
-    )(table, *sources)
+    )(table, place, *sources)
 
 
 def line_body(tokens, up_weight, block_mask):
@@ -564,37 +646,40 @@
     up1, down1, taken = lax.optimization_barrier((up1, down1, taken))
     up2, down2 = lax.ppermute(up1, "row", UP[1:]), lax.ppermute(down1, "row", DOWN[1:])
     taken.append(lax.ppermute(after(handed[2], taken), "col", SWAP_DIAGONAL))
-    light = light_columns(place, block_mask, table, [packed, up1, down1], tokens)
+    light = light_columns("near", place, block_mask, table, [packed, up1, down1], tokens)
     mine = lax.dynamic_slice_in_dim(tokens, (c * CORES + p) * piece, piece, 1)
     mine = lax.ppermute(after(mine, packed), "row", INWARD)
     end = lax.all_gather(after(mine, up2, down2, taken[2], light), ("col", "rep"), axis=0, tiled=True)
     (first,) = whole_columns(LIGHT + HEAVY, (HEAVY,), place, block_mask, table, up_weight, taken)
-    near2 = lax.ppermute(after(own_heavy, mine), "row", INWARD)
+    near2 = lax.ppermute(after(own_heavy, mine, first), "row", INWARD)
     up2, down2, first, mine = lax.optimization_barrier((up2, down2, first, mine))
     up3, down3 = lax.ppermute(up2, "row", UP[2:]), lax.ppermute(down2, "row", DOWN[2:])
     mid1 = lax.ppermute(after(first, mid2), "row", MIDDLE)
     near1 = lax.ppermute(first, "row", INWARD)
-    far2 = lax.ppermute(near2, "row", MIDDLE)
-    far1 = lax.ppermute(after(near1, mid1), "row", MIDDLE)
-    pieces = [up2, down2, up3, down3]
-
-    end = end.reshape(parts, rows, piece)
+    far1 = lax.ppermute(near1, "row", MIDDLE)
     at = jnp.stack([r, 3 - r, jnp.where(r <= 1, 0, 3), jnp.where(r <= 1, 3, 0), is_middle.astype(jnp.int32)])
     at = jnp.where(is_middle, at, jnp.zeros_like(at))
-
-    weights = [first, mid1, near1, far1, own_heavy, mid2, near2, far2]
-    first_here, second_here, first_end, second_end = products(at, weights, tokens, end)
+    early = [first, mid1, near1, own_heavy, mid2]
+    here_total1, here_total2 = early_products(at, early, tokens)
+    far2 = lax.ppermute(after(near2, near1, here_total1, up3, down3), "row", MIDDLE)
+    pieces = [up2, down2, up3, down3]
+
+    end = end.reshape(parts, rows, piece)
+    end_total1, end_total2 = early_products(at, early, after(end, here_total1))
+    first_here, first_end = last_products(at, [far1], tokens, end, here_total1, end_total1)
     back1 = lax.ppermute(first_end, "row", OUTWARD)
+    far2 = after(far2, first_end)
+    second_here, second_end = last_products(at, [near2, far2], tokens, end, here_total2, end_total2)
     back2 = lax.ppermute(second_end, "row", OUTWARD)
-    light = light_columns(place, block_mask, after(table, first_end), pieces, tokens, light)
-    hidden1 = jnp.where(is_middle, after(first_here, light), back1)
+    hidden1 = jnp.where(is_middle, after(first_here, second_here), back1)
     home = [lax.ppermute(hidden1, "col", pairs) for pairs in SWAPS]
-    hidden2 = jnp.where(is_middle, second_here, after(back2, *home))
+    light = light_columns("rest", place, block_mask, after(table, hidden1), pieces, tokens, light)
+    results = [light, second_here, after(back2, *home), hidden1, *home]
     return lax.cond(
         most > 2 * CAP,
-        lambda table, *_: gather_body(tokens, up_weight, given_mask),
-        lambda table, *results: in_order(table, results),
-        table, light, hidden2, hidden1, *home,
+        lambda *_: gather_body(tokens, up_weight, given_mask),
+        lambda table, *results: in_order(table, at, results),
+        table, *results,
     )
 
 

time: 206 us -> 196 us (0.951)
  the two profiles are of different devices: /device:TPU:10 before, /device:TPU:0 now
where the time goes in v3:
time: 196 us; the launch traced here: 195 us
  Pallas kernels  64.8 us (33%)
  waiting for transfers between devices  52.9 us (27%)
  starting transfers between devices  49.1 us (25%)
  between operations  14.5 us (7%)
  local copies, waits for them, and re-layouts  10.5 us (5%)
  other arithmetic  3.36 us (2%)
    pallas_call x2, Pallas kernels, light_columns(): pl.pallas_call(functools.partial(light_kernel, mode), grid_spec=pltpu.Pre...  33.4 us
    ppermute x1, waiting for transfers between devices, line_body(): lax.ppermute(handed[0], 'col', SWAP_X)  13.2 us
    ppermute x1, waiting for transfers between devices, line_body(): back1 = lax.ppermute(first_end, 'row', OUTWARD)  13 us
    ppermute x1, waiting for transfers between devices, line_body(): near1 = lax.ppermute(first, 'row', INWARD)  11 us
    pallas_call x1, Pallas kernels, pack_columns(): pl.pallas_call(pack_kernel, grid_spec=pltpu.PrefetchScalarGridSpec(num_sc...  9.97 us
    ppermute x1, starting transfers between devices, line_body(): near1 = lax.ppermute(first, 'row', INWARD)  9.54 us
    pallas_call x1, Pallas kernels, whole_columns(): pl.pallas_call(functools.partial(whole_kernel, first), grid_spec=pltpu.Pr...  7.32 us
    ppermute x1, starting transfers between devices, line_body(): mine = lax.ppermute(after(mine, packed), 'row', INWARD)  6.9 us
  transfers between devices with their start and end apart: 22, of which 8 were waited for; matrix products, arithmetic and copies ran while one was open for 3% of the time, Pallas kernels for 26%

profile of v3, /device:TPU:0, one launch (start us, length us, event | category | flops | bytes accessed | tf_op | source)
XLA Modules:
  0.0 195.1 jit_solution(11682699492188639710)
XLA Ops:
  6.5 0.9 pad_reduce_fusion
  7.5 0.1 pad_add_fusion.place
  7.5 10.0 %shard_map.39 = (s32[69]{0:T(128)S(1)}, s32[9]{0:T(128)S(1)}, bf16[4480,128]{1,0:T(8,128)(2,1)S(1)}, bf16[1280,256]{1,0:T(8,128)(2,1)S(1)}) custom-call(s32[3]{0:T(128)S(1)} %pad_add_fusion.place, s32[80,161]{1,0:T(8,128)S(1)} %get-tuple-element.117.mask, s32[161]{0:T(256)S(1)} %get-tuple-element.116.count, bf16[1280,2560]{1,0:T(8,128)(2,1)} %w_ref.3), custom_call_target="tpu_custom_call" | custom-call | flops 1 | bytes 1 | tf_op jit(solution)/shard_map/pallas_call | solution.py:198
  17.5 5.9 %collective-permute-start = (bf16[4480,128]{1,0:T(8,128)(2,1)S(1)}, bf16[4480,128]{1,0:T(8,128)(2,1)}, u32[]{:S(2)}, u32[]{:S(2)}) collective-permute-start(bf16[4480,128]{1,0:T(8,128)(2,1)S(1)} %get-tuple-element.76.rest_0_), channel_id=1, source_target_pairs={{0,8},{8,16},{16,24},{1,9},{9,17},{17,25},{2,10},{10,18},{18,26},{... | collective-permute-start | bytes 3440648 | tf_op jit(solution)/shard_map/ppermute | solution.py:638
  23.5 1.3 collective-permute-start.1
  24.8 2.5 %constant_dynamic-slice_fusion.1 = (bf16[1280,256]{1,0:T(8,128)(2,1)}, bf16[1280,256]{1,0:T(8,128)(2,1)S(1)}, bf16[1280,256]{1,0:T(8,128)(2,1)S(1)}) fusion(bf16[1280,2560]{1,0:T(8,128)(2,1)} %w_ref.3, s32[]{:T(128)S(6)} %select_n.154, s32[]{:T(128)S(6)} %select_n.153, s32[]{:T(128)S(6)} %select_n.152), kind=kLoop, calls=%fused_computation.72 | loop fusion | bytes 3932172 | tf_op jit(solution)/shard_map/dynamic_slice | solution.py:643
  27.3 1.5 collective-permute-start.2
  28.7 1.5 collective-permute-start.3
  30.3 13.2 %collective-permute-done.2.x_ref = bf16[1280,256]{1,0:T(8,128)(2,1)S(1)} collective-permute-done((bf16[1280,256]{1,0:T(8,128)(2,1)S(1)}, bf16[1280,256]{1,0:T(8,128)(2,1)S(1)}, u32[]{:S(2)}, u32[]{:S(2)}) %collective-permute-start.2) | collective-permute-done | bytes 655392 | tf_op jit(solution)/shard_map/ppermute | solution.py:644
  43.4 1.2 collective-permute-done.3.y_ref
  44.7 0.9 copy-done.6
  45.5 1.4 collective-permute-done.rest_1_
  47.0 5.2 %collective-permute-done.1.rest_2_ = bf16[4480,128]{1,0:T(8,128)(2,1)} collective-permute-done((bf16[4480,128]{1,0:T(8,128)(2,1)S(1)}, bf16[4480,128]{1,0:T(8,128)(2,1)}, u32[]{:S(2)}, u32[]{:S(2)}) %collective-permute-start.1) | collective-permute-done | bytes 1146912 | tf_op jit(solution)/shard_map/ppermute | solution.py:638
  52.2 1.7 collective-permute-start.4
  53.9 1.3 collective-permute-start.5
  55.1 1.3 constant_dynamic-slice_fusion
  56.4 6.9 %collective-permute-start.7 = (bf16[768,640]{1,0:T(8,128)(2,1)S(1)}, bf16[768,640]{1,0:T(8,128)(2,1)}, u32[]{:S(2)}, u32[]{:S(2)}) collective-permute-start(bf16[768,640]{1,0:T(8,128)(2,1)S(1)} %constant_dynamic-slice_fusion), channel_id=1, source_target_pairs={{0,8},{24,16},{1,9},{25,17},{2,10},{26,18},{3,11},{27,19},{4,12},{... | collective-permute-start | bytes 2949128 | tf_op jit(solution)/shard_map/ppermute | solution.py:651
  63.3 2.4 %collective-permute-start.6 = (bf16[1280,256]{1,0:T(8,128)(2,1)}, bf16[1280,256]{1,0:T(8,128)(2,1)S(1)}, u32[]{:S(2)}, u32[]{:S(2)}) collective-permute-start(bf16[1280,256]{1,0:T(8,128)(2,1)} %get-tuple-element.81), channel_id=1, source_target_pairs={{0,6},{6,0},{2,4},{4,2},{1,7},{7,1},{3,5},{5,3},{8,14},{14,8},{10,... | collective-permute-start | bytes 1966088 | tf_op jit(solution)/shard_map/ppermute | solution.py:648
  65.8 17.4 %shard_map.41.rest_5_ = f32[768,1024]{1,0:T(8,128)} custom-call(s32[3]{0:T(128)S(1)} %pad_add_fusion.place, s32[80,161]{1,0:T(8,128)S(1)} %get-tuple-element.117.mask, s32[69]{0:T(128)S(1)} %get-tuple-element.101.table, bf16[4480,128]{1,0:T(8,128)(2,1)S(1)} %get-tuple-element.76.rest_0_, bf16[4480,128]{1,0:T(8,128)(2,1)} %collective-permute-done.rest_1_, ...), custom_call_target="tpu_custom_call" | custom-call | flops 1 | bytes 1 | tf_op jit(solution)/shard_map/pallas_call | solution.py:430
  83.2 0.0 copy-start.8
  83.2 0.0 collective-permute-done.5.rest_1_
  83.3 0.0 all-gather.5.cloned.1.call-update
  83.3 0.7 copy-done.8
  84.0 0.7 collective-permute-start.10
  84.7 1.1 copy-done.7
  85.8 1.1 copy-done.9
  86.9 7.3 %shard_map.40.rest_0_ = bf16[1280,256]{1,0:T(8,128)(2,1)S(1)} custom-call(s32[3]{0:T(128)S(1)} %pad_add_fusion.place, s32[80,161]{1,0:T(8,128)S(1)} %get-tuple-element.117.mask, s32[69]{0:T(128)S(1)} %get-tuple-element.101.table, bf16[1280,2560]{1,0:T(8,128)(2,1)} %w_ref.3, bf16[1280,256]{1,0:T(8,128)(2,1)S(1)} %collective-permute-done.2.x_ref, ...), custom_call_target="tpu_custom_call" | custom-call | flops 1 | bytes 1 | tf_op jit(solution)/shard_map/pallas_call | solution.py:285
  94.2 1.7 collective-permute-start.13
  95.9 1.3 collective-permute-start.14
  97.2 9.5 %collective-permute-start.8 = (bf16[1280,256]{1,0:T(8,128)(2,1)S(1)}, bf16[1280,256]{1,0:T(8,128)(2,1)S(1)}, u32[]{:S(2)}, u32[]{:S(2)}) collective-permute-start(bf16[1280,256]{1,0:T(8,128)(2,1)S(1)} %shard_map.40.rest_0_), channel_id=1, source_target_pairs={{0,8},{24,16},{1,9},{25,17},{2,10},{26,18},{3,11},{27,19},{4,12},{... | collective-permute-start | bytes 1966088 | tf_op jit(solution)/shard_map/ppermute | solution.py:658
  106.7 0.7 collective-permute-start.11
  107.4 3.4 %collective-permute-start.12 = (bf16[1280,256]{1,0:T(8,128)(2,1)S(1)}, bf16[1280,256]{1,0:T(8,128)(2,1)}, u32[]{:S(2)}, u32[]{:S(2)}) collective-permute-start(bf16[1280,256]{1,0:T(8,128)(2,1)S(1)} %get-tuple-element.91.rest_3_), channel_id=1, source_target_pairs={{0,8},{24,16},{1,9},{25,17},{2,10},{26,18},{3,11},{27,19},{4,12},{... | collective-permute-start | bytes 1966088 | tf_op jit(solution)/shard_map/ppermute | solution.py:654
  110.8 11.0 %collective-permute-done.8.rest_2_ = bf16[1280,256]{1,0:T(8,128)(2,1)S(1)} collective-permute-done((bf16[1280,256]{1,0:T(8,128)(2,1)S(1)}, bf16[1280,256]{1,0:T(8,128)(2,1)S(1)}, u32[]{:S(2)}, u32[]{:S(2)}) %collective-permute-start.8) | collective-permute-done | bytes 655392 | tf_op jit(solution)/shard_map/ppermute | solution.py:658
  121.9 1.5 collective-permute-start.9
  123.4 0.1 stack.40
  123.5 2.1 %shard_map.42 = (f32[768,256]{1,0:T(8,128)S(1)}, f32[768,256]{1,0:T(8,128)S(1)}) custom-call(s32[5]{0:T(128)S(1)} %broadcast_select_fusion.1.place, bf16[1280,256]{1,0:T(8,128)(2,1)S(1)} %shard_map.40.rest_0_, bf16[1280,256]{1,0:T(8,128)(2,1)S(1)} %collective-permute-done.11.rest_1_, bf16[1280,256]{1,0:T(8,128)(2,1)S(1)} %collective-permute-done.8.rest_2_, ...), custom_call_target="tpu_custom_call" | custom-call | flops 1 | bytes 1 | tf_op jit(solution)/shard_map/pallas_call | solution.py:505
  125.6 0.9 copy-done
  126.5 0.9 copy-done.4
  127.4 5.2 %collective-permute-done.12.rest_0_ = bf16[1280,256]{1,0:T(8,128)(2,1)} collective-permute-done((bf16[1280,256]{1,0:T(8,128)(2,1)S(1)}, bf16[1280,256]{1,0:T(8,128)(2,1)}, u32[]{:S(2)}, u32[]{:S(2)}) %collective-permute-start.12) | collective-permute-done | bytes 655392 | tf_op jit(solution)/shard_map/ppermute | solution.py:654
  132.6 1.5 collective-permute-start.15
  134.1 0.1 slice.12
  134.2 0.1 and_select_fusion.5
  134.2 2.5 %all-gather.5.cloned.1.call-done = bf16[6144,640]{1,0:T(8,128)(2,1)} async-done(((bf16[768,640]{1,0:T(8,128)(2,1)}), bf16[6144,640]{1,0:T(8,128)(2,1)}) %all-gather.5.cloned.1.call-update) | async-done | bytes 7864336 | tf_op jit(solution)/shard_map/all_gather | solution.py:652
  136.8 2.1 %shard_map.43 = (f32[768,256]{1,0:T(8,128)S(1)}, f32[768,256]{1,0:T(8,128)S(1)}) custom-call(s32[5]{0:T(128)S(1)} %broadcast_select_fusion.1.place, bf16[1280,256]{1,0:T(8,128)(2,1)S(1)} %shard_map.40.rest_0_, bf16[1280,256]{1,0:T(8,128)(2,1)S(1)} %collective-permute-done.11.rest_1_, bf16[1280,256]{1,0:T(8,128)(2,1)S(1)} %collective-permute-done.8.rest_2_, ...), custom_call_target="tpu_custom_call" | custom-call | flops 1 | bytes 1 | tf_op jit(solution)/shard_map/pallas_call | solution.py:505
  138.9 0.9 copy-done.2
  139.8 2.1 %shard_map.44 = (bf16[768,256]{1,0:T(8,128)(2,1)S(1)}, bf16[768,256]{1,0:T(8,128)(2,1)S(1)}) custom-call(s32[5]{0:T(128)S(1)} %broadcast_select_fusion.1.place, bf16[1280,256]{1,0:T(8,128)(2,1)} %collective-permute-done.9.rest_0_, bf16[768,5120]{1,0:T(8,128)(2,1)} %rest_4_.1, bf16[8,768,640]{2,1,0:T(8,128)(2,1)} %bitcast.18, f32[768,256]{1,0:T(8,128)S(1)} %copy-done.5, ...), custom_call_target="tpu_custom_call" | custom-call | flops 1 | bytes 1 | tf_op jit(solution)/shard_map/pallas_call | solution.py:554
  141.9 1.5 collective-permute-start.16
  143.4 0.1 select_reduce_fusion.1
  143.5 0.1 slice_select_fusion.1
  143.6 0.2 convert_reduce_fusion
  143.8 4.2 %shard_map.45 = (bf16[768,256]{1,0:T(8,128)(2,1)}, bf16[768,256]{1,0:T(8,128)(2,1)S(1)}) custom-call(s32[5]{0:T(128)S(1)} %broadcast_select_fusion.1.place, bf16[1280,256]{1,0:T(8,128)(2,1)} %collective-permute-done.12.rest_0_, bf16[1280,256]{1,0:T(8,128)(2,1)} %collective-permute-done.15.rest_1_, bf16[768,5120]{1,0:T(8,128)(2,1)} %rest_4_.1, ...), custom_call_target="tpu_custom_call" | custom-call | flops 1 | bytes 1 | tf_op jit(solution)/shard_map/pallas_call | solution.py:554
  148.0 1.3 collective-permute-start.17
  149.3 13.0 %collective-permute-done.16 = bf16[768,256]{1,0:T(8,128)(2,1)} collective-permute-done((bf16[768,256]{1,0:T(8,128)(2,1)S(1)}, bf16[768,256]{1,0:T(8,128)(2,1)}, u32[]{:S(2)}, u32[]{:S(2)}) %collective-permute-start.16) | collective-permute-done | bytes 393248 | tf_op jit(solution)/shard_map/ppermute | solution.py:670
  162.3 1.0 broadcast_select_fusion
  163.3 1.5 collective-permute-start.18
  164.9 0.6 collective-permute-start.19
  165.4 1.5 collective-permute-start.20
  166.9 0.1 reshape.149
  167.0 0.1 reduce_sum.59
  167.1 0.7 reduce_max.9
  168.6 0.0 copy-start.10
  168.6 16.1 %shard_map.46 = bf16[768,1024]{1,0:T(8,128)(2,1)S(1)} custom-call(s32[3]{0:T(128)S(1)} %pad_add_fusion.place, s32[80,161]{1,0:T(8,128)S(1)} %get-tuple-element.117.mask, s32[69]{0:T(128)S(1)} %get-tuple-element.101.table, bf16[4480,128]{1,0:T(8,128)(2,1)} %collective-permute-done.4.rest_0_, bf16[4480,128]{1,0:T(8,128)(2,1)} %collective-permute-done.5.rest_1_, ...), custom_call_target="tpu_custom_call" | custom-call | flops 1 | bytes 1 | tf_op jit(solution)/shard_map/pallas_call | solution.py:430
  184.7 3.5 %conditional.1 = (bf16[768,1280]{1,0:T(8,128)(2,1)}) conditional(s32[]{:T(128)} %convert_element_type.36, (s32[69]{0:T(128)S(1)}, s32[5]{0:T(128)S(1)}, bf16[768,1024]{1,0:T(8,128)(2,1)S(1)}, bf16[768,256]{1,0:T(8,128)(2,1)S(1)}, bf16[768,256]{1,0:T(8,128)(2,1)S(1)}, /*index=5*/bf16[768,256]{1,0:T(8,128)(2,1)S(1)}, bf16[768,256]{1,0:T(8,128)(2,1)S(1)}, ...), branch_computations={%region_7.8_spmd, %region_8.9_spmd} | conditional | flops 16570380288 | bytes 94126296 | solution.py:678
  184.8 3.5 %branch_0_fun.1 = bf16[768,1280]{1,0:T(8,128)(2,1)} custom-call(s32[69]{0:T(128)S(1)} %get-tuple-element.32.table, s32[5]{0:T(128)S(1)} %get-tuple-element.33.place, bf16[768,1024]{1,0:T(8,128)(2,1)S(1)} %get-tuple-element.34.light, bf16[768,256]{1,0:T(8,128)(2,1)S(1)} %get-tuple-element.35.second_here, bf16[768,256]{1,0:T(8,128)(2,1)S(1)} %get-tuple-element.36.second_back, ...), custom_call_target="tpu_custom_call" | custom-call | flops 1 | bytes 1 | tf_op jit(solution)/shard_map/cond/branch_0_fun/pallas_call | solution.py:606
  (34 shorter events, 0.1 us)
Async XLA Ops:
  6.5 130.2 %all-gather.5.cloned.1.call-start = ((), (), s32[]{:S(2)}) async-start(), calls=%async_computation.1 | async-start | bytes 8847360 | tf_op jit(solution)/shard_map/all_gather | solution.py:652
  17.5 29.4 %collective-permute-start = (bf16[4480,128]{1,0:T(8,128)(2,1)S(1)}, bf16[4480,128]{1,0:T(8,128)(2,1)}, u32[]{:S(2)}, u32[]{:S(2)}) collective-permute-start(bf16[4480,128]{1,0:T(8,128)(2,1)S(1)} %get-tuple-element.76.rest_0_), channel_id=1, source_target_pairs={{0,8},{8,16},{16,24},{1,9},{9,17},{17,25},{2,10},{10,18},{18,26},{... | collective-permute-start | bytes 3440648 | tf_op jit(solution)/shard_map/ppermute | solution.py:638
  23.5 28.7 %collective-permute-start.1 = (bf16[4480,128]{1,0:T(8,128)(2,1)S(1)}, bf16[4480,128]{1,0:T(8,128)(2,1)}, u32[]{:S(2)}, u32[]{:S(2)}) collective-permute-start(bf16[4480,128]{1,0:T(8,128)(2,1)S(1)} %get-tuple-element.76.rest_0_), channel_id=1, source_target_pairs={{24,16},{16,8},{8,0},{25,17},{17,9},{9,1},{26,18},{18,10},{10,2},{... | collective-permute-start | bytes 3440648 | tf_op jit(solution)/shard_map/ppermute | solution.py:638
  27.3 16.2 %collective-permute-start.2 = (bf16[1280,256]{1,0:T(8,128)(2,1)S(1)}, bf16[1280,256]{1,0:T(8,128)(2,1)S(1)}, u32[]{:S(2)}, u32[]{:S(2)}) collective-permute-start(bf16[1280,256]{1,0:T(8,128)(2,1)S(1)} %get-tuple-element.115), channel_id=1, source_target_pairs={{0,2},{2,0},{4,6},{6,4},{1,3},{3,1},{5,7},{7,5},{8,10},{10,8},{12,... | collective-permute-start | bytes 1966088 | tf_op jit(solution)/shard_map/ppermute | solution.py:644
  28.7 15.9 %collective-permute-start.3 = (bf16[1280,256]{1,0:T(8,128)(2,1)S(1)}, bf16[1280,256]{1,0:T(8,128)(2,1)S(1)}, u32[]{:S(2)}, u32[]{:S(2)}) collective-permute-start(bf16[1280,256]{1,0:T(8,128)(2,1)S(1)} %get-tuple-element.114), channel_id=1, source_target_pairs={{0,4},{4,0},{2,6},{6,2},{1,5},{5,1},{3,7},{7,3},{8,12},{12,8},{10,... | collective-permute-start | bytes 1966088 | tf_op jit(solution)/shard_map/ppermute | solution.py:644
  44.7 0.9 copy-start.6
  52.2 31.0 %collective-permute-start.4 = (bf16[4480,128]{1,0:T(8,128)(2,1)}, bf16[4480,128]{1,0:T(8,128)(2,1)}, u32[]{:S(2)}, u32[]{:S(2)}) collective-permute-start(bf16[4480,128]{1,0:T(8,128)(2,1)} %collective-permute-done.rest_1_), channel_id=1, source_target_pairs={{8,16},{16,24},{9,17},{17,25},{10,18},{18,26},{11,19},{19,27},{12,... | collective-permute-start | bytes 3440648 | tf_op jit(solution)/shard_map/ppermute | solution.py:647
  53.9 29.4 %collective-permute-start.5 = (bf16[4480,128]{1,0:T(8,128)(2,1)}, bf16[4480,128]{1,0:T(8,128)(2,1)}, u32[]{:S(2)}, u32[]{:S(2)}) collective-permute-start(bf16[4480,128]{1,0:T(8,128)(2,1)} %collective-permute-done.1.rest_2_), channel_id=1, source_target_pairs={{16,8},{8,0},{17,9},{9,1},{18,10},{10,2},{19,11},{11,3},{20,12},{1... | collective-permute-start | bytes 3440648 | tf_op jit(solution)/shard_map/ppermute | solution.py:647
  56.4 26.7 %collective-permute-start.7 = (bf16[768,640]{1,0:T(8,128)(2,1)S(1)}, bf16[768,640]{1,0:T(8,128)(2,1)}, u32[]{:S(2)}, u32[]{:S(2)}) collective-permute-start(bf16[768,640]{1,0:T(8,128)(2,1)S(1)} %constant_dynamic-slice_fusion), channel_id=1, source_target_pairs={{0,8},{24,16},{1,9},{25,17},{2,10},{26,18},{3,11},{27,19},{4,12},{... | collective-permute-start | bytes 2949128 | tf_op jit(solution)/shard_map/ppermute | solution.py:651
  63.3 19.8 %collective-permute-start.6 = (bf16[1280,256]{1,0:T(8,128)(2,1)}, bf16[1280,256]{1,0:T(8,128)(2,1)S(1)}, u32[]{:S(2)}, u32[]{:S(2)}) collective-permute-start(bf16[1280,256]{1,0:T(8,128)(2,1)} %get-tuple-element.81), channel_id=1, source_target_pairs={{0,6},{6,0},{2,4},{4,2},{1,7},{7,1},{3,5},{5,3},{8,14},{14,8},{10,... | collective-permute-start | bytes 1966088 | tf_op jit(solution)/shard_map/ppermute | solution.py:648
  83.2 0.8 copy-start.8
  84.0 22.7 %collective-permute-start.10 = (bf16[1280,256]{1,0:T(8,128)(2,1)S(1)}, bf16[1280,256]{1,0:T(8,128)(2,1)S(1)}, u32[]{:S(2)}, u32[]{:S(2)}) collective-permute-start(bf16[1280,256]{1,0:T(8,128)(2,1)S(1)} %get-tuple-element.91.rest_3_), channel_id=1, source_target_pairs={{8,16},{16,8},{9,17},{17,9},{10,18},{18,10},{11,19},{19,11},{12,20... | collective-permute-start | bytes 1966088 | tf_op jit(solution)/shard_map/ppermute | solution.py:645
  84.7 1.1 copy-start.7
  85.8 1.1 copy-start.9
  94.2 38.4 %collective-permute-start.13 = (bf16[4480,128]{1,0:T(8,128)(2,1)}, bf16[4480,128]{1,0:T(8,128)(2,1)}, u32[]{:S(2)}, u32[]{:S(2)}) collective-permute-start(bf16[4480,128]{1,0:T(8,128)(2,1)} %collective-permute-done.4.rest_0_), channel_id=1, source_target_pairs={{16,24},{17,25},{18,26},{19,27},{20,28},{21,29},{22,30},{23,31}} | collective-permute-start | bytes 3440648 | tf_op jit(solution)/shard_map/ppermute | solution.py:656
  95.9 36.7 %collective-permute-start.14 = (bf16[4480,128]{1,0:T(8,128)(2,1)}, bf16[4480,128]{1,0:T(8,128)(2,1)}, u32[]{:S(2)}, u32[]{:S(2)}) collective-permute-start(bf16[4480,128]{1,0:T(8,128)(2,1)} %collective-permute-done.5.rest_1_), channel_id=1, source_target_pairs={{8,0},{9,1},{10,2},{11,3},{12,4},{13,5},{14,6},{15,7}} | collective-permute-start | bytes 3440648 | tf_op jit(solution)/shard_map/ppermute | solution.py:656
  97.2 24.7 %collective-permute-start.8 = (bf16[1280,256]{1,0:T(8,128)(2,1)S(1)}, bf16[1280,256]{1,0:T(8,128)(2,1)S(1)}, u32[]{:S(2)}, u32[]{:S(2)}) collective-permute-start(bf16[1280,256]{1,0:T(8,128)(2,1)S(1)} %shard_map.40.rest_0_), channel_id=1, source_target_pairs={{0,8},{24,16},{1,9},{25,17},{2,10},{26,18},{3,11},{27,19},{4,12},{... | collective-permute-start | bytes 1966088 | tf_op jit(solution)/shard_map/ppermute | solution.py:658
  106.7 16.7 %collective-permute-start.11 = (bf16[1280,256]{1,0:T(8,128)(2,1)S(1)}, bf16[1280,256]{1,0:T(8,128)(2,1)S(1)}, u32[]{:S(2)}, u32[]{:S(2)}) collective-permute-start(bf16[1280,256]{1,0:T(8,128)(2,1)S(1)} %shard_map.40.rest_0_), channel_id=1, source_target_pairs={{8,16},{16,8},{9,17},{17,9},{10,18},{18,10},{11,19},{19,11},{12,20... | collective-permute-start | bytes 1966088 | tf_op jit(solution)/shard_map/ppermute | solution.py:657
  107.4 25.1 %collective-permute-start.12 = (bf16[1280,256]{1,0:T(8,128)(2,1)S(1)}, bf16[1280,256]{1,0:T(8,128)(2,1)}, u32[]{:S(2)}, u32[]{:S(2)}) collective-permute-start(bf16[1280,256]{1,0:T(8,128)(2,1)S(1)} %get-tuple-element.91.rest_3_), channel_id=1, source_target_pairs={{0,8},{24,16},{1,9},{25,17},{2,10},{26,18},{3,11},{27,19},{4,12},{... | collective-permute-start | bytes 1966088 | tf_op jit(solution)/shard_map/ppermute | solution.py:654
  121.9 18.0 %collective-permute-start.9 = (bf16[1280,256]{1,0:T(8,128)(2,1)S(1)}, bf16[1280,256]{1,0:T(8,128)(2,1)}, u32[]{:S(2)}, u32[]{:S(2)}) collective-permute-start(bf16[1280,256]{1,0:T(8,128)(2,1)S(1)} %collective-permute-done.8.rest_2_), channel_id=1, source_target_pairs={{8,16},{16,8},{9,17},{17,9},{10,18},{18,10},{11,19},{19,11},{12,20... | collective-permute-start | bytes 1966088 | tf_op jit(solution)/shard_map/ppermute | solution.py:659
  125.6 0.9 copy-start
  126.5 0.9 copy-start.4
  132.6 11.2 %collective-permute-start.15 = (bf16[1280,256]{1,0:T(8,128)(2,1)}, bf16[1280,256]{1,0:T(8,128)(2,1)}, u32[]{:S(2)}, u32[]{:S(2)}) collective-permute-start(bf16[1280,256]{1,0:T(8,128)(2,1)} %collective-permute-done.12.rest_0_), channel_id=1, source_target_pairs={{8,16},{16,8},{9,17},{17,9},{10,18},{18,10},{11,19},{19,11},{12,20... | collective-permute-start | bytes 1966088 | tf_op jit(solution)/shard_map/ppermute | solution.py:664
  136.8 3.0 %copy-start.5 = (f32[768,256]{1,0:T(8,128)S(1)}, f32[768,256]{1,0:T(8,128)}, u32[]{:S(2)}) copy-start(f32[768,256]{1,0:T(8,128)} %copy-done.4) | copy-start | bytes 2359300
  138.9 0.9 copy-start.2
  139.8 4.0 %copy-start.1 = (f32[768,256]{1,0:T(8,128)S(1)}, f32[768,256]{1,0:T(8,128)}, u32[]{:S(2)}) copy-start(f32[768,256]{1,0:T(8,128)} %copy-done) | copy-start | bytes 2359300
  139.8 4.0 %copy-start.3 = (f32[768,256]{1,0:T(8,128)S(1)}, f32[768,256]{1,0:T(8,128)}, u32[]{:S(2)}) copy-start(f32[768,256]{1,0:T(8,128)} %copy-done.2) | copy-start | bytes 2359300
  141.9 20.4 %collective-permute-start.16 = (bf16[768,256]{1,0:T(8,128)(2,1)S(1)}, bf16[768,256]{1,0:T(8,128)(2,1)}, u32[]{:S(2)}, u32[]{:S(2)}) collective-permute-start(bf16[768,256]{1,0:T(8,128)(2,1)S(1)} %get-tuple-element.95), channel_id=1, source_target_pairs={{8,0},{16,24},{9,1},{17,25},{10,2},{18,26},{11,3},{19,27},{12,4},{... | collective-permute-start | bytes 1179656 | tf_op jit(solution)/shard_map/ppermute | solution.py:670
  148.0 36.7 %collective-permute-start.17 = (bf16[768,256]{1,0:T(8,128)(2,1)S(1)}, bf16[768,256]{1,0:T(8,128)(2,1)S(1)}, u32[]{:S(2)}, u32[]{:S(2)}) collective-permute-start(bf16[768,256]{1,0:T(8,128)(2,1)S(1)} %get-tuple-element.102), channel_id=1, source_target_pairs={{8,0},{16,24},{9,1},{17,25},{10,2},{18,26},{11,3},{19,27},{12,4},{... | collective-permute-start | bytes 1179656 | tf_op jit(solution)/shard_map/ppermute | solution.py:673
  163.3 21.3 %collective-permute-start.18 = (bf16[768,256]{1,0:T(8,128)(2,1)S(1)}, bf16[768,256]{1,0:T(8,128)(2,1)S(1)}, u32[]{:S(2)}, u32[]{:S(2)}) collective-permute-start(bf16[768,256]{1,0:T(8,128)(2,1)S(1)} %broadcast_select_fusion), channel_id=1, source_target_pairs={{0,2},{2,0},{4,6},{6,4},{1,3},{3,1},{5,7},{7,5},{8,10},{10,8},{12,... | collective-permute-start | bytes 1179656 | tf_op jit(solution)/shard_map/ppermute | solution.py:675
  164.9 19.8 %collective-permute-start.19 = (bf16[768,256]{1,0:T(8,128)(2,1)S(1)}, bf16[768,256]{1,0:T(8,128)(2,1)S(1)}, u32[]{:S(2)}, u32[]{:S(2)}) collective-permute-start(bf16[768,256]{1,0:T(8,128)(2,1)S(1)} %broadcast_select_fusion), channel_id=1, source_target_pairs={{0,4},{4,0},{2,6},{6,2},{1,5},{5,1},{3,7},{7,3},{8,12},{12,8},{10,... | collective-permute-start | bytes 1179656 | tf_op jit(solution)/shard_map/ppermute | solution.py:675
  165.4 19.3 %collective-permute-start.20 = (bf16[768,256]{1,0:T(8,128)(2,1)S(1)}, bf16[768,256]{1,0:T(8,128)(2,1)S(1)}, u32[]{:S(2)}, u32[]{:S(2)}) collective-permute-start(bf16[768,256]{1,0:T(8,128)(2,1)S(1)} %broadcast_select_fusion), channel_id=1, source_target_pairs={{0,6},{6,0},{2,4},{4,2},{1,7},{7,1},{3,5},{5,3},{8,14},{14,8},{10,... | collective-permute-start | bytes 1179656 | tf_op jit(solution)/shard_map/ppermute | solution.py:675
  168.6 16.2 %copy-start.10 = (bf16[768,256]{1,0:T(8,128)(2,1)S(1)}, bf16[768,256]{1,0:T(8,128)(2,1)}, u32[]{:S(2)}) copy-start(bf16[768,256]{1,0:T(8,128)(2,1)} %get-tuple-element.99) | copy-start | bytes 1179652
  168.6 16.2 %copy-start.11 = (s32[80,160]{1,0:T(8,128)S(1)}, s32[80,160]{1,0:T(8,128)}, u32[]{:S(2)}) copy-start(s32[80,160]{1,0:T(8,128)} %param.7) | copy-start | bytes 153604
Sparse Core Ops, SparseCore 0:
  83.4 53.3 all-gather.4

commit v4 on v3

--- a/solution.py
+++ b/solution.py
@@ -518,13 +518,11 @@
 
 
 def last_kernel(n, place, *rest):
-    pieces, here_refs, end_refs, rest = rest[:n], rest[n : 2 * n], rest[2 * n : 3 * n], rest[3 * n :]
-    here_total, end_total, out_here, out_end, weight, sems = rest
-    step = pl.program_id(0)
-    half = pl.num_programs(0) // 2
+    pieces, token_refs, rest = rest[:n], rest[n : 2 * n], rest[2 * n :]
+    *totals, out_ref, weight, sems = rest
     works = place[4] != 0
 
-    @pl.when(works & (step == 0))
+    @pl.when(works & (pl.program_id(0) == 0))
     def _():
         copies = [pltpu.make_async_copy(piece, weight.at[i], sems.at[i]) for i, piece in enumerate(pieces)]
         for copy in copies:
@@ -532,44 +530,32 @@
         for copy in copies:
             copy.wait()
 
-    def finish(refs, total, out_ref):
-        preact = total[...]
-        for i, ref in enumerate(refs):
-            preact += tokens_dot(ref, weight.at[i])
-        out_ref[...] = gelu(preact)
-
-    pl.when(works & (step < half))(lambda: finish(here_refs, here_total, out_here))
-    pl.when(works & (step >= half))(lambda: finish(end_refs, end_total, out_end))
-
-
-def last_products(place, pieces, here, end, here_total, end_total):
+    @pl.when(works)
+    def _():
+        terms = [total[...] for total in totals] + [tokens_dot(ref, weight.at[i]) for i, ref in enumerate(token_refs)]
+        out_ref[...] = gelu(sum(terms[1:], terms[0]))
+
+
+def last_products(place, pieces, tokens, *totals):
     n = len(pieces)
     depth, columns = pieces[0].shape
-    rows = here.shape[0]
-    steps = rows // ROW_TILE
-    here_at = lambda k: lambda i, place: (jnp.minimum(i, steps - 1) * place[4], place[k])
-    end_at = lambda k: lambda i, place: (jnp.maximum(i - steps, 0) * place[4], place[k])
-    total = lambda at: pl.BlockSpec((ROW_TILE, columns), lambda i, place: (at(i, place)[0], 0))
-    ks = range(4 - n, 4)
+    rows = tokens.shape[-2]
+    at = lambda k: lambda i, place: (i * place[4], place[k])
     return pl.pallas_call(
         functools.partial(last_kernel, n),
         grid_spec=pltpu.PrefetchScalarGridSpec(
             num_scalar_prefetch=1,
-            grid=(2 * steps,),
+            grid=(rows // ROW_TILE,),
             in_specs=[pl.BlockSpec(memory_space=pl.ANY)] * n
-            + [tokens_block(here, depth, ROW_TILE, here_at(k)) for k in ks]
-            + [tokens_block(end, depth, ROW_TILE, end_at(k)) for k in ks]
-            + [total(here_at(3)), total(end_at(3))],
-            out_specs=[
-                pl.BlockSpec((ROW_TILE, columns), lambda i, place: (jnp.minimum(i, steps - 1), 0)),
-                pl.BlockSpec((ROW_TILE, columns), lambda i, place: (jnp.maximum(i - steps, 0), 0)),
-            ],
+            + [tokens_block(tokens, depth, ROW_TILE, at(k)) for k in range(4 - n, 4)]
+            + [pl.BlockSpec((ROW_TILE, columns), lambda i, place: (i * place[4], 0))] * len(totals),
+            out_specs=pl.BlockSpec((ROW_TILE, columns), lambda i, place: (i, 0)),
             scratch_shapes=[pltpu.VMEM((n, depth, columns), jnp.bfloat16), pltpu.SemaphoreType.DMA((n,))],
         ),
-        out_shape=[jax.ShapeDtypeStruct((rows, columns), jnp.bfloat16)] * 2,
+        out_shape=jax.ShapeDtypeStruct((rows, columns), jnp.bfloat16),
         cost_estimate=BRIEF,
         compiler_params=vmem(48),
-    )(place, *pieces, *[here] * n, *[end] * n, here_total, end_total)
+    )(place, *pieces, *[tokens] * n, *totals)
 
 
 def order_kernel(table, place, light, second_here, second_back, *rest):
@@ -665,13 +651,13 @@
     pieces = [up2, down2, up3, down3]
 
     end = end.reshape(parts, rows, piece)
-    end_total1, end_total2 = early_products(at, early, after(end, here_total1))
-    first_here, first_end = last_products(at, [far1], tokens, end, here_total1, end_total1)
+    first_end = last_products(at, [first, mid1, near1, far1], after(end, here_total1))
     back1 = lax.ppermute(first_end, "row", OUTWARD)
-    far2 = after(far2, first_end)
-    second_here, second_end = last_products(at, [near2, far2], tokens, end, here_total2, end_total2)
+    first_here = last_products(at, [after(far1, first_end)], tokens, here_total1)
+    second_end = last_products(at, [own_heavy, mid2, near2, after(far2, first_here)], end)
     back2 = lax.ppermute(second_end, "row", OUTWARD)
-    hidden1 = jnp.where(is_middle, after(first_here, second_here), back1)
+    hidden1 = jnp.where(is_middle, after(first_here, second_end), back1)
+    second_here = last_products(at, [near2, after(far2, hidden1)], tokens, here_total2)
     home = [lax.ppermute(hidden1, "col", pairs) for pairs in SWAPS]
     light = light_columns("rest", place, block_mask, after(table, hidden1), pieces, tokens, light)
     results = [light, second_here, after(back2, *home), hidden1, *home]

time: 196 us -> 192 us (0.980)
  waiting for transfers between devices: 52.9 us -> 47.5 us
  Pallas kernels: 64.8 us -> 67.7 us
    ppermute x1, waiting for transfers between devices: 13 us -> 6.97 us  [line_body(): back1 = lax.ppermute(first_end, 'row', OUTWARD)]
    pallas_call x2 -> x4, Pallas kernels: 6.25 us -> 11.1 us  [last_products(): pl.pallas_call(functools.partial(last_kernel, n), grid_spec=pltpu.Prefetc...]
    pallas_call x2 -> x1, Pallas kernels: 4.28 us -> 2.14 us  [early_products(): pl.pallas_call(early_kernel, grid_spec=pltpu.PrefetchScalarGridSpec(num_s...]
    unnamed x24 -> x18, local copies, waits for them, and re-layouts: 6.44 us -> 6.72 us
  transfers between devices with their start and end apart: 22 -> 22, of which waited for: 8 -> 8; matrix products, arithmetic and copies ran while one was open for 3% -> 3% of each run, Pallas kernels for 26% -> 28%
where the time goes in v4:
time: 192 us; the launch traced here: 191 us
  Pallas kernels  67.7 us (35%)
  starting transfers between devices  48.3 us (25%)
  waiting for transfers between devices  47.5 us (25%)
  between operations  14.3 us (7%)
  local copies, waits for them, and re-layouts  10.7 us (6%)
  other arithmetic  2.26 us (1%)
    pallas_call x2, Pallas kernels, light_columns(): pl.pallas_call(functools.partial(light_kernel, mode), grid_spec=pltpu.Pre...  33.6 us
    ppermute x1, waiting for transfers between devices, line_body(): lax.ppermute(handed[0], 'col', SWAP_X)  13.2 us
    pallas_call x4, Pallas kernels, last_products(): pl.pallas_call(functools.partial(last_kernel, n), grid_spec=pltpu.Prefetc...  11.1 us
    ppermute x1, waiting for transfers between devices, line_body(): near1 = lax.ppermute(first, 'row', INWARD)  11 us
    pallas_call x1, Pallas kernels, pack_columns(): pl.pallas_call(pack_kernel, grid_spec=pltpu.PrefetchScalarGridSpec(num_sc...  9.97 us
    ppermute x1, starting transfers between devices, line_body(): near1 = lax.ppermute(first, 'row', INWARD)  9.53 us
    pallas_call x1, Pallas kernels, whole_columns(): pl.pallas_call(functools.partial(whole_kernel, first), grid_spec=pltpu.Pr...  7.33 us
    ppermute x1, waiting for transfers between devices, line_body(): back1 = lax.ppermute(first_end, 'row', OUTWARD)  6.97 us
  transfers between devices with their start and end apart: 22, of which 8 were waited for; matrix products, arithmetic and copies ran while one was open for 3% of the time, Pallas kernels for 28%

profile of v4, /device:TPU:0, one launch (start us, length us, event | category | flops | bytes accessed | tf_op | source)
XLA Modules:
  0.0 190.9 jit_solution(16058317031390903463)
XLA Ops:
  6.5 0.9 pad_reduce_fusion
  7.5 0.1 pad_add_fusion.place
  7.5 10.0 %shard_map.39 = (s32[69]{0:T(128)S(1)}, s32[9]{0:T(128)S(1)}, bf16[4480,128]{1,0:T(8,128)(2,1)S(1)}, bf16[1280,256]{1,0:T(8,128)(2,1)S(1)}) custom-call(s32[3]{0:T(128)S(1)} %pad_add_fusion.place, s32[80,161]{1,0:T(8,128)S(1)} %get-tuple-element.109.mask, s32[161]{0:T(256)S(1)} %get-tuple-element.108.count, bf16[1280,2560]{1,0:T(8,128)(2,1)} %w_ref.3), custom_call_target="tpu_custom_call" | custom-call | flops 1 | bytes 1 | tf_op jit(solution)/shard_map/pallas_call | solution.py:198
  17.5 6.0 %collective-permute-start = (bf16[4480,128]{1,0:T(8,128)(2,1)S(1)}, bf16[4480,128]{1,0:T(8,128)(2,1)}, u32[]{:S(2)}, u32[]{:S(2)}) collective-permute-start(bf16[4480,128]{1,0:T(8,128)(2,1)S(1)} %get-tuple-element.72.rest_0_), channel_id=1, source_target_pairs={{0,8},{8,16},{16,24},{1,9},{9,17},{17,25},{2,10},{10,18},{18,26},{... | collective-permute-start | bytes 3440648 | tf_op jit(solution)/shard_map/ppermute | solution.py:624
  23.5 1.3 collective-permute-start.1
  24.8 2.5 %constant_dynamic-slice_fusion.1 = (bf16[1280,256]{1,0:T(8,128)(2,1)}, bf16[1280,256]{1,0:T(8,128)(2,1)S(1)}, bf16[1280,256]{1,0:T(8,128)(2,1)S(1)}) fusion(bf16[1280,2560]{1,0:T(8,128)(2,1)} %w_ref.3, s32[]{:T(128)S(6)} %select_n.154, s32[]{:T(128)S(6)} %select_n.153, s32[]{:T(128)S(6)} %select_n.152), kind=kLoop, calls=%fused_computation.72 | loop fusion | bytes 3932172 | tf_op jit(solution)/shard_map/dynamic_slice | solution.py:629
  27.3 1.5 collective-permute-start.2
  28.8 1.5 collective-permute-start.3
  30.3 13.2 %collective-permute-done.2.x_ref = bf16[1280,256]{1,0:T(8,128)(2,1)S(1)} collective-permute-done((bf16[1280,256]{1,0:T(8,128)(2,1)S(1)}, bf16[1280,256]{1,0:T(8,128)(2,1)S(1)}, u32[]{:S(2)}, u32[]{:S(2)}) %collective-permute-start.2) | collective-permute-done | bytes 655392 | tf_op jit(solution)/shard_map/ppermute | solution.py:630
  43.5 1.2 collective-permute-done.3.y_ref
  44.7 0.9 copy-done.4
  45.5 1.4 collective-permute-done.rest_1_
  47.0 5.2 %collective-permute-done.1.rest_2_ = bf16[4480,128]{1,0:T(8,128)(2,1)} collective-permute-done((bf16[4480,128]{1,0:T(8,128)(2,1)S(1)}, bf16[4480,128]{1,0:T(8,128)(2,1)}, u32[]{:S(2)}, u32[]{:S(2)}) %collective-permute-start.1) | collective-permute-done | bytes 1146912 | tf_op jit(solution)/shard_map/ppermute | solution.py:624
  52.2 1.7 collective-permute-start.4
  53.8 1.3 collective-permute-start.5
  55.1 1.3 constant_dynamic-slice_fusion
  56.4 6.9 %collective-permute-start.7 = (bf16[768,640]{1,0:T(8,128)(2,1)S(1)}, bf16[768,640]{1,0:T(8,128)(2,1)}, u32[]{:S(2)}, u32[]{:S(2)}) collective-permute-start(bf16[768,640]{1,0:T(8,128)(2,1)S(1)} %constant_dynamic-slice_fusion), channel_id=1, source_target_pairs={{0,8},{24,16},{1,9},{25,17},{2,10},{26,18},{3,11},{27,19},{4,12},{... | collective-permute-start | bytes 2949128 | tf_op jit(solution)/shard_map/ppermute | solution.py:637
  63.3 2.4 %collective-permute-start.6 = (bf16[1280,256]{1,0:T(8,128)(2,1)}, bf16[1280,256]{1,0:T(8,128)(2,1)S(1)}, u32[]{:S(2)}, u32[]{:S(2)}) collective-permute-start(bf16[1280,256]{1,0:T(8,128)(2,1)} %get-tuple-element.77), channel_id=1, source_target_pairs={{0,6},{6,0},{2,4},{4,2},{1,7},{7,1},{3,5},{5,3},{8,14},{14,8},{10,... | collective-permute-start | bytes 1966088 | tf_op jit(solution)/shard_map/ppermute | solution.py:634
  65.8 17.5 %shard_map.41.rest_5_ = f32[768,1024]{1,0:T(8,128)} custom-call(s32[3]{0:T(128)S(1)} %pad_add_fusion.place, s32[80,161]{1,0:T(8,128)S(1)} %get-tuple-element.109.mask, s32[69]{0:T(128)S(1)} %get-tuple-element.92.table, bf16[4480,128]{1,0:T(8,128)(2,1)S(1)} %get-tuple-element.72.rest_0_, bf16[4480,128]{1,0:T(8,128)(2,1)} %collective-permute-done.rest_1_, ...), custom_call_target="tpu_custom_call" | custom-call | flops 1 | bytes 1 | tf_op jit(solution)/shard_map/pallas_call | solution.py:430
  83.3 0.0 copy-start.6
  83.3 0.0 all-gather.5.cloned.1.call-update
  83.3 0.8 copy-done.6
  84.1 0.7 collective-permute-start.10
  84.8 1.1 copy-done.5
  85.9 1.1 copy-done.7
  87.0 7.3 %shard_map.40.rest_0_ = bf16[1280,256]{1,0:T(8,128)(2,1)S(1)} custom-call(s32[3]{0:T(128)S(1)} %pad_add_fusion.place, s32[80,161]{1,0:T(8,128)S(1)} %get-tuple-element.109.mask, s32[69]{0:T(128)S(1)} %get-tuple-element.92.table, bf16[1280,2560]{1,0:T(8,128)(2,1)} %w_ref.3, bf16[1280,256]{1,0:T(8,128)(2,1)S(1)} %collective-permute-done.2.x_ref, ...), custom_call_target="tpu_custom_call" | custom-call | flops 1 | bytes 1 | tf_op jit(solution)/shard_map/pallas_call | solution.py:285
  94.3 1.7 collective-permute-start.13
  96.0 1.3 collective-permute-start.14
  97.3 9.5 %collective-permute-start.8 = (bf16[1280,256]{1,0:T(8,128)(2,1)S(1)}, bf16[1280,256]{1,0:T(8,128)(2,1)S(1)}, u32[]{:S(2)}, u32[]{:S(2)}) collective-permute-start(bf16[1280,256]{1,0:T(8,128)(2,1)S(1)} %shard_map.40.rest_0_), channel_id=1, source_target_pairs={{0,8},{24,16},{1,9},{25,17},{2,10},{26,18},{3,11},{27,19},{4,12},{... | collective-permute-start | bytes 1966088 | tf_op jit(solution)/shard_map/ppermute | solution.py:644
  106.8 1.5 collective-permute-start.11
  108.3 2.6 %collective-permute-start.12 = (bf16[1280,256]{1,0:T(8,128)(2,1)S(1)}, bf16[1280,256]{1,0:T(8,128)(2,1)}, u32[]{:S(2)}, u32[]{:S(2)}) collective-permute-start(bf16[1280,256]{1,0:T(8,128)(2,1)S(1)} %get-tuple-element.86.rest_3_.rest_0_), channel_id=1, source_target_pairs={{0,8},{24,16},{1,9},{25,17},{2,10},{26,18},{3,11},{27,19},{4,12},{... | collective-permute-start | bytes 1966088 | tf_op jit(solution)/shard_map/ppermute | solution.py:640
  111.0 11.0 %collective-permute-done.8.rest_2_ = bf16[1280,256]{1,0:T(8,128)(2,1)S(1)} collective-permute-done((bf16[1280,256]{1,0:T(8,128)(2,1)S(1)}, bf16[1280,256]{1,0:T(8,128)(2,1)S(1)}, u32[]{:S(2)}, u32[]{:S(2)}) %collective-permute-start.8) | collective-permute-done | bytes 655392 | tf_op jit(solution)/shard_map/ppermute | solution.py:644
  121.9 0.7 collective-permute-start.9
  122.7 0.1 stack.40
  122.8 2.1 %shard_map.42 = (f32[768,256]{1,0:T(8,128)S(1)}, f32[768,256]{1,0:T(8,128)S(1)}) custom-call(s32[5]{0:T(128)S(1)} %broadcast_select_fusion.1.place, bf16[1280,256]{1,0:T(8,128)(2,1)S(1)} %shard_map.40.rest_0_, bf16[1280,256]{1,0:T(8,128)(2,1)} %collective-permute-done.11.rest_1_, bf16[1280,256]{1,0:T(8,128)(2,1)S(1)} %collective-permute-done.8.rest_2_, ...), custom_call_target="tpu_custom_call" | custom-call | flops 1 | bytes 1 | tf_op jit(solution)/shard_map/pallas_call | solution.py:505
  124.9 0.9 copy-done
  125.8 0.9 copy-done.2
  126.7 6.0 %collective-permute-done.12.rest_2_.rest_0_ = bf16[1280,256]{1,0:T(8,128)(2,1)} collective-permute-done((bf16[1280,256]{1,0:T(8,128)(2,1)S(1)}, bf16[1280,256]{1,0:T(8,128)(2,1)}, u32[]{:S(2)}, u32[]{:S(2)}) %collective-permute-start.12) | collective-permute-done | bytes 655392 | tf_op jit(solution)/shard_map/ppermute | solution.py:640
  132.7 1.5 collective-permute-start.15
  134.2 0.1 slice.12
  134.3 0.1 and_select_fusion.5
  134.4 2.4 %all-gather.5.cloned.1.call-done = bf16[6144,640]{1,0:T(8,128)(2,1)} async-done(((bf16[768,640]{1,0:T(8,128)(2,1)}), bf16[6144,640]{1,0:T(8,128)(2,1)}) %all-gather.5.cloned.1.call-update) | async-done | bytes 7864336 | tf_op jit(solution)/shard_map/all_gather | solution.py:638
  136.8 4.0 %shard_map.43 = bf16[768,256]{1,0:T(8,128)(2,1)} custom-call(s32[5]{0:T(128)S(1)} %broadcast_select_fusion.1.place, bf16[1280,256]{1,0:T(8,128)(2,1)S(1)} %shard_map.40.rest_0_, bf16[1280,256]{1,0:T(8,128)(2,1)} %collective-permute-done.11.rest_1_, bf16[1280,256]{1,0:T(8,128)(2,1)S(1)} %collective-permute-done.8.rest_2_, ...), custom_call_target="tpu_custom_call" | custom-call | flops 1 | bytes 1 | tf_op jit(solution)/shard_map/pallas_call | solution.py:544
  140.8 1.3 collective-permute-start.16
  142.1 0.1 select_reduce_fusion.1
  142.3 0.1 slice_select_fusion.1
  142.3 0.2 convert_reduce_fusion
  142.5 1.1 copy-done.1
  143.7 1.8 shard_map.44
  145.4 3.3 %shard_map.45 = bf16[768,256]{1,0:T(8,128)(2,1)S(1)} custom-call(s32[5]{0:T(128)S(1)} %broadcast_select_fusion.1.place, bf16[1280,256]{1,0:T(8,128)(2,1)S(1)} %get-tuple-element.86.rest_3_.rest_0_, bf16[1280,256]{1,0:T(8,128)(2,1)S(1)} %collective-permute-done.10.rest_4_.rest_1_, bf16[1280,256]{1,0:T(8,128)(2,1)} %collective-permute-done.12.rest_2_.rest_0_, ...), custom_call_target="tpu_custom_call" | custom-call | flops 1 | bytes 1 | tf_op jit(solution)/shard_map/pallas_call | solution.py:544
  148.7 1.5 collective-permute-start.17
  150.2 7.0 %collective-permute-done.16 = bf16[768,256]{1,0:T(8,128)(2,1)S(1)} collective-permute-done((bf16[768,256]{1,0:T(8,128)(2,1)}, bf16[768,256]{1,0:T(8,128)(2,1)S(1)}, u32[]{:S(2)}, u32[]{:S(2)}) %collective-permute-start.16) | collective-permute-done | bytes 393248 | tf_op jit(solution)/shard_map/ppermute | solution.py:655
  157.2 1.5 collective-permute-start.18
  158.7 0.6 collective-permute-start.19
  159.3 1.5 collective-permute-start.20
  160.8 0.1 reshape.149
  160.9 0.1 reduce_sum.59
  161.0 0.6 reduce_max.9
  162.2 0.0 copy-start.3
  162.2 16.2 %shard_map.46 = bf16[768,1024]{1,0:T(8,128)(2,1)S(1)} custom-call(s32[3]{0:T(128)S(1)} %pad_add_fusion.place, s32[80,161]{1,0:T(8,128)S(1)} %get-tuple-element.109.mask, s32[69]{0:T(128)S(1)} %get-tuple-element.92.table, bf16[4480,128]{1,0:T(8,128)(2,1)} %collective-permute-done.4.rest_0_, bf16[4480,128]{1,0:T(8,128)(2,1)} %collective-permute-done.5.rest_1_, ...), custom_call_target="tpu_custom_call" | custom-call | flops 1 | bytes 1 | tf_op jit(solution)/shard_map/pallas_call | solution.py:430
  178.4 0.0 copy-start.8
  178.4 2.1 %shard_map.47 = bf16[768,256]{1,0:T(8,128)(2,1)S(1)} custom-call(s32[5]{0:T(128)S(1)} %broadcast_select_fusion.1.place, bf16[1280,256]{1,0:T(8,128)(2,1)} %collective-permute-done.12.rest_2_.rest_0_, bf16[1280,256]{1,0:T(8,128)(2,1)} %collective-permute-done.15.rest_3_.rest_1_, bf16[768,5120]{1,0:T(8,128)(2,1)} %rest_3_.3, bf16[768,5120]{1,0:T(8,128)(2,1)} %rest_3_.3, ...), custom_call_target="tpu_custom_call" | custom-call | flops 1 | bytes 1 | tf_op jit(solution)/shard_map/pallas_call | solution.py:544
  180.5 3.5 %conditional.1 = (bf16[768,1280]{1,0:T(8,128)(2,1)}) conditional(s32[]{:T(128)} %convert_element_type.36, (s32[69]{0:T(128)S(1)}, s32[5]{0:T(128)S(1)}, bf16[768,1024]{1,0:T(8,128)(2,1)S(1)}, bf16[768,256]{1,0:T(8,128)(2,1)S(1)}, bf16[768,256]{1,0:T(8,128)(2,1)S(1)}, /*index=5*/bf16[768,256]{1,0:T(8,128)(2,1)S(1)}, bf16[768,256]{1,0:T(8,128)(2,1)S(1)}, ...), branch_computations={%region_7.8_spmd, %region_8.9_spmd} | conditional | flops 16570380288 | bytes 94126296 | solution.py:664
  180.6 3.5 %branch_0_fun.1 = bf16[768,1280]{1,0:T(8,128)(2,1)} custom-call(s32[69]{0:T(128)S(1)} %get-tuple-element.32.table, s32[5]{0:T(128)S(1)} %get-tuple-element.33.place, bf16[768,1024]{1,0:T(8,128)(2,1)S(1)} %get-tuple-element.34.light, bf16[768,256]{1,0:T(8,128)(2,1)S(1)} %get-tuple-element.35.second_here, bf16[768,256]{1,0:T(8,128)(2,1)S(1)} %get-tuple-element.36.second_back, ...), custom_call_target="tpu_custom_call" | custom-call | flops 1 | bytes 1 | tf_op jit(solution)/shard_map/cond/branch_0_fun/pallas_call | solution.py:592
  (29 shorter events, 0.2 us)
Async XLA Ops:
  6.5 130.3 %all-gather.5.cloned.1.call-start = ((), (), s32[]{:S(2)}) async-start(), calls=%async_computation.1 | async-start | bytes 8847360 | tf_op jit(solution)/shard_map/all_gather | solution.py:638
  17.5 29.4 %collective-permute-start = (bf16[4480,128]{1,0:T(8,128)(2,1)S(1)}, bf16[4480,128]{1,0:T(8,128)(2,1)}, u32[]{:S(2)}, u32[]{:S(2)}) collective-permute-start(bf16[4480,128]{1,0:T(8,128)(2,1)S(1)} %get-tuple-element.72.rest_0_), channel_id=1, source_target_pairs={{0,8},{8,16},{16,24},{1,9},{9,17},{17,25},{2,10},{10,18},{18,26},{... | collective-permute-start | bytes 3440648 | tf_op jit(solution)/shard_map/ppermute | solution.py:624
  23.5 28.7 %collective-permute-start.1 = (bf16[4480,128]{1,0:T(8,128)(2,1)S(1)}, bf16[4480,128]{1,0:T(8,128)(2,1)}, u32[]{:S(2)}, u32[]{:S(2)}) collective-permute-start(bf16[4480,128]{1,0:T(8,128)(2,1)S(1)} %get-tuple-element.72.rest_0_), channel_id=1, source_target_pairs={{24,16},{16,8},{8,0},{25,17},{17,9},{9,1},{26,18},{18,10},{10,2},{... | collective-permute-start | bytes 3440648 | tf_op jit(solution)/shard_map/ppermute | solution.py:624
  27.3 16.2 %collective-permute-start.2 = (bf16[1280,256]{1,0:T(8,128)(2,1)S(1)}, bf16[1280,256]{1,0:T(8,128)(2,1)S(1)}, u32[]{:S(2)}, u32[]{:S(2)}) collective-permute-start(bf16[1280,256]{1,0:T(8,128)(2,1)S(1)} %get-tuple-element.107), channel_id=1, source_target_pairs={{0,2},{2,0},{4,6},{6,4},{1,3},{3,1},{5,7},{7,5},{8,10},{10,8},{12,... | collective-permute-start | bytes 1966088 | tf_op jit(solution)/shard_map/ppermute | solution.py:630
  28.8 15.9 %collective-permute-start.3 = (bf16[1280,256]{1,0:T(8,128)(2,1)S(1)}, bf16[1280,256]{1,0:T(8,128)(2,1)S(1)}, u32[]{:S(2)}, u32[]{:S(2)}) collective-permute-start(bf16[1280,256]{1,0:T(8,128)(2,1)S(1)} %get-tuple-element.106), channel_id=1, source_target_pairs={{0,4},{4,0},{2,6},{6,2},{1,5},{5,1},{3,7},{7,3},{8,12},{12,8},{10,... | collective-permute-start | bytes 1966088 | tf_op jit(solution)/shard_map/ppermute | solution.py:630
  44.7 0.9 copy-start.4
  52.2 31.1 %collective-permute-start.4 = (bf16[4480,128]{1,0:T(8,128)(2,1)}, bf16[4480,128]{1,0:T(8,128)(2,1)}, u32[]{:S(2)}, u32[]{:S(2)}) collective-permute-start(bf16[4480,128]{1,0:T(8,128)(2,1)} %collective-permute-done.rest_1_), channel_id=1, source_target_pairs={{8,16},{16,24},{9,17},{17,25},{10,18},{18,26},{11,19},{19,27},{12,... | collective-permute-start | bytes 3440648 | tf_op jit(solution)/shard_map/ppermute | solution.py:633
  53.8 29.4 %collective-permute-start.5 = (bf16[4480,128]{1,0:T(8,128)(2,1)}, bf16[4480,128]{1,0:T(8,128)(2,1)}, u32[]{:S(2)}, u32[]{:S(2)}) collective-permute-start(bf16[4480,128]{1,0:T(8,128)(2,1)} %collective-permute-done.1.rest_2_), channel_id=1, source_target_pairs={{16,8},{8,0},{17,9},{9,1},{18,10},{10,2},{19,11},{11,3},{20,12},{1... | collective-permute-start | bytes 3440648 | tf_op jit(solution)/shard_map/ppermute | solution.py:633
  56.4 26.8 %collective-permute-start.7 = (bf16[768,640]{1,0:T(8,128)(2,1)S(1)}, bf16[768,640]{1,0:T(8,128)(2,1)}, u32[]{:S(2)}, u32[]{:S(2)}) collective-permute-start(bf16[768,640]{1,0:T(8,128)(2,1)S(1)} %constant_dynamic-slice_fusion), channel_id=1, source_target_pairs={{0,8},{24,16},{1,9},{25,17},{2,10},{26,18},{3,11},{27,19},{4,12},{... | collective-permute-start | bytes 2949128 | tf_op jit(solution)/shard_map/ppermute | solution.py:637
  63.3 19.9 %collective-permute-start.6 = (bf16[1280,256]{1,0:T(8,128)(2,1)}, bf16[1280,256]{1,0:T(8,128)(2,1)S(1)}, u32[]{:S(2)}, u32[]{:S(2)}) collective-permute-start(bf16[1280,256]{1,0:T(8,128)(2,1)} %get-tuple-element.77), channel_id=1, source_target_pairs={{0,6},{6,0},{2,4},{4,2},{1,7},{7,1},{3,5},{5,3},{8,14},{14,8},{10,... | collective-permute-start | bytes 1966088 | tf_op jit(solution)/shard_map/ppermute | solution.py:634
  83.3 0.8 copy-start.6
  84.1 22.7 %collective-permute-start.10 = (bf16[1280,256]{1,0:T(8,128)(2,1)S(1)}, bf16[1280,256]{1,0:T(8,128)(2,1)S(1)}, u32[]{:S(2)}, u32[]{:S(2)}) collective-permute-start(bf16[1280,256]{1,0:T(8,128)(2,1)S(1)} %get-tuple-element.86.rest_3_.rest_0_), channel_id=1, source_target_pairs={{8,16},{16,8},{9,17},{17,9},{10,18},{18,10},{11,19},{19,11},{12,20... | collective-permute-start | bytes 1966088 | tf_op jit(solution)/shard_map/ppermute | solution.py:631
  84.8 1.1 copy-start.5
  85.9 1.1 copy-start.7
  94.3 38.4 %collective-permute-start.13 = (bf16[4480,128]{1,0:T(8,128)(2,1)}, bf16[4480,128]{1,0:T(8,128)(2,1)}, u32[]{:S(2)}, u32[]{:S(2)}) collective-permute-start(bf16[4480,128]{1,0:T(8,128)(2,1)} %collective-permute-done.4.rest_0_), channel_id=1, source_target_pairs={{16,24},{17,25},{18,26},{19,27},{20,28},{21,29},{22,30},{23,31}} | collective-permute-start | bytes 3440648 | tf_op jit(solution)/shard_map/ppermute | solution.py:642
  96.0 36.7 %collective-permute-start.14 = (bf16[4480,128]{1,0:T(8,128)(2,1)}, bf16[4480,128]{1,0:T(8,128)(2,1)}, u32[]{:S(2)}, u32[]{:S(2)}) collective-permute-start(bf16[4480,128]{1,0:T(8,128)(2,1)} %collective-permute-done.5.rest_1_), channel_id=1, source_target_pairs={{8,0},{9,1},{10,2},{11,3},{12,4},{13,5},{14,6},{15,7}} | collective-permute-start | bytes 3440648 | tf_op jit(solution)/shard_map/ppermute | solution.py:642
  97.3 24.7 %collective-permute-start.8 = (bf16[1280,256]{1,0:T(8,128)(2,1)S(1)}, bf16[1280,256]{1,0:T(8,128)(2,1)S(1)}, u32[]{:S(2)}, u32[]{:S(2)}) collective-permute-start(bf16[1280,256]{1,0:T(8,128)(2,1)S(1)} %shard_map.40.rest_0_), channel_id=1, source_target_pairs={{0,8},{24,16},{1,9},{25,17},{2,10},{26,18},{3,11},{27,19},{4,12},{... | collective-permute-start | bytes 1966088 | tf_op jit(solution)/shard_map/ppermute | solution.py:644
  106.8 15.9 %collective-permute-start.11 = (bf16[1280,256]{1,0:T(8,128)(2,1)S(1)}, bf16[1280,256]{1,0:T(8,128)(2,1)}, u32[]{:S(2)}, u32[]{:S(2)}) collective-permute-start(bf16[1280,256]{1,0:T(8,128)(2,1)S(1)} %shard_map.40.rest_0_), channel_id=1, source_target_pairs={{8,16},{16,8},{9,17},{17,9},{10,18},{18,10},{11,19},{19,11},{12,20... | collective-permute-start | bytes 1966088 | tf_op jit(solution)/shard_map/ppermute | solution.py:643
  108.3 24.4 %collective-permute-start.12 = (bf16[1280,256]{1,0:T(8,128)(2,1)S(1)}, bf16[1280,256]{1,0:T(8,128)(2,1)}, u32[]{:S(2)}, u32[]{:S(2)}) collective-permute-start(bf16[1280,256]{1,0:T(8,128)(2,1)S(1)} %get-tuple-element.86.rest_3_.rest_0_), channel_id=1, source_target_pairs={{0,8},{24,16},{1,9},{25,17},{2,10},{26,18},{3,11},{27,19},{4,12},{... | collective-permute-start | bytes 1966088 | tf_op jit(solution)/shard_map/ppermute | solution.py:640
  121.9 14.9 %collective-permute-start.9 = (bf16[1280,256]{1,0:T(8,128)(2,1)S(1)}, bf16[1280,256]{1,0:T(8,128)(2,1)S(1)}, u32[]{:S(2)}, u32[]{:S(2)}) collective-permute-start(bf16[1280,256]{1,0:T(8,128)(2,1)S(1)} %collective-permute-done.8.rest_2_), channel_id=1, source_target_pairs={{8,16},{16,8},{9,17},{17,9},{10,18},{18,10},{11,19},{19,11},{12,20... | collective-permute-start | bytes 1966088 | tf_op jit(solution)/shard_map/ppermute | solution.py:645
  124.9 0.9 copy-start
  125.8 0.9 copy-start.2
  132.7 12.7 %collective-permute-start.15 = (bf16[1280,256]{1,0:T(8,128)(2,1)}, bf16[1280,256]{1,0:T(8,128)(2,1)}, u32[]{:S(2)}, u32[]{:S(2)}) collective-permute-start(bf16[1280,256]{1,0:T(8,128)(2,1)} %collective-permute-done.12.rest_2_.rest_0_), channel_id=1, source_target_pairs={{8,16},{16,8},{9,17},{17,9},{10,18},{18,10},{11,19},{19,11},{12,20... | collective-permute-start | bytes 1966088 | tf_op jit(solution)/shard_map/ppermute | solution.py:650
  140.8 16.3 %collective-permute-start.16 = (bf16[768,256]{1,0:T(8,128)(2,1)}, bf16[768,256]{1,0:T(8,128)(2,1)S(1)}, u32[]{:S(2)}, u32[]{:S(2)}) collective-permute-start(bf16[768,256]{1,0:T(8,128)(2,1)} %shard_map.43), channel_id=1, source_target_pairs={{8,0},{16,24},{9,1},{17,25},{10,2},{18,26},{11,3},{19,27},{12,4},{... | collective-permute-start | bytes 1179656 | tf_op jit(solution)/shard_map/ppermute | solution.py:655
  142.5 1.1 copy-start.1
  148.7 31.8 %collective-permute-start.17 = (bf16[768,256]{1,0:T(8,128)(2,1)S(1)}, bf16[768,256]{1,0:T(8,128)(2,1)S(1)}, u32[]{:S(2)}, u32[]{:S(2)}) collective-permute-start(bf16[768,256]{1,0:T(8,128)(2,1)S(1)} %shard_map.45), channel_id=1, source_target_pairs={{8,0},{16,24},{9,1},{17,25},{10,2},{18,26},{11,3},{19,27},{12,4},{... | collective-permute-start | bytes 1179656 | tf_op jit(solution)/shard_map/ppermute | solution.py:658
  157.2 23.3 %collective-permute-start.18 = (bf16[768,256]{1,0:T(8,128)(2,1)S(1)}, bf16[768,256]{1,0:T(8,128)(2,1)S(1)}, u32[]{:S(2)}, u32[]{:S(2)}) collective-permute-start(bf16[768,256]{1,0:T(8,128)(2,1)S(1)} %broadcast_select_fusion), channel_id=1, source_target_pairs={{0,2},{2,0},{4,6},{6,4},{1,3},{3,1},{5,7},{7,5},{8,10},{10,8},{12,... | collective-permute-start | bytes 1179656 | tf_op jit(solution)/shard_map/ppermute | solution.py:661
  158.7 21.8 %collective-permute-start.19 = (bf16[768,256]{1,0:T(8,128)(2,1)S(1)}, bf16[768,256]{1,0:T(8,128)(2,1)S(1)}, u32[]{:S(2)}, u32[]{:S(2)}) collective-permute-start(bf16[768,256]{1,0:T(8,128)(2,1)S(1)} %broadcast_select_fusion), channel_id=1, source_target_pairs={{0,4},{4,0},{2,6},{6,2},{1,5},{5,1},{3,7},{7,3},{8,12},{12,8},{10,... | collective-permute-start | bytes 1179656 | tf_op jit(solution)/shard_map/ppermute | solution.py:661
  159.3 21.2 %collective-permute-start.20 = (bf16[768,256]{1,0:T(8,128)(2,1)S(1)}, bf16[768,256]{1,0:T(8,128)(2,1)S(1)}, u32[]{:S(2)}, u32[]{:S(2)}) collective-permute-start(bf16[768,256]{1,0:T(8,128)(2,1)S(1)} %broadcast_select_fusion), channel_id=1, source_target_pairs={{0,6},{6,0},{2,4},{4,2},{1,7},{7,1},{3,5},{5,3},{8,14},{14,8},{10,... | collective-permute-start | bytes 1179656 | tf_op jit(solution)/shard_map/ppermute | solution.py:661
  162.2 16.2 %copy-start.3 = (f32[768,256]{1,0:T(8,128)S(1)}, f32[768,256]{1,0:T(8,128)}, u32[]{:S(2)}) copy-start(f32[768,256]{1,0:T(8,128)} %copy-done.2) | copy-start | bytes 2359300
  178.4 2.1 %copy-start.8 = (s32[80,160]{1,0:T(8,128)S(1)}, s32[80,160]{1,0:T(8,128)}, u32[]{:S(2)}) copy-start(s32[80,160]{1,0:T(8,128)} %param.7) | copy-start | bytes 153604
Sparse Core Ops, SparseCore 0:
  83.4 53.3 all-gather.4
